TPU v7x, 32 devices: a whole 2x2x4 slice. The times are simulated.
32 devices in a mesh: dp: 8 (over y, x, core), seq: 4 (over z).
Axes of the slice: x: 2, y: 2, z: 4, core: 2. Of those that a mesh axis runs over, the one named last changes fastest.
Arguments:
- tokens: bfloat16 [8, 2048, 2048], P('dp', 'seq'), may hold values from -6 to 6
- lengths: int32 [8, 6], P('dp'), may hold values from 1 to 1537, as said below
- gain_one: float32 [2048], P(('dp', 'seq')), may hold values from 0.5 to 1.5
- w_query: float32 [2048, 2048], P(('dp', 'seq')), may hold values from -0.125 to 0.125
- w_key: float32 [2048, 128], P(('dp', 'seq')), may hold values from -0.125 to 0.125
- w_value: float32 [2048, 128], P(('dp', 'seq')), may hold values from -0.125 to 0.125
- w_out: float32 [2048, 2048], P(('dp', 'seq')), may hold values from -1.5 to 1.5
- gain_two: float32 [2048], P(('dp', 'seq')), may hold values from 0.5 to 1.5
- w_gate: float32 [2048, 5632], P(('dp', 'seq')), may hold values from -0.125 to 0.125
- w_up: float32 [2048, 5632], P(('dp', 'seq')), may hold values from -0.125 to 0.125
- w_down: float32 [5632, 2048], P(('dp', 'seq')), may hold values from -0.078125 to 0.078125
- cotangent: bfloat16 [8, 2048, 2048], P('dp', 'seq'), may hold values from -6 to 6
Outputs:
- output: bfloat16 [8, 2048, 2048], P('dp', 'seq')
- tokens_grad: bfloat16 [8, 2048, 2048], P('dp', 'seq')
- gain_one_grad: float32 [2048], P(('dp', 'seq'))
- w_query_grad: float32 [2048, 2048], P(('dp', 'seq'))
- w_key_grad: float32 [2048, 128], P(('dp', 'seq'))
- w_value_grad: float32 [2048, 128], P(('dp', 'seq'))
- w_out_grad: float32 [2048, 2048], P(('dp', 'seq'))
- gain_two_grad: float32 [2048], P(('dp', 'seq'))
- w_gate_grad: float32 [2048, 5632], P(('dp', 'seq'))
- w_up_grad: float32 [2048, 5632], P(('dp', 'seq'))
- w_down_grad: float32 [5632, 2048], P(('dp', 'seq'))
Inputs may be any that keep to these rules, and one draw needn't show every extreme that they name: Each row's lengths sum to 2048.
All inputs are finite; a program needn't handle non-finite values.
Results may differ from a plain program's by a relative error of at most 0.014.
The roundings to bfloat16 on the way count: a program that leaves them out, or rounds other values in their place, can miss the bound.
Values may be sent and summed in bfloat16 or wider, within the bound.
A program may use at most 384 MiB of HBM per device.

v0:
```python
import math

import jax
import jax.numpy as jnp
from jax import lax
from jax.sharding import PartitionSpec as P

HEADS = 16
HEAD = 128
WINDOW = 512


EPS = 1e-05


def shifted(value, axis, steps):
    count = lax.axis_size(axis)
    initial, last = (max(0, -steps), min(count, count - steps))
    return lax.ppermute(value, axis, [(source, source + steps) for source in range(initial, last)])


def documents(doc_lengths, index):
    ends = jnp.cumsum(doc_lengths, axis=-1)
    passed = (index[None, :, None] >= ends[:, None, :]).astype(jnp.int32)
    segment = jnp.sum(passed, axis=-1)
    before = jnp.sum(passed * doc_lengths[:, None, :], axis=-1)
    return (segment, index[None, :] - before)


def rope_tables(position):
    half = HEAD // 2
    freq = jnp.exp(jnp.arange(half, dtype=jnp.float32) * (-2.0 * math.log(10000.0) / HEAD))
    angles = position.astype(jnp.float32)[..., None] * freq
    return (jnp.cos(angles), jnp.sin(angles))


def rotate(vec, cosine, sine):
    half = vec.shape[-1] // 2
    first = vec[..., :half]
    second = vec[..., half:]
    return jnp.concatenate(
        [first * cosine - second * sine, second * cosine + first * sine], axis=-1
    )


def norm_back(grad_normed, rows, scale, gain):
    inner = grad_normed * gain
    grad_gain = jnp.sum(grad_normed * rows * scale, axis=0)
    grad_rows = scale * inner - rows * (scale * scale * scale) * jnp.mean(
        inner * rows, axis=-1, keepdims=True
    )
    return (grad_rows, grad_gain)


def matmul(left, right):
    return jnp.dot(left, right, preferred_element_type=jnp.float32)


def on_device(
    tokens,
    lengths,
    gain_one,
    w_query,
    w_key,
    w_value,
    w_out,
    gain_two,
    w_gate,
    w_up,
    w_down,
    cotangent,
):
    half_type = jnp.bfloat16
    batch, group, width = tokens.shape
    count = batch * group
    gain_a, query_w, key_w, value_w, out_w = (
        lax.all_gather(gain_one.astype(half_type), ("dp", "seq"), axis=0, tiled=True),
        lax.all_gather(w_query.astype(half_type), ("dp", "seq"), axis=0, tiled=True),
        lax.all_gather(w_key.astype(half_type), ("dp", "seq"), axis=0, tiled=True),
        lax.all_gather(w_value.astype(half_type), ("dp", "seq"), axis=0, tiled=True),
        lax.all_gather(w_out.astype(half_type), ("dp", "seq"), axis=0, tiled=True),
    )
    gain_b, gate_w, up_w, down_w = (
        lax.all_gather(gain_two.astype(half_type), ("dp", "seq"), axis=0, tiled=True),
        lax.all_gather(w_gate.astype(half_type), ("dp", "seq"), axis=0, tiled=True),
        lax.all_gather(w_up.astype(half_type), ("dp", "seq"), axis=0, tiled=True),
        lax.all_gather(w_down.astype(half_type), ("dp", "seq"), axis=0, tiled=True),
    )
    reach = (WINDOW - 2) // group + 1
    offset = lax.axis_index("seq") * group
    query_at = offset + jnp.arange(group, dtype=jnp.int32)
    key_at = offset - reach * group + jnp.arange((reach + 1) * group, dtype=jnp.int32)
    query_seg, query_pos = documents(lengths, query_at)
    key_seg = documents(lengths, key_at)[0]
    allowed = (
        (key_at[None, :] >= 0)
        & (query_at[:, None] >= key_at[None, :])
        & (query_at[:, None] - key_at[None, :] < WINDOW)
    )
    allowed = (allowed[None] & (query_seg[:, :, None] == key_seg[:, None, :]))[:, None]
    cosine, sine = rope_tables(query_pos)
    factor = 1.0 / math.sqrt(HEAD)
    rows = tokens.astype(jnp.float32).reshape(count, width)
    scale_one = lax.rsqrt(jnp.mean(rows * rows, axis=-1, keepdims=True) + EPS)
    normed = (rows * scale_one * gain_a).astype(half_type)
    query = matmul(normed, query_w).reshape(batch, group, HEADS, HEAD)
    key = matmul(normed, key_w).reshape(batch, group, HEAD)
    value = matmul(normed, value_w).astype(half_type).reshape(batch, group, HEAD)
    query_turned = rotate(query, cosine[:, :, None, :], sine[:, :, None, :]).astype(half_type)
    key_turned = rotate(key, cosine, sine).astype(half_type)
    paired = jnp.concatenate([key_turned, value], axis=-1)
    pieces = []
    for step in range(reach, 0, -1):
        pieces.append(shifted(paired, "seq", step))
    pieces.append(paired)
    seen = jnp.concatenate(pieces, axis=1)
    keys_seen = seen[..., :HEAD]
    values_seen = seen[..., HEAD:]

    def scores_of():
        raw = jnp.einsum(
            "bqhe,bke->bhqk", query_turned, keys_seen, preferred_element_type=jnp.float32
        )
        return jnp.where(allowed, raw * factor, -1e30)

    scores = scores_of()
    top = jnp.max(scores, axis=-1, keepdims=True)
    weight = jnp.exp(scores - top)
    total = jnp.sum(weight, axis=-1, keepdims=True)
    log_total = top + jnp.log(total)
    probs = (weight / total).astype(half_type)
    mixed = jnp.einsum("bhqk,bke->bqhe", probs, values_seen, preferred_element_type=jnp.float32)
    mixed = mixed.astype(half_type).reshape(count, HEADS * HEAD)
    mid = rows + matmul(mixed, out_w)
    scale_two = lax.rsqrt(jnp.mean(mid * mid, axis=-1, keepdims=True) + EPS)
    normed_two = (mid * scale_two * gain_b).astype(half_type)
    gate = matmul(normed_two, gate_w)
    up_val = matmul(normed_two, up_w)
    sigma = jax.nn.sigmoid(gate)
    swish = gate * sigma
    hidden = (swish * up_val).astype(half_type)
    output = (mid + matmul(hidden, down_w)).astype(half_type).reshape(batch, group, width)
    grad_out = cotangent.reshape(count, width)
    down_term = matmul(hidden.T, grad_out)
    grad_hidden = matmul(grad_out, down_w.T)
    grad_gate = (grad_hidden * up_val * (sigma * (1.0 + gate * (1.0 - sigma)))).astype(half_type)
    grad_up = (grad_hidden * swish).astype(half_type)
    gate_term = matmul(normed_two.T, grad_gate)
    up_term = matmul(normed_two.T, grad_up)
    grad_normed_two = matmul(grad_gate, gate_w.T) + matmul(grad_up, up_w.T)
    back_mid, gain_two_term = norm_back(grad_normed_two, mid, scale_two, gain_b)
    grad_mid = grad_out.astype(jnp.float32) + back_mid
    ffn_done = (
        lax.psum_scatter(gain_two_term, ("dp", "seq"), scatter_dimension=0, tiled=True),
        lax.psum_scatter(gate_term, ("dp", "seq"), scatter_dimension=0, tiled=True),
        lax.psum_scatter(up_term, ("dp", "seq"), scatter_dimension=0, tiled=True),
        lax.psum_scatter(down_term, ("dp", "seq"), scatter_dimension=0, tiled=True),
    )
    grad_branch = grad_mid.astype(half_type)
    out_term = matmul(mixed.T, grad_branch)
    grad_mixed = matmul(grad_branch, out_w.T).astype(half_type).reshape(batch, group, HEADS, HEAD)
    probs_full = jnp.exp(scores_of() - log_total)
    grad_probs = jnp.einsum(
        "bqhe,bke->bhqk", grad_mixed, values_seen, preferred_element_type=jnp.float32
    )
    grad_values = jnp.einsum(
        "bhqk,bqhe->bke", probs, grad_mixed, preferred_element_type=jnp.float32
    )
    centre = jnp.sum(probs_full * grad_probs, axis=-1, keepdims=True)
    grad_scores = (probs_full * (grad_probs - centre)).astype(half_type)
    grad_query = (
        jnp.einsum("bhqk,bke->bqhe", grad_scores, keys_seen, preferred_element_type=jnp.float32)
        * factor
    )
    grad_keys = (
        jnp.einsum("bhqk,bqhe->bke", grad_scores, query_turned, preferred_element_type=jnp.float32)
        * factor
    )
    grad_seen = jnp.concatenate([grad_keys, grad_values], axis=-1)
    own = grad_seen[:, reach * group :]
    for step in range(1, reach + 1):
        part = grad_seen[:, (reach - step) * group : (reach - step + 1) * group]
        own = own + shifted(part.astype(jnp.bfloat16), "seq", -step).astype(part.dtype)
    grad_key = rotate(own[..., :HEAD], cosine, -sine).astype(half_type).reshape(count, HEAD)
    grad_value = own[..., HEAD:].astype(half_type).reshape(count, HEAD)
    grad_q = (
        rotate(grad_query, cosine[:, :, None, :], -sine[:, :, None, :])
        .astype(half_type)
        .reshape(count, HEADS * HEAD)
    )
    query_term = matmul(normed.T, grad_q)
    key_term = matmul(normed.T, grad_key)
    value_term = matmul(normed.T, grad_value)
    grad_normed = (
        matmul(grad_q, query_w.T) + matmul(grad_key, key_w.T) + matmul(grad_value, value_w.T)
    )
    back_rows, gain_one_term = norm_back(grad_normed, rows, scale_one, gain_a)
    grad_rows = (grad_mid + back_rows).astype(half_type).reshape(batch, group, width)
    attn_done = (
        lax.psum_scatter(gain_one_term, ("dp", "seq"), scatter_dimension=0, tiled=True),
        lax.psum_scatter(query_term, ("dp", "seq"), scatter_dimension=0, tiled=True),
        lax.psum_scatter(key_term, ("dp", "seq"), scatter_dimension=0, tiled=True),
        lax.psum_scatter(value_term, ("dp", "seq"), scatter_dimension=0, tiled=True),
        lax.psum_scatter(out_term, ("dp", "seq"), scatter_dimension=0, tiled=True),
    )
    return (
        output,
        grad_rows,
        attn_done[0],
        attn_done[1],
        attn_done[2],
        attn_done[3],
        attn_done[4],
        ffn_done[0],
        ffn_done[1],
        ffn_done[2],
        ffn_done[3],
    )


def solution(mesh):
    in_specs = (
        P("dp", "seq", None),
        P("dp", None),
        P(("dp", "seq")),
        P(("dp", "seq"), None),
        P(("dp", "seq"), None),
        P(("dp", "seq"), None),
        P(("dp", "seq"), None),
        P(("dp", "seq")),
        P(("dp", "seq"), None),
        P(("dp", "seq"), None),
        P(("dp", "seq"), None),
        P("dp", "seq", None),
    )
    out_specs = (
        P("dp", "seq", None),
        P("dp", "seq", None),
        P(("dp", "seq")),
        P(("dp", "seq"), None),
        P(("dp", "seq"), None),
        P(("dp", "seq"), None),
        P(("dp", "seq"), None),
        P(("dp", "seq")),
        P(("dp", "seq"), None),
        P(("dp", "seq"), None),
        P(("dp", "seq"), None),
    )
    return jax.shard_map(
        on_device, mesh=mesh, in_specs=in_specs, out_specs=out_specs, check_vma=False
    )
```

profile of v0, /device:TPU:0, one launch (start us, length us, event | category | flops | bytes accessed | tf_op | source)
XLA Modules:
  0.0 4722.3 jit_solution(15261906221473910742)
XLA Ops:
  17.5 42.4 all-reduce.5
  62.9 74.1 %all_gather.28 = bf16[2048,128]{1,0:T(8,128)(2,1)S(1)} all-gather(bf16[64,128]{1,0:T(8,128)(2,1)S(1)} %convert_element_type.171), channel_id=1, replica_groups=mesh['dp'=8,'seq'=4] {'dp','seq'}, dimensions={0}, use_global_device_ids=true | all-gather | bytes 540672 | tf_op jit(solution)/shard_map/all_gather | solution.py:79
  138.5 73.4 %all_gather.29 = bf16[2048,128]{1,0:T(8,128)(2,1)S(1)} all-gather(bf16[64,128]{1,0:T(8,128)(2,1)S(1)} %convert_element_type.173), channel_id=1, replica_groups=mesh['dp'=8,'seq'=4] {'dp','seq'}, dimensions={0}, use_global_device_ids=true | all-gather | bytes 540672 | tf_op jit(solution)/shard_map/all_gather | solution.py:80
  305.2 20.8 all-gather.10.cloned.1.call-done
  326.1 19.2 fusion.101
  345.3 126.9 %all-gather.12.cloned.1.call-done = bf16[2048,5632]{1,0:T(8,128)(2,1)} async-done(((bf16[64,5632]{1,0:T(8,128)(2,1)}), bf16[2048,5632]{1,0:T(8,128)(2,1)}) %all-gather.12.cloned.1.call-update) | async-done | bytes 23068688 | tf_op jit(solution)/shard_map/all_gather | solution.py:86
  472.2 19.1 fusion.102
  491.2 126.4 %all-gather.14.cloned.1.call-done = bf16[5632,2048]{1,0:T(8,128)(2,1)} async-done(((bf16[176,2048]{1,0:T(8,128)(2,1)}), bf16[5632,2048]{1,0:T(8,128)(2,1)}) %all-gather.14.cloned.1.call-update) | async-done | bytes 23068688 | tf_op jit(solution)/shard_map/all_gather | solution.py:87
  617.7 28.3 multiply_convert_fusion
  645.9 19.5 fusion.103
  665.4 19.5 multiply_reduce_fusion
  715.7 23.5 fusion
  739.2 28.0 fusion.5
  827.5 20.9 fusion.105
  848.5 20.9 fusion.106
  871.1 20.9 fusion.31
  900.8 19.2 fusion.29
  925.6 38.7 all-reduce.4
  971.4 90.5 %reduce-scatter.12.cloned.1.call-done = f32[64,128]{1,0:T(8,128)} async-done(((f32[2048,128]{1,0:T(8,128)}), f32[64,128]{1,0:T(8,128)}) %reduce-scatter.12.cloned.1.call-update) | async-done | bytes 32784 | tf_op jit(solution)/shard_map/reduce_scatter | solution.py:203
  1061.9 363.9 %reduce-scatter.8.cloned.1.call-done = f32[64,2048]{1,0:T(8,128)} async-done(((f32[2048,2048]{1,0:T(8,128)}), f32[64,2048]{1,0:T(8,128)}) %reduce-scatter.8.cloned.1.call-update) | async-done | bytes 524304 | tf_op jit(solution)/shard_map/reduce_scatter | solution.py:201
  1425.9 365.1 %reduce-scatter.14.cloned.1.call-done = f32[64,2048]{1,0:T(8,128)} async-done(((f32[2048,2048]{1,0:T(8,128)}), f32[64,2048]{1,0:T(8,128)}) %reduce-scatter.14.cloned.1.call-update) | async-done | bytes 524304 | tf_op jit(solution)/shard_map/reduce_scatter | solution.py:204
  1790.9 973.1 %reduce-scatter.16.cloned.1.call-done = f32[64,5632]{1,0:T(8,128)} async-done(((f32[2048,5632]{1,0:T(8,128)}), f32[64,5632]{1,0:T(8,128)}) %reduce-scatter.16.cloned.1.call-update) | async-done | bytes 1441808 | tf_op jit(solution)/shard_map/reduce_scatter | solution.py:155
  2764.0 975.7 %reduce-scatter.18.cloned.1.call-done = f32[64,5632]{1,0:T(8,128)} async-done(((f32[2048,5632]{1,0:T(8,128)}), f32[64,5632]{1,0:T(8,128)}) %reduce-scatter.18.cloned.1.call-update) | async-done | bytes 1441808 | tf_op jit(solution)/shard_map/reduce_scatter | solution.py:156
  3739.7 975.5 %reduce-scatter.20.cloned.1.call-done = f32[176,2048]{1,0:T(8,128)} async-done(((f32[5632,2048]{1,0:T(8,128)}), f32[176,2048]{1,0:T(8,128)}) %reduce-scatter.20.cloned.1.call-update) | async-done | bytes 1441808 | tf_op jit(solution)/shard_map/reduce_scatter | solution.py:157
  (210 shorter events, 221.3 us)
Async XLA Ops:
  7.2 219.7 %all-gather.6.cloned.1.call-start = ((), (), s32[]{:S(2)}) async-start(), calls=%async_computation.7 | async-start | bytes 8650752 | tf_op jit(solution)/shard_map/all_gather | solution.py:78
  9.1 285.9 %all-gather.8.cloned.1.call-start = ((), (), s32[]{:S(2)}) async-start(), calls=%async_computation.8 | async-start | bytes 8650752 | tf_op jit(solution)/shard_map/all_gather | solution.py:81
  11.0 50.5 %copy-start.53 = (s32[1,6]{1,0:T(1,128)S(1)}, s32[1,6]{1,0:T(1,128)}, u32[]{:S(2)}) copy-start(s32[1,6]{1,0:T(1,128)} %param.13) | copy-start | bytes 76
  11.0 50.8 %copy-start = (bf16[1,512,2048]{2,1,0:T(8,128)(2,1)S(1)}, bf16[1,512,2048]{2,1,0:T(8,128)(2,1)}, u32[]{:S(2)}) copy-start(bf16[1,512,2048]{2,1,0:T(8,128)(2,1)} %param.12) | copy-start | bytes 6291460
  11.0 315.1 %all-gather.10.cloned.1.call-start = ((), (), s32[]{:S(2)}) async-start(), calls=%async_computation.9 | async-start | bytes 23789568 | tf_op jit(solution)/shard_map/all_gather | solution.py:85
  13.5 458.6 %all-gather.12.cloned.1.call-start = ((), (), s32[]{:S(2)}) async-start(), calls=%async_computation.10 | async-start | bytes 23789568 | tf_op jit(solution)/shard_map/all_gather | solution.py:86
  14.5 603.1 %all-gather.14.cloned.1.call-start = ((), (), s32[]{:S(2)}) async-start(), calls=%async_computation.11 | async-start | bytes 23789568 | tf_op jit(solution)/shard_map/all_gather | solution.py:87
  16.9 954.5 %reduce-scatter.10.cloned.1.call-start = ((), (), s32[]{:S(2)}) async-start(), calls=%async_computation.13 | async-start | bytes 1081344 | tf_op jit(solution)/shard_map/reduce_scatter | solution.py:202
  60.0 179.4 %copy-start.40 = (f32[2048]{0:T(1024)}, f32[2048]{0:T(1024)S(1)}, u32[]{:S(2)}) copy-start(f32[2048]{0:T(1024)S(1)} %convert_element_type.169) | copy-start | bytes 24580
  61.7 155.4 %copy-start.51 = (f32[64]{0:T(128)}, f32[64]{0:T(128)S(1)}, u32[]{:S(2)}) copy-start(f32[64]{0:T(128)S(1)} %multiply_exponential_fusion) | copy-start | bytes 772
  61.8 155.3 %copy-start.43 = (f32[512]{0:T(512)}, f32[512]{0:T(512)S(1)}, u32[]{:S(2)}) copy-start(f32[512]{0:T(512)S(1)} %subtract_convert_fusion.1) | copy-start | bytes 6148
  62.9 149.9 %copy-start.45 = (f32[512]{0:T(512)}, f32[512]{0:T(512)S(1)}, u32[]{:S(2)}) copy-start(f32[512]{0:T(512)S(1)} %get-tuple-element.36) | copy-start | bytes 6148
  137.0 75.8 %copy-start.13 = (bf16[2048,128]{1,0:T(8,128)(2,1)}, bf16[2048,128]{1,0:T(8,128)(2,1)S(1)}, u32[]{:S(2)}) copy-start(bf16[2048,128]{1,0:T(8,128)(2,1)S(1)} %all_gather.28) | copy-start | bytes 1572868
  212.9 12.9 collective-permute-start
  219.9 58.4 %copy-start.7 = (pred[512,1024]{0,1:T(8,128)(4,1)}, pred[512,1024]{0,1:T(8,128)(4,1)S(1)}, u32[]{:S(2)}) copy-start(pred[512,1024]{0,1:T(8,128)(4,1)S(1)} %fusion.41) | copy-start | bytes 1572868
  226.9 51.5 %copy-start.17 = (bf16[1,1024,256]{1,2,0:T(8,128)(2,1)}, bf16[1,1024,256]{1,2,0:T(8,128)(2,1)S(1)}, u32[]{:S(2)}) copy-start(bf16[1,1024,256]{1,2,0:T(8,128)(2,1)S(1)} %maximum_maximum_fusion) | copy-start | bytes 1572868
  305.2 166.9 %copy-start.11 = (bf16[512,2048]{1,0:T(8,128)(2,1)}, bf16[512,2048]{1,0:T(8,128)(2,1)S(1)}, u32[]{:S(2)}) copy-start(bf16[512,2048]{1,0:T(8,128)(2,1)S(1)} %multiply_convert_fusion.3) | copy-start | bytes 6291460
  779.2 10.4 collective-permute-start.1
  792.8 269.1 %reduce-scatter.12.cloned.1.call-start = ((), (), s32[]{:S(2)}) async-start(), calls=%async_computation.14 | async-start | bytes 1081344 | tf_op jit(solution)/shard_map/reduce_scatter | solution.py:203
  794.9 631.0 %reduce-scatter.8.cloned.1.call-start = ((), (), s32[]{:S(2)}) async-start(), calls=%async_computation.12 | async-start | bytes 17301504 | tf_op jit(solution)/shard_map/reduce_scatter | solution.py:201
  814.0 977.0 %reduce-scatter.14.cloned.1.call-start = ((), (), s32[]{:S(2)}) async-start(), calls=%async_computation.15 | async-start | bytes 17301504 | tf_op jit(solution)/shard_map/reduce_scatter | solution.py:204
  825.9 1938.1 %reduce-scatter.16.cloned.1.call-start = ((), (), s32[]{:S(2)}) async-start(), calls=%async_computation.16 | async-start | bytes 47579136 | tf_op jit(solution)/shard_map/reduce_scatter | solution.py:155
  848.5 2891.2 %reduce-scatter.18.cloned.1.call-start = ((), (), s32[]{:S(2)}) async-start(), calls=%async_computation.17 | async-start | bytes 47579136 | tf_op jit(solution)/shard_map/reduce_scatter | solution.py:156
  869.5 3845.7 %reduce-scatter.20.cloned.1.call-start = ((), (), s32[]{:S(2)}) async-start(), calls=%async_computation.18 | async-start | bytes 47579136 | tf_op jit(solution)/shard_map/reduce_scatter | solution.py:157
  (47 other events, 523.4 us)
Sparse Core Ops, SparseCore 0:
  11.5 81.5 all-gather.5
  96.1 80.0 all-gather.7
  179.6 146.4 all-gather.9
  329.4 142.7 all-gather.11
  474.9 142.7 all-gather.13
  793.0 133.7 reduce-scatter.9
  929.7 132.2 reduce-scatter.11
  1064.8 361.0 reduce-scatter.7
  1428.7 362.1 reduce-scatter.13
  1793.6 970.2 reduce-scatter.15
  2766.9 972.7 reduce-scatter.17
  3742.4 972.7 reduce-scatter.19
where the time goes:
time: 4730 us; the launch traced here: 4720 us
  waiting for transfers between devices  4030 us (85%)
  matrix products  340 us (7%)
  blocking collectives  229 us (5%)
  other arithmetic  69.9 us (1%)
    reduce_scatter x1, waiting for transfers between devices, on_device(): lax.psum_scatter(up_term, ('dp', 'seq'), scatter_dimension=0, tiled=True)  976 us
    reduce_scatter x1, waiting for transfers between devices, on_device(): lax.psum_scatter(down_term, ('dp', 'seq'), scatter_dimension=0, tiled=True)  976 us
    reduce_scatter x1, waiting for transfers between devices, on_device(): lax.psum_scatter(gate_term, ('dp', 'seq'), scatter_dimension=0, tiled=True)  973 us
    reduce_scatter x1, waiting for transfers between devices, on_device(): lax.psum_scatter(out_term, ('dp', 'seq'), scatter_dimension=0, tiled=True)  365 us
    reduce_scatter x1, waiting for transfers between devices, on_device(): lax.psum_scatter(query_term, ('dp', 'seq'), scatter_dimension=0, tiled=True)  364 us
    dot_general x21, matrix products, matmul(): return jnp.dot(left, right, preferred_element_type=jnp.float32)  248 us
    all_gather x1, waiting for transfers between devices, on_device(): lax.all_gather(w_up.astype(half_type), ('dp', 'seq'), axis=0, tiled=True)  127 us
    all_gather x1, waiting for transfers between devices, on_device(): lax.all_gather(w_down.astype(half_type), ('dp', 'seq'), axis=0, tiled=True)  126 us
  transfers between devices with their start and end apart: 14, of which 11 were waited for; matrix products, arithmetic and copies ran while one was open for 6% of the time, Pallas kernels for 0%

commit v1 on v0

v1 whole, which is shorter than its diff:
```python
import functools
import math

import jax
import jax.numpy as jnp
from jax import lax
from jax.experimental import pallas as pl
from jax.experimental.pallas import tpu as pltpu
from jax.sharding import PartitionSpec as P

HEADS = 16
HEAD = 128
WINDOW = 512


EPS = 1e-05


def shifted(value, axis, steps):
    count = lax.axis_size(axis)
    initial, last = (max(0, -steps), min(count, count - steps))
    return lax.ppermute(value, axis, [(source, source + steps) for source in range(initial, last)])


def documents(doc_lengths, index):
    ends = jnp.cumsum(doc_lengths, axis=-1)
    passed = (index[None, :, None] >= ends[:, None, :]).astype(jnp.int32)
    segment = jnp.sum(passed, axis=-1)
    before = jnp.sum(passed * doc_lengths[:, None, :], axis=-1)
    return (segment, index[None, :] - before)


def rope_tables(position):
    half = HEAD // 2
    freq = jnp.exp(jnp.arange(half, dtype=jnp.float32) * (-2.0 * math.log(10000.0) / HEAD))
    angles = position.astype(jnp.float32)[..., None] * freq
    return (jnp.cos(angles), jnp.sin(angles))


def rotate(vec, cosine, sine):
    half = vec.shape[-1] // 2
    first = vec[..., :half]
    second = vec[..., half:]
    return jnp.concatenate(
        [first * cosine - second * sine, second * cosine + first * sine], axis=-1
    )


def norm_back(grad_normed, rows, scale, gain):
    inner = grad_normed * gain
    grad_gain = jnp.sum(grad_normed * rows * scale, axis=0)
    grad_rows = scale * inner - rows * (scale * scale * scale) * jnp.mean(
        inner * rows, axis=-1, keepdims=True
    )
    return (grad_rows, grad_gain)


def matmul(left, right):
    return jnp.dot(left, right, preferred_element_type=jnp.float32)


def after(values, *others):
    return lax.optimization_barrier((values, others))[0]


def partner(value, bit):
    count = lax.axis_size("dp")
    return lax.ppermute(value, "dp", [(source, source ^ (1 << bit)) for source in range(count)])


def around(value, steps):
    count = lax.axis_size("seq")
    return lax.ppermute(
        value, "seq", [(source, (source + steps) % count) for source in range(count)]
    )


def dp_bits():
    return lax.axis_size("dp").bit_length() - 1


MIB = 1 << 20
ANYWHERE = pl.BlockSpec(memory_space=pl.ANY)


def kernel_params(flops, traffic):
    return {
        "compiler_params": pltpu.CompilerParams(vmem_limit_bytes=58 * MIB),
        "cost_estimate": pl.CostEstimate(flops=flops, bytes_accessed=traffic, transcendentals=0),
    }


def owner(number):
    return lax.bitwise_xor(lax.axis_index("dp"), number)


def rows_kernel(count, gained, near, left, *refs):
    pieces, rest = refs[:count], refs[count:]
    if gained:
        out, normed, gains, held, sems = rest
    else:
        out, held, sems = rest
    step = pl.program_id(0)
    rows, columns = held.shape[1], out.shape[1]
    copies = [
        pltpu.make_async_copy(piece, held.at[number], sems.at[number])
        for number, piece in enumerate(pieces)
    ]

    @pl.when(step == 0)
    def _():
        for copy in copies:
            copy.start()

    for number, copy in enumerate(copies):

        @pl.when(step == number)
        def _(copy=copy):
            copy.wait()

    start = pl.multiple_of(owner(step) * rows, rows)
    block = left[:, pl.ds(start, rows)]
    if gained:
        turned = held[step, :, columns:].astype(jnp.float32).T
        gains[...] = turned[:8]
        block = (block * turned[:1]).astype(normed.dtype)
        normed[...] = block
    part = matmul(block, held[step, :, :columns])

    @pl.when(step == 0)
    def _():
        out[...] = part

    @pl.when(step > 0)
    def _():
        out[...] += part


def near_places(count):
    return lax.bitwise_xor(lax.axis_index("dp"), jnp.arange(count, dtype=jnp.int32))


def by_rows(left, held, columns):
    count, (rows, wide) = len(held), held[0].shape
    tokens = left.shape[0]
    gained = wide > columns
    out_shape = [jax.ShapeDtypeStruct((tokens, columns), jnp.float32)]
    out_specs = [pl.BlockSpec((tokens, columns), lambda step, near: (0, 0))]
    if gained:
        out_shape += [
            jax.ShapeDtypeStruct(left.shape, held[0].dtype),
            jax.ShapeDtypeStruct((8, left.shape[1]), jnp.float32),
        ]
        out_specs += [
            pl.BlockSpec((tokens, rows), lambda step, near: (0, near[step])),
            pl.BlockSpec((8, rows), lambda step, near: (0, near[step])),
        ]
    return pl.pallas_call(
        functools.partial(rows_kernel, count, gained),
        out_shape=out_shape,
        grid_spec=pltpu.PrefetchScalarGridSpec(
            num_scalar_prefetch=1,
            grid=(count,),
            in_specs=[pl.BlockSpec(left.shape, lambda step, near: (0, 0))] + [ANYWHERE] * count,
            out_specs=out_specs,
            scratch_shapes=[
                pltpu.VMEM((count, rows, wide), held[0].dtype),
                pltpu.SemaphoreType.DMA((count,)),
            ],
        ),
        **kernel_params(2 * tokens * count * rows * columns, 2 * count * rows * columns),
    )(near_places(count), left, *[held[place] for place in range(count)])


def back_kernel(count, many, near, *refs):
    lefts = refs[:many]
    pieces = refs[many : many + many * count]
    out, held, sems = refs[many + many * count :]
    step = pl.program_id(0)

    def copy(number, which, slot):
        return pltpu.make_async_copy(
            pieces[which * count + number], held.at[slot, which], sems.at[slot, which]
        )

    for number in range(count):

        @pl.when(step == max(number - 1, 0))
        def _(number=number):
            for which in range(many):
                copy(number, which, number % 2).start()

    slot = lax.rem(step, 2)
    total = None
    for which in range(many):
        copy(0, which, slot).wait()
        part = lax.dot_general(
            lefts[which][...],
            held[slot, which, :, : lefts[which].shape[1]],
            (((1,), (1,)), ((), ())),
            preferred_element_type=jnp.float32,
        )
        total = part if total is None else total + part
    out[...] = total.astype(out.dtype)


def back_by_rows(lefts, helds, dtype):
    count, many = len(helds[0]), len(lefts)
    rows, wide = helds[0][0].shape
    tokens, columns = lefts[0].shape
    near = near_places(count)
    return pl.pallas_call(
        functools.partial(back_kernel, count, many),
        out_shape=jax.ShapeDtypeStruct((tokens, count * rows), dtype),
        grid_spec=pltpu.PrefetchScalarGridSpec(
            num_scalar_prefetch=1,
            grid=(count,),
            in_specs=[pl.BlockSpec((tokens, columns), lambda step, near: (0, 0))] * many
            + [ANYWHERE] * (many * count),
            out_specs=pl.BlockSpec((tokens, rows), lambda step, near: (0, near[step])),
            scratch_shapes=[
                pltpu.VMEM((2, many, rows, wide), helds[0][0].dtype),
                pltpu.SemaphoreType.DMA((2, many)),
            ],
        ),
        **kernel_params(
            2 * tokens * many * count * rows * columns, 2 * many * count * rows * columns
        ),
    )(near, *lefts, *[held[place] for held in helds for place in range(count)])


def gate_kernel(count, left, *refs):
    pieces = refs[: 2 * count]
    gate, up, hidden, turned, held, sems = refs[2 * count :]
    step, steps = pl.program_id(0), pl.num_programs(0)
    rows, tile = pieces[0].shape[0], gate.shape[1]

    def copies(number, slot):
        column = pl.multiple_of(number * tile, tile)
        for which in range(2):
            for place in range(count):
                start = pl.multiple_of(owner(place) * rows, rows)
                yield pltpu.make_async_copy(
                    pieces[which * count + place].at[:, pl.ds(column, tile)],
                    held.at[slot, which, pl.ds(start, rows), :],
                    sems.at[slot, which, place],
                )

    @pl.when(step == 0)
    def _():
        for copy in copies(0, 0):
            copy.start()

    @pl.when(step + 1 < steps)
    def _():
        for copy in copies(step + 1, lax.rem(step + 1, 2)):
            copy.start()

    slot = lax.rem(step, 2)
    for copy in copies(step, slot):
        copy.wait()
    gate_tile = matmul(left[...], held[slot, 0])
    gate[...] = gate_tile
    up_tile = matmul(left[...], held[slot, 1])
    up[...] = up_tile
    value = (gate_tile * jax.nn.sigmoid(gate_tile) * up_tile).astype(hidden.dtype)
    hidden[...] = value
    turned[...] = value.T


def gate_up(left, gates, ups):
    count, (rows, columns) = len(gates), gates[0].shape
    tokens = left.shape[0]
    tile = next(size for size in (512, 256, 128) if columns % size == 0)
    across = pl.BlockSpec((tokens, tile), lambda step: (0, step))
    return pl.pallas_call(
        functools.partial(gate_kernel, count),
        out_shape=[
            jax.ShapeDtypeStruct((tokens, columns), jnp.float32),
            jax.ShapeDtypeStruct((tokens, columns), jnp.float32),
            jax.ShapeDtypeStruct((tokens, columns), left.dtype),
            jax.ShapeDtypeStruct((columns, tokens), left.dtype),
        ],
        grid=(columns // tile,),
        in_specs=[pl.BlockSpec(left.shape, lambda step: (0, 0))] + [ANYWHERE] * (2 * count),
        out_specs=[across, across, across, pl.BlockSpec((tile, tokens), lambda step: (step, 0))],
        scratch_shapes=[
            pltpu.VMEM((2, 2, count * rows, tile), left.dtype),
            pltpu.SemaphoreType.DMA((2, 2, count)),
        ],
        **kernel_params(
            4 * tokens * count * rows * columns, 4 * columns * (count * rows + 3 * tokens)
        ),
    )(left, *[held[place] for held in (gates, ups) for place in range(count)])


def down_kernel(count, together, near, hidden, gate, up, cot, mid, *refs):
    pieces = refs[: 2 * count]
    output, grad_gate, grad_up, held, total, sems = refs[2 * count :]
    step, steps = pl.program_id(0), pl.num_programs(0)
    rows, side = pieces[0].shape

    def copies(number, slot):
        for part in range(together):
            spot = lax.rem(owner(part), together)
            start = pl.multiple_of(spot * rows, rows)
            for which in range(2):
                yield pltpu.make_async_copy(
                    pieces[which * count + number * together + part],
                    held.at[slot, pl.ds(start, rows), which * side : (which + 1) * side],
                    sems.at[slot, part, which],
                )

    for number in range(count // together):

        @pl.when(step == max(number - 1, 0))
        def _(number=number):
            for copy in copies(number, number % 2):
                copy.start()

    slot = lax.rem(step, 2)
    for copy in copies(0, slot):
        copy.wait()
    chunk = 128

    @pl.loop(0, cot.shape[0] // chunk)
    def _(index):
        start = pl.ds(pl.multiple_of(index * chunk, chunk), chunk)
        weight = held[slot]
        grad = lax.dot_general(
            cot[start, :], weight, (((1,), (1,)), ((), ())), preferred_element_type=jnp.float32
        )
        gate_rows, up_rows = gate[start, :], up[start, :]
        sigma = jax.nn.sigmoid(gate_rows)
        grad_up[start, :] = (grad * (gate_rows * sigma)).astype(grad_up.dtype)
        grad_gate[start, :] = (
            grad * up_rows * (sigma * (1.0 + gate_rows * (1.0 - sigma)))
        ).astype(grad_gate.dtype)
        added = matmul(hidden[start, :], weight)

        @pl.when(step == 0)
        def _():
            total[start, :] = mid[start, :] + added

        @pl.when(step > 0)
        def _():
            total[start, :] += added

    @pl.when(step == steps - 1)
    def _():
        output[...] = total[...].astype(output.dtype)


def down_and_back(hidden, gate, up, cot, mid, helds):
    count, (rows, side) = len(helds[0]), helds[0][0].shape
    tokens, width = cot.shape
    together = next(size for size in (1, 2, 4, 8, 16) if size * rows % 128 == 0)
    tile = together * rows
    dp = lax.axis_index("dp")
    near = lax.bitwise_xor(
        lax.div(dp, together), jnp.arange(count // together, dtype=jnp.int32)
    )
    across = pl.BlockSpec((tokens, tile), lambda step, near: (0, near[step]))

    def fixed(size):
        return pl.BlockSpec((tokens, size), lambda step, near: (0, 0))

    columns = count * rows
    return pl.pallas_call(
        functools.partial(down_kernel, count, together),
        out_shape=[
            jax.ShapeDtypeStruct((tokens, width), jnp.bfloat16),
            jax.ShapeDtypeStruct((tokens, columns), jnp.bfloat16),
            jax.ShapeDtypeStruct((tokens, columns), jnp.bfloat16),
        ],
        grid_spec=pltpu.PrefetchScalarGridSpec(
            num_scalar_prefetch=1,
            grid=(count // together,),
            in_specs=[across, across, across, fixed(width), fixed(width)]
            + [ANYWHERE] * (2 * count),
            out_specs=[fixed(width), across, across],
            scratch_shapes=[
                pltpu.VMEM((2, tile, width), hidden.dtype),
                pltpu.VMEM((tokens, width), jnp.float32),
                pltpu.SemaphoreType.DMA((2, together, 2)),
            ],
        ),
        **kernel_params(4 * tokens * width * columns, 2 * columns * (width + 7 * tokens)),
    )(
        near, hidden, gate, up, cot, mid,
        *[held[place] for held in helds for place in range(count)],
    )


class Flow:
    def __init__(self):
        self.ended = []

    def round(self, moves):
        values = after([value for value, _ in moves], self.ended)
        got = [partner(value, bit) for value, (_, bit) in zip(values, moves)]
        self.ended = list(got)
        return got

    def holds(self, *results):
        self.ended.extend(results)


class Spreads:
    def __init__(self, order):
        self.order, self.helds = order, [{}, {}]

    def direct(self, flow, number, line, also=()):
        held = self.helds[number]
        held[0] = line
        moves = [(line, 0)] + [(line, bit) for bit in self.order] + list(also)
        got = flow.round(moves)
        held[1] = got[0]
        for bit, piece in zip(self.order, got[1:]):
            held[1 << bit] = piece
        return got[1 + len(self.order) :]

    def double(self):
        return [
            (number, place)
            for number, held in enumerate(self.helds)
            for place in sorted(held)
            if not place & 1 and place | 1 not in held
        ]

    def moves(self, names):
        return [(self.helds[number][place], 0) for number, place in names]

    def put(self, names, got):
        for (number, place), piece in zip(names, got):
            self.helds[number][place | 1] = piece

    def cross(self, flow, level, also):
        names, targets, moves = self.double(), [], []
        for number, turn in enumerate((self.order, self.order[::-1])):
            for place in range(2 << len(self.order)):
                bits = [bit for bit in turn if place >> bit & 1]
                if not place & 1 and len(bits) == level:
                    targets.append((number, place))
                    moves.append((self.helds[number][place ^ (1 << bits[-1])], bits[-1]))
        got = flow.round(moves + self.moves(names) + list(also))
        for (number, place), piece in zip(targets, got):
            self.helds[number][place] = piece
        end = len(targets) + len(names)
        self.put(names, got[len(targets) : end])
        return got[end:]

    def crosses(self, flow, also=()):
        extra = []
        for level in range(2, len(self.order) + 1):
            extra += self.cross(flow, level, also if level == 2 else ())
        return extra


def places_of(order):
    places = [0]
    for bit in reversed(order):
        places = places + [place | (1 << bit) for place in places]
    return places


def arranged(turned, order):
    dp, me = lax.axis_size("dp"), lax.axis_index("dp")
    block = turned.shape[0] // dp
    return jnp.concatenate(
        [
            lax.dynamic_slice_in_dim(turned, lax.bitwise_xor(me, place) * block, block, 0)
            for place in places_of(order)
        ],
        axis=0,
    )


class Scattered:
    def __init__(self, turned, right, order):
        self.lhs, self.right, self.order = arranged(turned, order), right, order
        self.arrived, self.step = [], 0

    def total(self, rows, parts):
        total = matmul(rows, self.right)
        for part in parts:
            total = total + part.astype(jnp.float32)
        return total

    def send(self):
        half = self.lhs.shape[0] // 2
        sent = self.total(self.lhs[half:], [part[half:] for part in self.arrived])
        self.sent = sent.astype(jnp.bfloat16)
        self.lhs = self.lhs[:half]
        self.arrived = [part[:half] for part in self.arrived]
        return self.sent

    def move(self):
        return (self.sent, self.order[self.step])

    def receive(self, got):
        self.arrived.append(got)
        self.step += 1

    def line(self):
        self.sent = self.total(self.lhs, self.arrived).astype(jnp.bfloat16)
        return self.sent


def finish(jobs):
    sent = jnp.concatenate([job.sent for job in jobs], axis=1)
    return lax.psum_scatter(sent, "seq", scatter_dimension=0, tiled=True).astype(jnp.float32)


def on_device(
    tokens,
    lengths,
    gain_one,
    w_query,
    w_key,
    w_value,
    w_out,
    gain_two,
    w_gate,
    w_up,
    w_down,
    cotangent,
):
    half_type = jnp.bfloat16
    batch, group, width = tokens.shape
    count = batch * group
    upper = tuple(range(1, dp_bits()))
    inner = w_query.shape[1]
    middle = w_down.shape[1] // 2

    def along(shard):
        return lax.all_gather(shard, "seq", axis=0, tiled=True)

    gains = jnp.stack([gain_one, gain_two], axis=1)
    first = jnp.concatenate(
        [w_query, w_key, w_value, jnp.pad(gains, ((0, 0), (0, HEAD - 2)))], axis=1
    ).astype(half_type)
    columns_first = inner + 2 * HEAD
    flow = Flow()
    line_first = along(first)
    line_out = along(after(w_out.astype(half_type), line_first))
    line_gate = along(after(w_gate.astype(half_type), line_out))
    line_up = along(after(w_up.astype(half_type), line_gate))
    down_half = w_down.astype(half_type)
    line_left = along(after(down_half[:, :middle], line_up))
    line_right = along(after(down_half[:, middle:], line_left))
    one_spread, two_spread, three_spread = Spreads(upper), Spreads(upper), Spreads(upper)
    one_spread.direct(flow, 0, line_first)
    flow.holds(line_out)
    one_spread.direct(flow, 1, line_out)
    one_spread.crosses(flow)
    flow.holds(line_gate)
    left_over = one_spread.double()
    got = two_spread.direct(flow, 0, line_gate, one_spread.moves(left_over))
    one_spread.put(left_over, got)
    full_one = one_spread.helds

    reach = (WINDOW - 2) // group + 1
    offset = lax.axis_index("seq") * group
    query_at = offset + jnp.arange(group, dtype=jnp.int32)
    key_at = offset - reach * group + jnp.arange((reach + 1) * group, dtype=jnp.int32)
    query_seg, query_pos = documents(lengths, query_at)
    key_seg = documents(lengths, key_at)[0]
    allowed = (
        (key_at[None, :] >= 0)
        & (query_at[:, None] >= key_at[None, :])
        & (query_at[:, None] - key_at[None, :] < WINDOW)
    )
    allowed = (allowed[None] & (query_seg[:, :, None] == key_seg[:, None, :]))[:, None]
    cosine, sine = rope_tables(query_pos)
    factor = 1.0 / math.sqrt(HEAD)
    rows = tokens.astype(jnp.float32).reshape(count, width)
    scale_one = lax.rsqrt(jnp.mean(rows * rows, axis=-1, keepdims=True) + EPS)
    mapped, normed, gain_rows = by_rows(rows * scale_one, full_one[0], columns_first)
    gain_a, gain_b = gain_rows[0], gain_rows[1]
    query = mapped[:, :inner].reshape(batch, group, HEADS, HEAD)
    key = mapped[:, inner : inner + HEAD].reshape(batch, group, HEAD)
    value = mapped[:, inner + HEAD :].astype(half_type).reshape(batch, group, HEAD)
    query_turned = rotate(query, cosine[:, :, None, :], sine[:, :, None, :]).astype(half_type)
    key_turned = rotate(key, cosine, sine).astype(half_type)
    paired = jnp.concatenate([key_turned, value], axis=-1)
    pieces = []
    for step in range(reach, 0, -1):
        pieces.append(shifted(paired, "seq", step))
    pieces.append(paired)
    seen = jnp.concatenate(pieces, axis=1)
    keys_seen = seen[..., :HEAD]
    values_seen = seen[..., HEAD:]

    def scores_of():
        raw = jnp.einsum(
            "bqhe,bke->bhqk", query_turned, keys_seen, preferred_element_type=jnp.float32
        )
        return jnp.where(allowed, raw * factor, -1e30)

    scores = scores_of()
    flow.holds(line_up, query_turned)
    two_spread.direct(flow, 1, line_up)
    top = jnp.max(scores, axis=-1, keepdims=True)
    weight = jnp.exp(scores - top)
    total = jnp.sum(weight, axis=-1, keepdims=True)
    log_total = top + jnp.log(total)
    probs = (weight / total).astype(half_type)
    mixed = jnp.einsum("bhqk,bke->bqhe", probs, values_seen, preferred_element_type=jnp.float32)
    mixed = mixed.astype(half_type).reshape(count, HEADS * HEAD)
    mid = rows + by_rows(mixed, full_one[1], width)[0]
    scale_two = lax.rsqrt(jnp.mean(mid * mid, axis=-1, keepdims=True) + EPS)
    normed_two = (mid * scale_two * gain_b).astype(half_type)

    flow.holds(normed_two, line_left)
    two_spread.crosses(flow)
    flow.holds(line_right)
    left_over = two_spread.double()
    got = three_spread.direct(flow, 0, line_left, two_spread.moves(left_over))
    two_spread.put(left_over, got)
    full_two = two_spread.helds
    gate, up_val, hidden, hidden_turned = gate_up(normed_two, *full_two)

    grad_out = cotangent.reshape(count, width)
    orders = ((0,) + upper, (0,) + upper[::-1])
    three = [
        Scattered(hidden_turned, grad_out[:, :middle], orders[0]),
        Scattered(hidden_turned, grad_out[:, middle:], orders[1]),
    ]

    def send(jobs):
        return [job.send() for job in jobs]

    three_spread.direct(flow, 1, line_right)
    flow.holds(*send(three))
    got = three_spread.crosses(flow, [job.move() for job in three])
    for job, piece in zip(three, got):
        job.receive(piece)
    send(three)
    left_over = three_spread.double()

    def exchange(jobs, also=()):
        got = flow.round([job.move() for job in jobs] + list(also))
        for job, piece in zip(jobs, got):
            job.receive(piece)
        return got[len(jobs) :]

    got = exchange(three, three_spread.moves(left_over))
    three_spread.put(left_over, got)
    full_three = three_spread.helds
    output, grad_gate, grad_up = down_and_back(hidden, gate, up_val, grad_out, mid, full_three)
    output = output.reshape(batch, group, width)
    turned_two = normed_two.T
    two = [Scattered(turned_two, grad_gate, orders[0]), Scattered(turned_two, grad_up, orders[1])]
    flow.holds(*send(two))
    for step in range(len(upper) - 1):
        send(three)
        if step == 0:
            got = exchange(three, [job.move() for job in two])
            for job, piece in zip(two, got):
                job.receive(piece)
        else:
            exchange(three)
    done = [job.line() for job in three]
    sent = send(two)
    grad_gate, grad_up = after((grad_gate, grad_up), sent, done)
    exchange(two)
    down_done = finish(three)
    grad_normed_two = back_by_rows([grad_gate, grad_up], full_two, jnp.float32)
    back_mid, gain_two_term = norm_back(grad_normed_two, mid, scale_two, gain_b)
    grad_mid = grad_out.astype(jnp.float32) + back_mid
    grad_branch = grad_mid.astype(half_type)
    one_b = Scattered(mixed.T, grad_branch, orders[1])
    sent = one_b.send()
    grad_branch = after(grad_branch, sent)
    grad_mixed = back_by_rows([grad_branch], full_one[1:], half_type).reshape(batch, group, HEADS, HEAD)
    probs_full = jnp.exp(scores_of() - log_total)
    grad_probs = jnp.einsum(
        "bqhe,bke->bhqk", grad_mixed, values_seen, preferred_element_type=jnp.float32
    )
    grad_values = jnp.einsum(
        "bhqk,bqhe->bke", probs, grad_mixed, preferred_element_type=jnp.float32
    )
    centre = jnp.sum(probs_full * grad_probs, axis=-1, keepdims=True)
    grad_scores = (probs_full * (grad_probs - centre)).astype(half_type)
    flow.holds(grad_scores)
    for step in range(len(upper) - 1):
        sent = send(two)
        grad_scores = after(grad_scores, sent)
        if step == 0:
            one_b.receive(exchange(two, [one_b.move()])[0])
        else:
            exchange(two)
    grad_query = (
        jnp.einsum("bhqk,bke->bqhe", grad_scores, keys_seen, preferred_element_type=jnp.float32)
        * factor
    )
    grad_keys = (
        jnp.einsum("bhqk,bqhe->bke", grad_scores, query_turned, preferred_element_type=jnp.float32)
        * factor
    )
    grad_seen = jnp.concatenate([grad_keys, grad_values], axis=-1)
    own = grad_seen[:, reach * group :]
    for step in range(1, reach + 1):
        part = grad_seen[:, (reach - step) * group : (reach - step + 1) * group]
        own = own + shifted(part.astype(jnp.bfloat16), "seq", -step).astype(part.dtype)
    grad_key = rotate(own[..., :HEAD], cosine, -sine).astype(half_type).reshape(count, HEAD)
    grad_value = own[..., HEAD:].astype(half_type).reshape(count, HEAD)
    grad_q = (
        rotate(grad_query, cosine[:, :, None, :], -sine[:, :, None, :])
        .astype(half_type)
        .reshape(count, HEADS * HEAD)
    )
    grad_first = jnp.concatenate([grad_q, grad_key, grad_value], axis=1)
    one_a = Scattered(normed.T, grad_first, orders[0])
    sent = one_a.send()
    one = [one_a, one_b]
    done = [job.line() for job in two]
    gate_done, up_done = [finish([job]) for job in two]
    grad_first = after(grad_first, sent, done)
    grad_normed = back_by_rows([grad_first], full_one[:1], jnp.float32)
    back_rows, gain_one_term = norm_back(grad_normed, rows, scale_one, gain_a)
    grad_rows = (grad_mid + back_rows).astype(half_type).reshape(batch, group, width)
    gain_terms = jnp.stack([gain_one_term, gain_two_term])
    one_a.receive(flow.round([one_a.move()])[0])
    bits = [0] + list(upper)
    for step in range(len(upper)):
        send(one)
        got = exchange(one, [(gain_terms, bits.pop(0))])
        gain_terms = gain_terms + got[0]
    done = [job.line() for job in one]
    one_done = finish(one)
    first_done, out_done = one_done[:, : one_done.shape[1] - width], one_done[:, -width:]
    for bit in bits:
        gain_terms = gain_terms + partner(gain_terms, bit)
    gain_terms = sum(
        [around(gain_terms, steps) for steps in range(1, lax.axis_size("seq"))], gain_terms
    )
    owned = gain_one.shape[0]
    mine = (lax.axis_index("dp") * lax.axis_size("seq") + lax.axis_index("seq")) * owned
    gain_done = lax.dynamic_slice_in_dim(gain_terms, mine, owned, 1)
    return (
        output,
        grad_rows,
        gain_done[0],
        first_done[:, :inner],
        first_done[:, inner : inner + HEAD],
        first_done[:, inner + HEAD :],
        out_done,
        gain_done[1],
        gate_done,
        up_done,
        down_done,
    )


def solution(mesh):
    in_specs = (
        P("dp", "seq", None),
        P("dp", None),
        P(("dp", "seq")),
        P(("dp", "seq"), None),
        P(("dp", "seq"), None),
        P(("dp", "seq"), None),
        P(("dp", "seq"), None),
        P(("dp", "seq")),
        P(("dp", "seq"), None),
        P(("dp", "seq"), None),
        P(("dp", "seq"), None),
        P("dp", "seq", None),
    )
    out_specs = (
        P("dp", "seq", None),
        P("dp", "seq", None),
        P(("dp", "seq")),
        P(("dp", "seq"), None),
        P(("dp", "seq"), None),
        P(("dp", "seq"), None),
        P(("dp", "seq"), None),
        P(("dp", "seq")),
        P(("dp", "seq"), None),
        P(("dp", "seq"), None),
        P(("dp", "seq"), None),
    )
    return jax.shard_map(
        on_device, mesh=mesh, in_specs=in_specs, out_specs=out_specs, check_vma=False
    )
```

time: 4730 us -> 1080 us (0.23)
  waiting for transfers between devices: 4030 us -> 432 us
  blocking collectives: 229 us -> 0 us
  Pallas kernels: 0 us -> 190 us
  matrix products: 340 us -> 228 us
  starting transfers between devices: 6.31 us -> 53.9 us
    reduce_scatter x7 -> x4, waiting for transfers between devices: 3740 us -> 22 us  [finish(): lax.psum_scatter(sent, 'seq', scatter_dimension=0, tiled=True)]
    ppermute x0 -> x66, waiting for transfers between devices: none -> 300 us  [the longest x63 300 us: partner(): lax.ppermute(value, 'dp', [(source, source ^ 1 << bit) for source in rang...]
    pallas_call x0 -> x7, Pallas kernels: none -> 190 us  [the longest x3 64 us: back_by_rows(): pl.pallas_call(functools.partial(back_kernel, count, many), out_shape=jax...]
    all_gather x5 -> x6, waiting for transfers between devices: 274 us -> 103 us  [along(): return lax.all_gather(shard, 'seq', axis=0, tiled=True)]
    all_gather x2 -> x0, blocking collectives: 147 us -> none  [the longest x1 74.1 us: on_device(): lax.all_gather(w_key.astype(half_type), ('dp', 'seq'), axis=0, tiled=True)]
    dot_general x21 -> x24, matrix products: 248 us -> 132 us  [matmul(): return jnp.dot(left, right, preferred_element_type=jnp.float32)]
    unnamed x2 -> x0, blocking collectives: 81.2 us -> none
    ppermute x0 -> x66, starting transfers between devices: none -> 50.3 us  [the longest x63 37.6 us: partner(): lax.ppermute(value, 'dp', [(source, source ^ 1 << bit) for source in rang...]
  transfers between devices with their start and end apart: 14 -> 78, of which waited for: 11 -> 36; matrix products, arithmetic and copies ran while one was open for 6% -> 33% of each run, Pallas kernels for 0% -> 18%
where the time goes in v1:
time: 1080 us; the launch traced here: 1070 us
  waiting for transfers between devices  432 us (40%)
  matrix products  228 us (21%)
  Pallas kernels  190 us (18%)
  other arithmetic  105 us (10%)
  starting transfers between devices  53.9 us (5%)
  local copies, waits for them, and re-layouts  42.3 us (4%)
  between operations  15.6 us (1%)
    ppermute x63, waiting for transfers between devices, partner(): lax.ppermute(value, 'dp', [(source, source ^ 1 << bit) for source in rang...  300 us
    dot_general x24, matrix products, matmul(): return jnp.dot(left, right, preferred_element_type=jnp.float32)  132 us
    all_gather x6, waiting for transfers between devices, along(): return lax.all_gather(shard, 'seq', axis=0, tiled=True)  103 us
    pallas_call x3, Pallas kernels, back_by_rows(): pl.pallas_call(functools.partial(back_kernel, count, many), out_shape=jax...  64 us
    pallas_call x1, Pallas kernels, down_and_back(): pl.pallas_call(functools.partial(down_kernel, count, together), out_shape...  58.5 us
    ppermute x63, starting transfers between devices, partner(): lax.ppermute(value, 'dp', [(source, source ^ 1 << bit) for source in rang...  37.6 us
    pallas_call x1, Pallas kernels, gate_up(): pl.pallas_call(functools.partial(gate_kernel, count), out_shape=[jax.Shap...  36.2 us
    pallas_call x2, Pallas kernels, by_rows(): pl.pallas_call(functools.partial(rows_kernel, count, gained), out_shape=o...  31.6 us
  transfers between devices with their start and end apart: 78, of which 36 were waited for; matrix products, arithmetic and copies ran while one was open for 33% of the time, Pallas kernels for 18%

profile of v1, /device:TPU:0, one launch (start us, length us, event | category | flops | bytes accessed | tf_op | source)
XLA Modules:
  0.0 1067.3 jit_solution(10727629892562972717)
XLA Ops:
  13.5 32.6 %all-gather.7.cloned.1.call-done.refs_0_.refs_1_ = bf16[256,2432]{1,0:T(8,128)(2,1)} async-done(((bf16[64,2432]{1,0:T(8,128)(2,1)}), bf16[256,2432]{1,0:T(8,128)(2,1)}) %all-gather.7.cloned.1.call-update) | async-done | bytes 1245200 | tf_op jit(solution)/shard_map/all_gather | solution.py:537
  50.1 25.1 %all-gather.9.cloned.1.call-done.refs_0_.refs_1_ = bf16[256,2048]{1,0:T(8,128)(2,1)} async-done(((bf16[64,2048]{1,0:T(8,128)(2,1)}), bf16[256,2048]{1,0:T(8,128)(2,1)}) %all-gather.9.cloned.1.call-update) | async-done | bytes 1048592 | tf_op jit(solution)/shard_map/all_gather | solution.py:537
  78.3 22.1 %collective-permute-done.3.refs_4_.refs_5_ = bf16[256,2048]{1,0:T(8,128)(2,1)} collective-permute-done((bf16[256,2048]{1,0:T(8,128)(2,1)}, bf16[256,2048]{1,0:T(8,128)(2,1)}, u32[]{:S(2)}, u32[]{:S(2)}) %collective-permute-start.3) | collective-permute-done | bytes 1048608 | tf_op jit(solution)/shard_map/ppermute | solution.py:68
  110.6 19.6 %collective-permute-done.9.refs_6_.refs_7_ = bf16[256,2048]{1,0:T(8,128)(2,1)} collective-permute-done((bf16[256,2048]{1,0:T(8,128)(2,1)}, bf16[256,2048]{1,0:T(8,128)(2,1)}, u32[]{:S(2)}, u32[]{:S(2)}) %collective-permute-start.9) | collective-permute-done | bytes 1048608 | tf_op jit(solution)/shard_map/ppermute | solution.py:68
  144.4 17.1 %shard_map.203 = (f32[512,2304]{1,0:T(8,128)}, bf16[512,2048]{1,0:T(8,128)(2,1)}, f32[8,2048]{1,0:T(8,128)}) custom-call(s32[8]{0:T(128)} %iota_xor_fusion.near, f32[512,2048]{1,0:T(8,128)} %convert_multiply_fusion.3.left, bf16[256,2432]{1,0:T(8,128)(2,1)} %all-gather.7.cloned.1.call-done.refs_0_.refs_1_, ...), custom_call_target="tpu_custom_call" | custom-call | flops 4831838208 | bytes 9437184 | tf_op jit(solution)/shard_map/pallas_call | solution.py:158
  183.3 14.2 %fusion.4 = (f32[16,512]{1,0:T(8,128)S(1)}, f32[1024,512,16]{1,0,2:T(8,128)}) fusion(pred[512,1024]{0,1:T(8,128)(4,1)S(1)} %fusion.46, bf16[512,16,64]{2,0,1:T(8,128)(2,1)S(1)} %get-tuple-element.186, bf16[512,16,64]{2,0,1:T(8,128)(2,1)S(1)} %get-tuple-element.185, bf16[1,1024,256]{2,1,0:T(8,128)(2,1)S(1)} %maximum_maximum_fusion), kind=kOutput, calls=%fused_computation.10 | convolution fusion | flops 2176835584 | bytes 38567936 | tf_op jit(solution)/shard_map/bqhe,bke->bhqk/dot_general | solution.py:596
  197.6 14.4 %fusion.3 = f32[16,512]{1,0:T(8,128)S(1)} fusion(f32[1024,512,16]{1,0,2:T(8,128)} %get-tuple-element.239, f32[16,512]{1,0:T(8,128)S(1)} %get-tuple-element.238, pred[512,1024]{0,1:T(8,128)(4,1)S(1)} %fusion.46), kind=kLoop, calls=%fused_computation.9 | loop fusion | flops 33546240 | bytes 34144256 | tf_op jit(solution)/shard_map/reduce_sum | solution.py:606
  213.2 16.4 %fusion.49 = bf16[128,16,512]{2,0,1:T(8,128)(2,1)} fusion(bf16[1,1024,256]{2,1,0:T(8,128)(2,1)S(1)} %maximum_maximum_fusion, f32[1024,512,16]{1,0,2:T(8,128)} %get-tuple-element.239, f32[16,512]{1,0:T(8,128)S(1)} %fusion.3, f32[16,512]{1,0:T(8,128)S(1)} %get-tuple-element.238, pred[512,1024]{0,1:T(8,128)(4,1)S(1)} %fusion.46), kind=kOutput, calls=%fused_computation.104 | convolution fusion | flops 2190475264 | bytes 36503552 | tf_op jit(solution)/shard_map/bhqk,bke->bqhe/dot_general | solution.py:609
  233.5 14.5 %shard_map.204 = f32[512,2048]{1,0:T(8,128)} custom-call(s32[8]{0:T(128)} %iota_xor_fusion.near, bf16[512,2048]{1,0:T(8,128)(2,1)} %copy.86.left, bf16[256,2048]{1,0:T(8,128)(2,1)} %all-gather.9.cloned.1.call-done.refs_0_.refs_1_, bf16[256,2048]{1,0:T(8,128)(2,1)} %collective-permute-done.5.refs_1_.refs_2_, ...), custom_call_target="tpu_custom_call" | custom-call | flops 4294967296 | bytes 8388608 | tf_op jit(solution)/shard_map/pallas_call | solution.py:158
  256.2 20.6 %collective-permute-done.18.refs_12_.refs_14_ = bf16[256,5632]{1,0:T(8,128)(2,1)} collective-permute-done((bf16[256,5632]{1,0:T(8,128)(2,1)}, bf16[256,5632]{1,0:T(8,128)(2,1)}, u32[]{:S(2)}, u32[]{:S(2)}) %collective-permute-start.18) | collective-permute-done | bytes 2883616 | tf_op jit(solution)/shard_map/ppermute | solution.py:68
  287.1 41.4 %all-gather.17.cloned.1.call-done.refs_8_ = bf16[704,1024]{1,0:T(8,128)(2,1)} async-done(((bf16[176,1024]{1,0:T(8,128)(2,1)}), bf16[704,1024]{1,0:T(8,128)(2,1)}) %all-gather.17.cloned.1.call-update) | async-done | bytes 1441808 | tf_op jit(solution)/shard_map/all_gather | solution.py:537
  328.5 13.6 %collective-permute-done.23.refs_6_.refs_8_ = bf16[256,5632]{1,0:T(8,128)(2,1)} collective-permute-done((bf16[256,5632]{1,0:T(8,128)(2,1)}, bf16[256,5632]{1,0:T(8,128)(2,1)}, u32[]{:S(2)}, u32[]{:S(2)}) %collective-permute-start.23) | collective-permute-done | bytes 2883616 | tf_op jit(solution)/shard_map/ppermute | solution.py:68
  355.2 23.0 %collective-permute-done.30.refs_2_ = bf16[704,1024]{1,0:T(8,128)(2,1)} collective-permute-done((bf16[704,1024]{1,0:T(8,128)(2,1)}, bf16[704,1024]{1,0:T(8,128)(2,1)}, u32[]{:S(2)}, u32[]{:S(2)}) %collective-permute-start.30) | collective-permute-done | bytes 1441824 | tf_op jit(solution)/shard_map/ppermute | solution.py:68
  380.4 36.2 %shard_map.205 = (f32[512,5632]{1,0:T(8,128)}, f32[512,5632]{1,0:T(8,128)}, bf16[512,5632]{1,0:T(8,128)(2,1)}, bf16[5632,512]{1,0:T(8,128)(2,1)}) custom-call(bf16[512,2048]{1,0:T(8,128)(2,1)} %multiply_convert_fusion.left, bf16[256,5632]{1,0:T(8,128)(2,1)} %all-gather.11.cloned.1.call-done.refs_0_.refs_2_, ...), custom_call_target="tpu_custom_call" | custom-call | flops 23622320128 | bytes 80740352 | tf_op jit(solution)/shard_map/pallas_call | solution.py:276
  485.2 58.5 %shard_map.206 = (bf16[512,2048]{1,0:T(8,128)(2,1)}, bf16[512,5632]{1,0:T(8,128)(2,1)}, bf16[512,5632]{1,0:T(8,128)(2,1)}) custom-call(s32[4]{0:T(128)} %iota_xor_fusion.1.near, bf16[512,5632]{1,0:T(8,128)(2,1)} %get-tuple-element.128.hidden, f32[512,5632]{1,0:T(8,128)} %get-tuple-element.129.gate, f32[512,5632]{1,0:T(8,128)} %get-tuple-element.130.up, ...), custom_call_target="tpu_custom_call" | custom-call | flops 23622320128 | bytes 63438848 | tf_op jit(solution)/shard_map/pallas_call | solution.py:369
  580.5 28.0 %collective-permute-done.50 = bf16[704,1024]{1,0:T(8,128)(2,1)} collective-permute-done((bf16[704,1024]{1,0:T(8,128)(2,1)}, bf16[704,1024]{1,0:T(8,128)(2,1)}, u32[]{:S(2)}, u32[]{:S(2)}) %collective-permute-start.50) | collective-permute-done | bytes 1441824 | tf_op jit(solution)/shard_map/ppermute | solution.py:68
  635.5 38.2 %shard_map.207 = f32[512,2048]{1,0:T(8,128)} custom-call(s32[8]{0:T(128)} %iota_xor_fusion.near, bf16[512,5632]{1,0:T(8,128)(2,1)} %get-tuple-element.157.refs_0_, bf16[512,5632]{1,0:T(8,128)(2,1)} %get-tuple-element.158.refs_1_, bf16[256,5632]{1,0:T(8,128)(2,1)} %all-gather.11.cloned.1.call-done.refs_0_.refs_2_, ...), custom_call_target="tpu_custom_call" | custom-call | flops 23622320128 | bytes 46137344 | tf_op jit(solution)/shard_map/pallas_call | solution.py:212
  701.8 27.2 %fusion = (f32[16,512]{1,0:T(8,128)S(1)}, f32[1024,512,16]{1,0,2:T(8,128)}) fusion(f32[1024,512,16]{1,0,2:T(8,128)} %get-tuple-element.239, f32[16,512]{1,0:T(8,128)S(1)} %log_add_fusion, pred[512,1024]{0,1:T(8,128)(4,1)S(1)} %copy-done.6, bf16[512,16,128]{0,2,1:T(8,128)(2,1)S(1)} %bitcast.208, bf16[1,1024,256]{2,1,0:T(8,128)(2,1)S(1)} %copy-done.16), kind=kOutput, calls=%fused_computation.3 | convolution fusion | flops 2189418496 | bytes 70057984 | tf_op jit(solution)/shard_map/bqhe,bke->bhqk/dot_general | solution.py:678
  729.0 28.0 %fusion.2 = bf16[1,16,512,1024]{2,3,1,0:T(8,128)(2,1)} fusion(f32[1024,512,16]{1,0,2:T(8,128)} %get-tuple-element.241, f32[1024,512,16]{1,0,2:T(8,128)} %get-tuple-element.239, f32[16,512]{1,0:T(8,128)S(1)} %get-tuple-element.240, f32[16,512]{1,0:T(8,128)S(1)} %log_add_fusion, pred[512,1024]{0,1:T(8,128)(4,1)S(1)} %copy-done.6), kind=kLoop, calls=%fused_computation.5 | loop fusion | flops 50331648 | bytes 84475904 | tf_op jit(solution)/shard_map/convert_element_type | solution.py:685
  775.6 14.7 %fusion.56 = f32[1,1024,128]{2,1,0:T(8,128)S(1)} fusion(bf16[512,16,128]{0,2,1:T(8,128)(2,1)S(1)} %bitcast.209, f32[1024,512,16]{1,0,2:T(8,128)} %get-tuple-element.239, f32[16,512]{1,0:T(8,128)S(1)} %fusion.3, f32[16,512]{1,0:T(8,128)S(1)} %get-tuple-element.238, pred[512,1024]{0,1:T(8,128)(4,1)S(1)} %copy-done.6), kind=kOutput, calls=%fused_computation.115 | convolution fusion | flops 2189426688 | bytes 36765696 | tf_op jit(solution)/shard_map/bhqk,bqhe->bke/dot_general | solution.py:681
  805.0 33.5 %collective-permute-done.55 = bf16[256,5632]{1,0:T(8,128)(2,1)} collective-permute-done((bf16[256,5632]{1,0:T(8,128)(2,1)}, bf16[256,5632]{1,0:T(8,128)(2,1)}, u32[]{:S(2)}, u32[]{:S(2)}) %collective-permute-start.55) | collective-permute-done | bytes 2883616 | tf_op jit(solution)/shard_map/ppermute | solution.py:68
  917.7 44.5 %collective-permute-done.60 = bf16[512,2048]{1,0:T(8,128)(2,1)S(1)} collective-permute-done((bf16[512,2048]{1,0:T(8,128)(2,1)S(1)}, bf16[512,2048]{1,0:T(8,128)(2,1)S(1)}, u32[]{:S(2)}, u32[]{:S(2)}) %collective-permute-start.60) | collective-permute-done | bytes 2097184 | tf_op jit(solution)/shard_map/ppermute | solution.py:68
  974.3 21.8 %collective-permute-done.67 = bf16[256,2048]{1,0:T(8,128)(2,1)S(1)} collective-permute-done((bf16[256,2048]{1,0:T(8,128)(2,1)S(1)}, bf16[256,2048]{1,0:T(8,128)(2,1)S(1)}, u32[]{:S(2)}, u32[]{:S(2)}) %collective-permute-start.67) | collective-permute-done | bytes 1048608 | tf_op jit(solution)/shard_map/ppermute | solution.py:68
  1034.9 21.9 %reduce-scatter.5.cloned.1.call-done = bf16[64,4352]{1,0:T(8,128)(2,1)} async-done(((bf16[256,4352]{1,0:T(8,128)(2,1)}), bf16[64,4352]{1,0:T(8,128)(2,1)}) %reduce-scatter.5.cloned.1.call-update) | async-done | bytes 557072 | tf_op jit(solution)/shard_map/reduce_scatter | solution.py:512
  (391 shorter events, 424.6 us)
Async XLA Ops:
  46.1 90.0 %all-gather.11.cloned.1.call-start = ((), (), s32[]{:S(2)}) async-start(), calls=%async_computation.6 | async-start | bytes 3604480 | tf_op jit(solution)/shard_map/all_gather | solution.py:537
  75.2 136.7 %all-gather.13.cloned.1.call-start = ((), (), s32[]{:S(2)}) async-start(), calls=%async_computation.7 | async-start | bytes 3604480 | tf_op jit(solution)/shard_map/all_gather | solution.py:537
  140.9 71.1 %collective-permute-start.15 = (bf16[256,5632]{1,0:T(8,128)(2,1)}, bf16[256,5632]{1,0:T(8,128)(2,1)}, u32[]{:S(2)}, u32[]{:S(2)}) collective-permute-start(bf16[256,5632]{1,0:T(8,128)(2,1)} %all-gather.11.cloned.1.call-done.refs_0_.refs_2_), channel_id=1, source_target_pairs={{0,4},{4,0},{8,12},{12,8},{16,20},{20,16},{24,28},{28,24},{1,5},{5... | collective-permute-start | bytes 8650760 | tf_op jit(solution)/shard_map/ppermute | solution.py:68
  141.4 70.6 %collective-permute-start.16 = (bf16[256,5632]{1,0:T(8,128)(2,1)}, bf16[256,5632]{1,0:T(8,128)(2,1)}, u32[]{:S(2)}, u32[]{:S(2)}) collective-permute-start(bf16[256,5632]{1,0:T(8,128)(2,1)} %all-gather.11.cloned.1.call-done.refs_0_.refs_2_), channel_id=1, source_target_pairs={{0,8},{4,12},{8,0},{12,4},{16,24},{20,28},{24,16},{28,20},{1,9},{5... | collective-permute-start | bytes 8650760 | tf_op jit(solution)/shard_map/ppermute | solution.py:68
  142.9 69.1 %collective-permute-start.17 = (bf16[256,5632]{1,0:T(8,128)(2,1)}, bf16[256,5632]{1,0:T(8,128)(2,1)}, u32[]{:S(2)}, u32[]{:S(2)}) collective-permute-start(bf16[256,5632]{1,0:T(8,128)(2,1)} %all-gather.11.cloned.1.call-done.refs_0_.refs_2_), channel_id=1, source_target_pairs={{0,16},{4,20},{8,24},{12,28},{16,0},{20,4},{24,8},{28,12},{1,17},{... | collective-permute-start | bytes 8650760 | tf_op jit(solution)/shard_map/ppermute | solution.py:68
  144.3 67.6 %collective-permute-start.14 = (bf16[256,2048]{1,0:T(8,128)(2,1)}, bf16[256,2048]{1,0:T(8,128)(2,1)}, u32[]{:S(2)}, u32[]{:S(2)}) collective-permute-start(bf16[256,2048]{1,0:T(8,128)(2,1)} %collective-permute-done.9.refs_6_.refs_7_), channel_id=1, source_target_pairs={{0,4},{4,0},{8,12},{12,8},{16,20},{20,16},{24,28},{28,24},{1,5},{5... | collective-permute-start | bytes 3145736 | tf_op jit(solution)/shard_map/ppermute | solution.py:68
  144.4 111.8 %all-gather.15.cloned.1.call-start = ((), (), s32[]{:S(2)}) async-start(), calls=%async_computation.8 | async-start | bytes 1802240 | tf_op jit(solution)/shard_map/all_gather | solution.py:537
  212.0 64.7 %collective-permute-start.18 = (bf16[256,5632]{1,0:T(8,128)(2,1)}, bf16[256,5632]{1,0:T(8,128)(2,1)}, u32[]{:S(2)}, u32[]{:S(2)}) collective-permute-start(bf16[256,5632]{1,0:T(8,128)(2,1)} %all-gather.13.cloned.1.call-done.refs_8_.refs_10_), channel_id=1, source_target_pairs={{0,16},{4,20},{8,24},{12,28},{16,0},{20,4},{24,8},{28,12},{1,17},{... | collective-permute-start | bytes 8650760 | tf_op jit(solution)/shard_map/ppermute | solution.py:68
  212.5 64.4 %collective-permute-start.19 = (bf16[256,5632]{1,0:T(8,128)(2,1)}, bf16[256,5632]{1,0:T(8,128)(2,1)}, u32[]{:S(2)}, u32[]{:S(2)}) collective-permute-start(bf16[256,5632]{1,0:T(8,128)(2,1)} %all-gather.13.cloned.1.call-done.refs_8_.refs_10_), channel_id=1, source_target_pairs={{0,8},{4,12},{8,0},{12,4},{16,24},{20,28},{24,16},{28,20},{1,9},{5... | collective-permute-start | bytes 8650760 | tf_op jit(solution)/shard_map/ppermute | solution.py:68
  213.1 115.4 %all-gather.17.cloned.1.call-start = ((), (), s32[]{:S(2)}) async-start(), calls=%async_computation.9 | async-start | bytes 1802240 | tf_op jit(solution)/shard_map/all_gather | solution.py:537
  277.4 64.7 %collective-permute-start.23 = (bf16[256,5632]{1,0:T(8,128)(2,1)}, bf16[256,5632]{1,0:T(8,128)(2,1)}, u32[]{:S(2)}, u32[]{:S(2)}) collective-permute-start(bf16[256,5632]{1,0:T(8,128)(2,1)} %collective-permute-done.16.refs_2_.refs_4_), channel_id=1, source_target_pairs={{0,16},{4,20},{8,24},{12,28},{16,0},{20,4},{24,8},{28,12},{1,17},{... | collective-permute-start | bytes 8650760 | tf_op jit(solution)/shard_map/ppermute | solution.py:68
  279.0 64.4 %collective-permute-start.24 = (bf16[256,5632]{1,0:T(8,128)(2,1)}, bf16[256,5632]{1,0:T(8,128)(2,1)}, u32[]{:S(2)}, u32[]{:S(2)}) collective-permute-start(bf16[256,5632]{1,0:T(8,128)(2,1)} %collective-permute-done.18.refs_12_.refs_14_), channel_id=1, source_target_pairs={{0,8},{4,12},{8,0},{12,4},{16,24},{20,28},{24,16},{28,20},{1,9},{5... | collective-permute-start | bytes 8650760 | tf_op jit(solution)/shard_map/ppermute | solution.py:68
  279.4 64.0 %collective-permute-start.25 = (bf16[256,5632]{1,0:T(8,128)(2,1)}, bf16[256,5632]{1,0:T(8,128)(2,1)}, u32[]{:S(2)}, u32[]{:S(2)}) collective-permute-start(bf16[256,5632]{1,0:T(8,128)(2,1)} %collective-permute-done.19.refs_10_.refs_12_), channel_id=1, source_target_pairs={{0,4},{4,0},{8,12},{12,8},{16,20},{20,16},{24,28},{28,24},{1,5},{5... | collective-permute-start | bytes 8650760 | tf_op jit(solution)/shard_map/ppermute | solution.py:68
  286.6 718.1 %reduce-scatter.11.cloned.1.call-start = ((), (), s32[]{:S(2)}) async-start(), calls=%async_computation.13 | async-start | bytes 3604480 | tf_op jit(solution)/shard_map/reduce_scatter | solution.py:512
  481.9 83.0 %collective-permute-start.46 = (bf16[1408,1024]{1,0:T(8,128)(2,1)}, bf16[1408,1024]{1,0:T(8,128)(2,1)}, u32[]{:S(2)}, u32[]{:S(2)}) collective-permute-start(bf16[1408,1024]{1,0:T(8,128)(2,1)} %add_convert_fusion.2), channel_id=1, source_target_pairs={{0,16},{4,20},{8,24},{12,28},{16,0},{20,4},{24,8},{28,12},{1,17},{... | collective-permute-start | bytes 8650760 | tf_op jit(solution)/shard_map/ppermute | solution.py:68
  483.5 85.4 %collective-permute-start.45 = (bf16[1408,1024]{1,0:T(8,128)(2,1)}, bf16[1408,1024]{1,0:T(8,128)(2,1)S(1)}, u32[]{:S(2)}, u32[]{:S(2)}) collective-permute-start(bf16[1408,1024]{1,0:T(8,128)(2,1)} %add_convert_fusion.3), channel_id=1, source_target_pairs={{0,8},{4,12},{8,0},{12,4},{16,24},{20,28},{24,16},{28,20},{1,9},{5... | collective-permute-start | bytes 8650760 | tf_op jit(solution)/shard_map/ppermute | solution.py:68
  617.1 412.5 %reduce-scatter.9.cloned.1.call-start = ((), (), s32[]{:S(2)}) async-start(), calls=%async_computation.12 | async-start | bytes 3604480 | tf_op jit(solution)/shard_map/reduce_scatter | solution.py:512
  633.3 125.9 %collective-permute-start.52 = (bf16[512,5632]{1,0:T(8,128)(2,1)}, bf16[512,5632]{1,0:T(8,128)(2,1)}, u32[]{:S(2)}, u32[]{:S(2)}) collective-permute-start(bf16[512,5632]{1,0:T(8,128)(2,1)} %add_convert_fusion), channel_id=1, source_target_pairs={{0,16},{4,20},{8,24},{12,28},{16,0},{20,4},{24,8},{28,12},{1,17},{... | collective-permute-start | bytes 17301512 | tf_op jit(solution)/shard_map/ppermute | solution.py:68
  635.1 132.1 %collective-permute-start.51 = (bf16[512,5632]{1,0:T(8,128)(2,1)}, bf16[512,5632]{1,0:T(8,128)(2,1)}, u32[]{:S(2)}, u32[]{:S(2)}) collective-permute-start(bf16[512,5632]{1,0:T(8,128)(2,1)} %add_convert_fusion.1), channel_id=1, source_target_pairs={{0,8},{4,12},{8,0},{12,4},{16,24},{20,28},{24,16},{28,20},{1,9},{5... | collective-permute-start | bytes 17301512 | tf_op jit(solution)/shard_map/ppermute | solution.py:68
  790.3 92.4 %collective-permute-start.54 = (bf16[256,5632]{1,0:T(8,128)(2,1)}, bf16[256,5632]{1,0:T(8,128)(2,1)}, u32[]{:S(2)}, u32[]{:S(2)}) collective-permute-start(bf16[256,5632]{1,0:T(8,128)(2,1)} %fusion.22), channel_id=1, source_target_pairs={{0,16},{4,20},{8,24},{12,28},{16,0},{20,4},{24,8},{28,12},{1,17},{... | collective-permute-start | bytes 8650760 | tf_op jit(solution)/shard_map/ppermute | solution.py:68
  792.1 90.7 %collective-permute-start.56 = (bf16[1024,2048]{1,0:T(8,128)(2,1)}, bf16[1024,2048]{1,0:T(8,128)(2,1)}, u32[]{:S(2)}, u32[]{:S(2)}) collective-permute-start(bf16[1024,2048]{1,0:T(8,128)(2,1)} %convolution_convert_fusion.5), channel_id=1, source_target_pairs={{0,4},{4,0},{8,12},{12,8},{16,20},{20,16},{24,28},{28,24},{1,5},{5... | collective-permute-start | bytes 12582920 | tf_op jit(solution)/shard_map/ppermute | solution.py:68
  803.7 66.5 %collective-permute-start.53 = (bf16[1,512,256]{2,1,0:T(8,128)(2,1)S(1)}, bf16[1,512,256]{2,1,0:T(8,128)(2,1)S(1)}, u32[]{:S(2)}, u32[]{:S(2)}) collective-permute-start(bf16[1,512,256]{2,1,0:T(8,128)(2,1)S(1)} %fusion.113), channel_id=1, source_target_pairs={{1,0},{2,1},{3,2},{5,4},{6,5},{7,6},{9,8},{10,9},{11,10},{13,12},{... | collective-permute-start | bytes 786440 | tf_op jit(solution)/shard_map/ppermute | solution.py:22
  848.1 183.9 %reduce-scatter.7.cloned.1.call-start = ((), (), s32[]{:S(2)}) async-start(), calls=%async_computation.11 | async-start | bytes 3604480 | tf_op jit(solution)/shard_map/reduce_scatter | solution.py:512
  890.6 166.2 %reduce-scatter.5.cloned.1.call-start = ((), (), s32[]{:S(2)}) async-start(), calls=%async_computation.10 | async-start | bytes 2785280 | tf_op jit(solution)/shard_map/reduce_scatter | solution.py:512
  (120 other events, 2870.0 us)
Sparse Core Ops, SparseCore 0:
  11.7 34.2 all-gather.6
  48.2 26.9 all-gather.8
  77.4 58.6 all-gather.10
  144.5 57.9 all-gather.12
  213.2 42.9 all-gather.14
  286.8 41.7 all-gather.16
  617.2 63.1 reduce-scatter.10
  848.2 62.7 reduce-scatter.8
  913.3 56.0 reduce-scatter.6
  1003.4 53.3 reduce-scatter.4

commit v2 on v1

--- a/solution.py
+++ b/solution.py
@@ -86,7 +86,9 @@
 def kernel_params(flops, traffic):
     return {
         "compiler_params": pltpu.CompilerParams(vmem_limit_bytes=58 * MIB),
-        "cost_estimate": pl.CostEstimate(flops=flops, bytes_accessed=traffic, transcendentals=0),
+        "cost_estimate": pl.CostEstimate(
+            flops=flops, bytes_accessed=traffic, transcendentals=0
+        ),
     }
 
 
@@ -229,6 +231,103 @@
     )(near, *lefts, *[held[place] for held in helds for place in range(count)])
 
 
+def across_rows(left, right):
+    return lax.dot_general(
+        left, right, (((1,), (1,)), ((), ())), preferred_element_type=jnp.float32
+    )
+
+
+def attend_kernel(bias, query, keys, values_turned, mixed, log_total):
+    block = min(256, query.shape[0])
+    for number in range(query.shape[0] // block):
+        mine = slice(number * block, (number + 1) * block)
+        seen = slice(number * block, (number + 1) * block + WINDOW)
+        scores = across_rows(keys[seen, :], query[mine, :]) * (1.0 / math.sqrt(HEAD))
+        scores = scores + bias[seen, mine]
+        top = jnp.max(scores, axis=0, keepdims=True)
+        weight = jnp.exp(scores - top)
+        total = jnp.sum(weight, axis=0, keepdims=True)
+        probs = (weight * (1.0 / total)).astype(jnp.bfloat16)
+        mixed[mine, :] = matmul(values_turned[:, seen], probs).T.astype(mixed.dtype)
+        log_total[0, :, mine] = top + jnp.log(total)
+
+
+def head_specs(group, length):
+    def whole(*shape):
+        return pl.BlockSpec(shape, lambda head: (0, 0))
+
+    column = pl.BlockSpec((group, HEAD), lambda head: (0, head))
+    row = pl.BlockSpec((1, 1, group), lambda head: (head, 0, 0))
+    return whole, column, row
+
+
+def attend(bias, query, keys, values_turned):
+    length, group = bias.shape
+    whole, column, row = head_specs(group, length)
+    heads = query.shape[1] // HEAD
+    return pl.pallas_call(
+        attend_kernel,
+        out_shape=[
+            jax.ShapeDtypeStruct(query.shape, query.dtype),
+            jax.ShapeDtypeStruct((heads, 1, group), jnp.float32),
+        ],
+        grid=(heads,),
+        in_specs=[whole(length, group), column, whole(length, HEAD), whole(HEAD, length)],
+        out_specs=[column, row],
+        **kernel_params(4 * length * query.shape[0] * query.shape[1], 8 * query.size),
+    )(bias, query, keys, values_turned)
+
+
+def attend_back_kernel(
+    bias, cosine, sine, query, grad_mixed, log_total, keys, keys_turned, values, grad_query,
+    grad_keys, grad_values,
+):
+    block = min(256, query.shape[0])
+    factor = 1.0 / math.sqrt(HEAD)
+
+    @pl.when(pl.program_id(0) == 0)
+    def _():
+        grad_keys[...] = jnp.zeros_like(grad_keys)
+        grad_values[...] = jnp.zeros_like(grad_values)
+
+    for number in range(query.shape[0] // block):
+        mine = slice(number * block, (number + 1) * block)
+        seen = slice(number * block, (number + 1) * block + WINDOW)
+        query_rows, grad_rows = query[mine, :], grad_mixed[mine, :]
+        scores = across_rows(keys[seen, :], query_rows) * factor + bias[seen, mine]
+        probs = jnp.exp(scores - log_total[0, :, mine])
+        grad_probs = across_rows(values[seen, :], grad_rows)
+        centre = jnp.sum(probs * grad_probs, axis=0, keepdims=True)
+        grad_scores = (probs * (grad_probs - centre)).astype(jnp.bfloat16)
+        grad_keys[seen, :] += matmul(grad_scores, query_rows) * factor
+        grad_values[seen, :] += matmul(probs.astype(jnp.bfloat16), grad_rows)
+        turned = matmul(keys_turned[:, seen], grad_scores) * factor
+        first, second = turned[: HEAD // 2], turned[HEAD // 2 :]
+        cos, sin = cosine[:, mine], sine[:, mine]
+        grad_query[mine, :HEAD // 2] = (first * cos + second * sin).T.astype(grad_query.dtype)
+        grad_query[mine, HEAD // 2 :] = (second * cos - first * sin).T.astype(grad_query.dtype)
+
+
+def attend_back(bias, cosine, sine, query, grad_mixed, log_total, keys, values):
+    length, group = bias.shape
+    whole, column, row = head_specs(group, length)
+    heads = query.shape[1] // HEAD
+    half = whole(HEAD // 2, group)
+    return pl.pallas_call(
+        attend_back_kernel,
+        out_shape=[
+            jax.ShapeDtypeStruct(query.shape, query.dtype),
+            jax.ShapeDtypeStruct((length, HEAD), jnp.float32),
+            jax.ShapeDtypeStruct((length, HEAD), jnp.float32),
+        ],
+        grid=(heads,),
+        in_specs=[whole(length, group), half, half, column, column, row]
+        + [whole(length, HEAD), whole(HEAD, length), whole(length, HEAD)],
+        out_specs=[column, whole(length, HEAD), whole(length, HEAD)],
+        **kernel_params(10 * length * query.shape[0] * query.shape[1], 12 * query.size),
+    )(bias, cosine, sine, query, grad_mixed, log_total, keys, keys.T, values)
+
+
 def gate_kernel(count, left, *refs):
     pieces = refs[: 2 * count]
     gate, up, hidden, turned, held, sems = refs[2 * count :]
@@ -294,20 +393,50 @@
     )(left, *[held[place] for held in (gates, ups) for place in range(count)])
 
 
-def down_kernel(count, together, near, hidden, gate, up, cot, mid, *refs):
-    pieces = refs[: 2 * count]
-    output, grad_gate, grad_up, held, total, sems = refs[2 * count :]
+def turn_kernel(source, out):
+    out[...] = source[...].T
+
+
+def turned_over(source):
+    rows, columns = source.shape
+    return pl.pallas_call(
+        turn_kernel,
+        out_shape=jax.ShapeDtypeStruct((columns, rows), source.dtype),
+        grid=(columns // 512,),
+        in_specs=[pl.BlockSpec((rows, 512), lambda step: (0, step))],
+        out_specs=pl.BlockSpec((512, rows), lambda step: (step, 0)),
+        **kernel_params(0, 4 * rows * columns),
+    )(source)
+
+
+def down_kernel(count, together, sides, back, near, *refs):
+    if back:
+        gate, up, cot = refs[:3]
+        refs = refs[3:]
+    else:
+        hidden, mid = refs[:2]
+        refs = refs[2:]
+    own, other = refs[:2]
+    halves = len(sides) - 1
+    pieces = refs[2 : 2 + halves * count]
+    if back:
+        grad_gate, grad_up, held, sems = refs[2 + halves * count :]
+    else:
+        output, held, total, sems = refs[2 + halves * count :]
     step, steps = pl.program_id(0), pl.num_programs(0)
-    rows, side = pieces[0].shape
+    rows = own.shape[1]
 
     def copies(number, slot):
         for part in range(together):
             spot = lax.rem(owner(part), together)
             start = pl.multiple_of(spot * rows, rows)
-            for which in range(2):
+            place = number * together + part
+            sources = [(other if place & 1 else own).at[place >> 1]]
+            sources += [pieces[half * count + place] for half in range(halves)]
+            for which, (left, right) in enumerate(sides):
                 yield pltpu.make_async_copy(
-                    pieces[which * count + number * together + part],
-                    held.at[slot, pl.ds(start, rows), which * side : (which + 1) * side],
+                    sources[which],
+                    held.at[slot, pl.ds(start, rows), left:right],
                     sems.at[slot, part, which],
                 )
 
@@ -321,75 +450,65 @@
     slot = lax.rem(step, 2)
     for copy in copies(0, slot):
         copy.wait()
-    chunk = 128
-
-    @pl.loop(0, cot.shape[0] // chunk)
-    def _(index):
-        start = pl.ds(pl.multiple_of(index * chunk, chunk), chunk)
-        weight = held[slot]
-        grad = lax.dot_general(
-            cot[start, :], weight, (((1,), (1,)), ((), ())), preferred_element_type=jnp.float32
+    weight = held[slot]
+    if back:
+        grad = across_rows(cot[...], weight)
+        gate_rows, up_rows = gate[...], up[...]
+        sigma = jax.nn.sigmoid(gate_rows)
+        grad_up[...] = (grad * (gate_rows * sigma)).astype(grad_up.dtype)
+        grad_gate[...] = (grad * up_rows * (sigma * (1.0 + gate_rows * (1.0 - sigma)))).astype(
+            grad_gate.dtype
         )
-        gate_rows, up_rows = gate[start, :], up[start, :]
-        sigma = jax.nn.sigmoid(gate_rows)
-        grad_up[start, :] = (grad * (gate_rows * sigma)).astype(grad_up.dtype)
-        grad_gate[start, :] = (
-            grad * up_rows * (sigma * (1.0 + gate_rows * (1.0 - sigma)))
-        ).astype(grad_gate.dtype)
-        added = matmul(hidden[start, :], weight)
-
-        @pl.when(step == 0)
-        def _():
-            total[start, :] = mid[start, :] + added
-
-        @pl.when(step > 0)
-        def _():
-            total[start, :] += added
+        return
+    added = matmul(hidden[...], weight)
+
+    @pl.when(step == 0)
+    def _():
+        total[...] = mid[...] + added
+
+    @pl.when(step > 0)
+    def _():
+        total[...] += added
 
     @pl.when(step == steps - 1)
     def _():
         output[...] = total[...].astype(output.dtype)
 
 
-def down_and_back(hidden, gate, up, cot, mid, helds):
-    count, (rows, side) = len(helds[0]), helds[0][0].shape
-    tokens, width = cot.shape
-    together = next(size for size in (1, 2, 4, 8, 16) if size * rows % 128 == 0)
+def with_down(operands, early, helds, back):
+    count, (blocks, rows, first) = len(helds[0]), early[0].shape
+    tokens, width = operands[-1].shape
+    ends = [0, first]
+    for held in helds:
+        ends.append(ends[-1] + held[0].shape[1])
+    sides = tuple(zip(ends, ends[1:]))
+    together = next(size for size in (2, 4, 8, 16) if size * rows % 128 == 0)
     tile = together * rows
     dp = lax.axis_index("dp")
     near = lax.bitwise_xor(
         lax.div(dp, together), jnp.arange(count // together, dtype=jnp.int32)
     )
     across = pl.BlockSpec((tokens, tile), lambda step, near: (0, near[step]))
-
-    def fixed(size):
-        return pl.BlockSpec((tokens, size), lambda step, near: (0, 0))
-
+    fixed = pl.BlockSpec((tokens, width), lambda step, near: (0, 0))
     columns = count * rows
+    wide = jax.ShapeDtypeStruct((tokens, columns), jnp.bfloat16)
+    scratch = [pltpu.VMEM((2, tile, width), jnp.bfloat16)]
+    if not back:
+        scratch.append(pltpu.VMEM((tokens, width), jnp.float32))
+    scratch.append(pltpu.SemaphoreType.DMA((2, together, len(sides))))
     return pl.pallas_call(
-        functools.partial(down_kernel, count, together),
-        out_shape=[
-            jax.ShapeDtypeStruct((tokens, width), jnp.bfloat16),
-            jax.ShapeDtypeStruct((tokens, columns), jnp.bfloat16),
-            jax.ShapeDtypeStruct((tokens, columns), jnp.bfloat16),
-        ],
+        functools.partial(down_kernel, count, together, sides, back),
+        out_shape=[wide, wide] if back else jax.ShapeDtypeStruct((tokens, width), jnp.bfloat16),
         grid_spec=pltpu.PrefetchScalarGridSpec(
             num_scalar_prefetch=1,
             grid=(count // together,),
-            in_specs=[across, across, across, fixed(width), fixed(width)]
-            + [ANYWHERE] * (2 * count),
-            out_specs=[fixed(width), across, across],
-            scratch_shapes=[
-                pltpu.VMEM((2, tile, width), hidden.dtype),
-                pltpu.VMEM((tokens, width), jnp.float32),
-                pltpu.SemaphoreType.DMA((2, together, 2)),
-            ],
+            in_specs=([across, across, fixed] if back else [across, fixed])
+            + [ANYWHERE] * (2 + len(helds) * count),
+            out_specs=[across, across] if back else fixed,
+            scratch_shapes=scratch,
         ),
-        **kernel_params(4 * tokens * width * columns, 2 * columns * (width + 7 * tokens)),
-    )(
-        near, hidden, gate, up, cot, mid,
-        *[held[place] for held in helds for place in range(count)],
-    )
+        **kernel_params(2 * tokens * width * columns, 2 * columns * (width + 5 * tokens)),
+    )(near, *operands, *early, *[held[place] for held in helds for place in range(count)])
 
 
 class Flow:
@@ -398,12 +517,73 @@
 
     def round(self, moves):
         values = after([value for value, _ in moves], self.ended)
-        got = [partner(value, bit) for value, (_, bit) in zip(values, moves)]
+        self.fence = values
+        got = [
+            bit(value) if callable(bit) else partner(value, bit)
+            for value, (_, bit) in zip(values, moves)
+        ]
         self.ended = list(got)
         return got
 
     def holds(self, *results):
         self.ended.extend(results)
+
+
+def exchange(flow, jobs, also=()):
+    moves = [job.moves() for job in jobs]
+    got = flow.round([move for found in moves for move in found] + list(also))
+    for job, found in zip(jobs, moves):
+        job.receive(got[: len(found)])
+        got = got[len(found) :]
+    return got
+
+
+class Order:
+    def __init__(self):
+        self.last = []
+
+    def __call__(self, work, *operands):
+        got = work(*after(operands, self.last))
+        self.last = [got]
+        return got
+
+    def first(self, job):
+        job.right = after(job.right, self.last)
+        self.last = [job.first()]
+
+    def send(self, job):
+        job.right = after(job.right, self.last)
+        self.last = list(job.send())
+
+    def line(self, job):
+        job.right = after(job.right, self.last)
+        self.last = [job.line()]
+        return self.last[0]
+
+
+class Shallow:
+    def __init__(self, shard, order):
+        self.order, self.pieces, self.level = order, {0: shard}, 0
+
+    def moves(self):
+        self.level += 1
+        self.places = [
+            place
+            for place in range(2 << len(self.order))
+            if not place & 1 and bin(place).count("1") == self.level
+        ]
+        found = []
+        for place in self.places:
+            bit = next(bit for bit in self.order if place >> bit & 1)
+            found.append((self.pieces[place ^ (1 << bit)], bit))
+        return found
+
+    def put(self, got):
+        for place, piece in zip(self.places, got):
+            self.pieces[place] = piece
+
+    def left(self):
+        return self.level < len(self.order)
 
 
 class Spreads:
@@ -420,6 +600,14 @@
             held[1 << bit] = piece
         return got[1 + len(self.order) :]
 
+    def both(self, flow, lines):
+        got = flow.round([(line, bit) for line in lines for bit in self.order])
+        for number, line in enumerate(lines):
+            held = self.helds[number]
+            held[0] = line
+            for place, bit in enumerate(self.order):
+                held[1 << bit] = got[number * len(self.order) + place]
+
     def double(self):
         return [
             (number, place)
@@ -435,8 +623,8 @@
         for (number, place), piece in zip(names, got):
             self.helds[number][place | 1] = piece
 
-    def cross(self, flow, level, also):
-        names, targets, moves = self.double(), [], []
+    def cross(self, flow, level, also, cores):
+        names, targets, moves = self.double() if cores else [], [], []
         for number, turn in enumerate((self.order, self.order[::-1])):
             for place in range(2 << len(self.order)):
                 bits = [bit for bit in turn if place >> bit & 1]
@@ -450,10 +638,10 @@
         self.put(names, got[len(targets) : end])
         return got[end:]
 
-    def crosses(self, flow, also=()):
+    def crosses(self, flow, also=(), cores=True):
         extra = []
         for level in range(2, len(self.order) + 1):
-            extra += self.cross(flow, level, also if level == 2 else ())
+            extra += self.cross(flow, level, also if level == 2 else (), cores)
         return extra
 
 
@@ -464,52 +652,160 @@
     return places
 
 
-def arranged(turned, order):
-    dp, me = lax.axis_size("dp"), lax.axis_index("dp")
-    block = turned.shape[0] // dp
-    return jnp.concatenate(
-        [
-            lax.dynamic_slice_in_dim(turned, lax.bitwise_xor(me, place) * block, block, 0)
-            for place in places_of(order)
-        ],
-        axis=0,
-    )
-
-
-class Scattered:
+def sum_kernel(shared, each, table, turned, right, *refs):
+    outs = refs[shared + 2 * each :]
+    total = matmul(turned[...], right[...])
+    for part in refs[:shared]:
+        total = total + part[...].astype(jnp.float32)
+    sides = 2 if len(outs) == 2 or each else 1
+    for side in range(sides):
+
+        @pl.when(pl.program_id(0) == side)
+        def _(side=side):
+            mine = total
+            for part in refs[shared + side * each : shared + (side + 1) * each]:
+                mine = mine + part[...].astype(jnp.float32)
+            out = outs[side % len(outs)]
+            out[...] = mine.astype(out.dtype)
+
+
+def summed_rows(turned, right, rows, shared=(), parts=((), ()), apart=False):
+    sides, count = len(rows), len(rows[0])
+    tokens, columns = right.shape[0], right.shape[1] // sides
+    block = turned.shape[0] // lax.axis_size("dp")
+    table = [[place for side in rows for place in side]]
+    table += [[places.index(place) for side in rows for place in side] for _, places in shared]
+    for side in range(sides):
+        table += [[places.index(place) for place in rows[side]] * sides for _, places in parts[side]]
+    spots = jnp.array(table, jnp.int32)
+    spots = spots.at[0].set(lax.bitwise_xor(spots[0], lax.axis_index("dp")))
+    each = len(parts[0])
+
+    def shared_spec(line):
+        return pl.BlockSpec(
+            (block, columns),
+            lambda now, step, spots: (spots[line, now * count + step], now),
+        )
+
+    def one_side(side, row):
+        def index(now, step, spots):
+            step = jnp.where(now == side, step, jnp.where(now < side, 0, count - 1))
+            return (row(step, spots), 0)
+
+        return pl.BlockSpec((block, columns), index)
+
+    def part_spec(side, line):
+        return one_side(side, lambda step, spots: spots[line, step])
+
+    if apart:
+        out_shape = [jax.ShapeDtypeStruct((count * block, columns), jnp.bfloat16)] * sides
+        out_specs = [one_side(side, lambda step, spots: step) for side in range(sides)]
+    else:
+        out_shape = [jax.ShapeDtypeStruct((count * block, sides * columns), jnp.bfloat16)]
+        out_specs = [pl.BlockSpec((block, columns), lambda now, step, spots: (step, now))]
+    base = 1 + len(shared)
+    return pl.pallas_call(
+        functools.partial(sum_kernel, len(shared), each),
+        out_shape=out_shape,
+        grid_spec=pltpu.PrefetchScalarGridSpec(
+            num_scalar_prefetch=1,
+            grid=(sides, count),
+            in_specs=[
+                pl.BlockSpec(
+                    (block, tokens),
+                    lambda now, step, spots: (spots[0, now * count + step], 0),
+                ),
+                pl.BlockSpec((tokens, columns), lambda now, step, spots: (0, now)),
+            ]
+            + [shared_spec(1 + number) for number in range(len(shared))]
+            + [
+                part_spec(side, base + side * each + number)
+                for side in range(sides)
+                for number in range(each)
+            ],
+            out_specs=out_specs,
+        ),
+        **kernel_params(
+            2 * tokens * sides * count * block * columns,
+            2 * sides * count * block * columns * (1 + len(shared) + each),
+        ),
+    )(spots, turned, right, *[part for part, _ in shared], *[p for side in parts for p, _ in side])
+
+
+class Pair:
     def __init__(self, turned, right, order):
-        self.lhs, self.right, self.order = arranged(turned, order), right, order
-        self.arrived, self.step = [], 0
-
-    def total(self, rows, parts):
-        total = matmul(rows, self.right)
-        for part in parts:
-            total = total + part.astype(jnp.float32)
-        return total
+        self.turned, self.right = turned, right
+        self.orders = (order, order[::-1])
+        self.kept = [places_of(turn) for turn in self.orders]
+        self.whole = places_of(order)
+        self.shared, self.parts, self.step = [], ([], []), 0
+
+    def first(self):
+        places = [place | 1 for place in self.whole]
+        self.sent = summed_rows(self.turned, self.right, [places])
+        return self.sent[0]
+
+    def first_move(self):
+        return (self.sent[0], 0)
+
+    def first_receive(self, got):
+        self.shared = [(got, self.whole)]
 
     def send(self):
-        half = self.lhs.shape[0] // 2
-        sent = self.total(self.lhs[half:], [part[half:] for part in self.arrived])
-        self.sent = sent.astype(jnp.bfloat16)
-        self.lhs = self.lhs[:half]
-        self.arrived = [part[:half] for part in self.arrived]
+        half = len(self.kept[0]) // 2
+        self.sent = summed_rows(
+            self.turned,
+            self.right,
+            [kept[half:] for kept in self.kept],
+            self.shared,
+            self.parts,
+            apart=True,
+        )
+        self.kept = [kept[:half] for kept in self.kept]
         return self.sent
 
-    def move(self):
-        return (self.sent, self.order[self.step])
+    def moves(self):
+        return [(sent, turn[self.step]) for sent, turn in zip(self.sent, self.orders)]
 
     def receive(self, got):
-        self.arrived.append(got)
+        for piece, parts, kept in zip(got, self.parts, self.kept):
+            parts.append((piece, kept))
         self.step += 1
 
+    def left(self):
+        return len(self.orders[0]) - self.step
+
     def line(self):
-        self.sent = self.total(self.lhs, self.arrived).astype(jnp.bfloat16)
-        return self.sent
-
-
-def finish(jobs):
-    sent = jnp.concatenate([job.sent for job in jobs], axis=1)
-    return lax.psum_scatter(sent, "seq", scatter_dimension=0, tiled=True).astype(jnp.float32)
+        self.sent = summed_rows(self.turned, self.right, self.kept, self.shared, self.parts)
+        return self.sent[0]
+
+
+def finish(line):
+    return lax.psum_scatter(line, "seq", scatter_dimension=0, tiled=True).astype(jnp.float32)
+
+
+class Halved:
+    def __init__(self, blocks, order):
+        self.order, self.step = order, 0
+        self.kept = [block.astype(jnp.float32) for block in blocks]
+
+    def left(self):
+        return len(self.order) - self.step
+
+    def moves(self):
+        half = len(self.kept) // 2
+        sent = jnp.concatenate(self.kept[half:], axis=0).astype(jnp.bfloat16)
+        self.kept = self.kept[:half]
+        return [(sent, self.order[self.step])]
+
+    def receive(self, got):
+        (got,) = got
+        rows = got.shape[0] // len(self.kept)
+        self.kept = [
+            kept + got[number * rows : (number + 1) * rows].astype(jnp.float32)
+            for number, kept in enumerate(self.kept)
+        ]
+        self.step += 1
 
 
 def on_device(
@@ -544,20 +840,22 @@
     flow = Flow()
     line_first = along(first)
     line_out = along(after(w_out.astype(half_type), line_first))
-    line_gate = along(after(w_gate.astype(half_type), line_out))
+    one_spread, two_spread, three_spread = Spreads(upper), Spreads(upper), Spreads(upper)
+    one_spread.direct(flow, 0, line_first)
+    line_gate = along(after(w_gate.astype(half_type), line_out, flow.ended))
     line_up = along(after(w_up.astype(half_type), line_gate))
     down_half = w_down.astype(half_type)
-    line_left = along(after(down_half[:, :middle], line_up))
-    line_right = along(after(down_half[:, middle:], line_left))
-    one_spread, two_spread, three_spread = Spreads(upper), Spreads(upper), Spreads(upper)
-    one_spread.direct(flow, 0, line_first)
+    quarter = middle + middle // 2
+    line_right = along(after(down_half[:, middle:], line_up))
+    early_spread = Shallow(down_half[:, :middle], upper)
     flow.holds(line_out)
-    one_spread.direct(flow, 1, line_out)
+    early_spread.put(one_spread.direct(flow, 1, line_out, early_spread.moves()))
     one_spread.crosses(flow)
     flow.holds(line_gate)
     left_over = one_spread.double()
-    got = two_spread.direct(flow, 0, line_gate, one_spread.moves(left_over))
-    one_spread.put(left_over, got)
+    one_spread.put(
+        left_over, two_spread.direct(flow, 0, line_gate, one_spread.moves(left_over))
+    )
     full_one = one_spread.helds
 
     reach = (WINDOW - 2) // group + 1
@@ -571,9 +869,9 @@
         & (query_at[:, None] >= key_at[None, :])
         & (query_at[:, None] - key_at[None, :] < WINDOW)
     )
-    allowed = (allowed[None] & (query_seg[:, :, None] == key_seg[:, None, :]))[:, None]
+    allowed = allowed & (query_seg[0][:, None] == key_seg[0][None, :])
+    bias = jnp.where(allowed.T, 0.0, -1e30)
     cosine, sine = rope_tables(query_pos)
-    factor = 1.0 / math.sqrt(HEAD)
     rows = tokens.astype(jnp.float32).reshape(count, width)
     scale_one = lax.rsqrt(jnp.mean(rows * rows, axis=-1, keepdims=True) + EPS)
     mapped, normed, gain_rows = by_rows(rows * scale_one, full_one[0], columns_first)
@@ -592,145 +890,156 @@
     keys_seen = seen[..., :HEAD]
     values_seen = seen[..., HEAD:]
 
-    def scores_of():
-        raw = jnp.einsum(
-            "bqhe,bke->bhqk", query_turned, keys_seen, preferred_element_type=jnp.float32
-        )
-        return jnp.where(allowed, raw * factor, -1e30)
-
-    scores = scores_of()
+    query_turned = query_turned.reshape(count, HEADS * HEAD)
+    keys_seen, values_seen = keys_seen[0], values_seen[0]
     flow.holds(line_up, query_turned)
-    two_spread.direct(flow, 1, line_up)
-    top = jnp.max(scores, axis=-1, keepdims=True)
-    weight = jnp.exp(scores - top)
-    total = jnp.sum(weight, axis=-1, keepdims=True)
-    log_total = top + jnp.log(total)
-    probs = (weight / total).astype(half_type)
-    mixed = jnp.einsum("bhqk,bke->bqhe", probs, values_seen, preferred_element_type=jnp.float32)
-    mixed = mixed.astype(half_type).reshape(count, HEADS * HEAD)
+    early_spread.put(two_spread.direct(flow, 1, line_up, early_spread.moves()))
+    while early_spread.left():
+        early_spread.put(flow.round(early_spread.moves()))
+    places = sorted(early_spread.pieces)
+    early = jnp.stack([early_spread.pieces[place] for place in places])
+    early = lax.all_gather(after(early, line_right), "seq", axis=1, tiled=True)
+    mixed, log_total = attend(bias, query_turned, keys_seen, values_seen.T)
     mid = rows + by_rows(mixed, full_one[1], width)[0]
     scale_two = lax.rsqrt(jnp.mean(mid * mid, axis=-1, keepdims=True) + EPS)
     normed_two = (mid * scale_two * gain_b).astype(half_type)
 
-    flow.holds(normed_two, line_left)
+    turned_one, turned_mixed, turned_two = map(turned_over, (normed, mixed, normed_two))
+    flow.holds(normed_two, line_right, turned_one, turned_mixed, turned_two)
     two_spread.crosses(flow)
-    flow.holds(line_right)
     left_over = two_spread.double()
-    got = three_spread.direct(flow, 0, line_left, two_spread.moves(left_over))
+    lines_three = [line_right[:, : quarter - middle], line_right[:, quarter - middle :]]
+    got = flow.round(two_spread.moves(left_over) + [(line, 0) for line in lines_three])
     two_spread.put(left_over, got)
+    for held, piece in zip(three_spread.helds, got[len(left_over) :]):
+        held[1] = piece
     full_two = two_spread.helds
-    gate, up_val, hidden, hidden_turned = gate_up(normed_two, *full_two)
+    three_spread.both(flow, lines_three)
+    order = Order()
+    gate, up_val, hidden, hidden_turned = order(
+        lambda left: gate_up(left, *full_two), normed_two
+    )
 
     grad_out = cotangent.reshape(count, width)
-    orders = ((0,) + upper, (0,) + upper[::-1])
-    three = [
-        Scattered(hidden_turned, grad_out[:, :middle], orders[0]),
-        Scattered(hidden_turned, grad_out[:, middle:], orders[1]),
-    ]
-
-    def send(jobs):
-        return [job.send() for job in jobs]
-
-    three_spread.direct(flow, 1, line_right)
-    flow.holds(*send(three))
-    got = three_spread.crosses(flow, [job.move() for job in three])
-    for job, piece in zip(three, got):
-        job.receive(piece)
-    send(three)
+    flow.holds(order.last)
+    early = [early] + three_spread.crosses(flow, [(early, 0)], False)
+    job_down = Pair(hidden_turned, grad_out, upper)
+    order.first(job_down)
+    flow.holds(order.last)
     left_over = three_spread.double()
-
-    def exchange(jobs, also=()):
-        got = flow.round([job.move() for job in jobs] + list(also))
-        for job, piece in zip(jobs, got):
-            job.receive(piece)
-        return got[len(jobs) :]
-
-    got = exchange(three, three_spread.moves(left_over))
-    three_spread.put(left_over, got)
+    three_spread.put(left_over, flow.round(three_spread.moves(left_over)))
+    job_down.first_receive(partner(after(job_down.sent[0], flow.ended), 0))
     full_three = three_spread.helds
-    output, grad_gate, grad_up = down_and_back(hidden, gate, up_val, grad_out, mid, full_three)
-    output = output.reshape(batch, group, width)
-    turned_two = normed_two.T
-    two = [Scattered(turned_two, grad_gate, orders[0]), Scattered(turned_two, grad_up, orders[1])]
-    flow.holds(*send(two))
-    for step in range(len(upper) - 1):
-        send(three)
-        if step == 0:
-            got = exchange(three, [job.move() for job in two])
-            for job, piece in zip(two, got):
-                job.receive(piece)
-        else:
-            exchange(three)
-    done = [job.line() for job in three]
-    sent = send(two)
-    grad_gate, grad_up = after((grad_gate, grad_up), sent, done)
-    exchange(two)
-    down_done = finish(three)
-    grad_normed_two = back_by_rows([grad_gate, grad_up], full_two, jnp.float32)
+    grad_gate, grad_up = order(
+        lambda *operands: with_down(operands, early, full_three, True), gate, up_val, grad_out
+    )
+    job_gate = Pair(turned_two, grad_gate, upper)
+    job_up = Pair(turned_two, grad_up, upper)
+
+    def rest(job):
+        while job.left() > 1:
+            order.send(job)
+            exchange(flow, [job])
+
+    order.first(job_gate)
+    job_gate.first_receive(partner(*job_gate.first_move()))
+    order.first(job_up)
+    job_down.right = after(job_down.right, order.last)
+    order.last = summed_rows(job_down.turned, job_down.right, [job_down.whole], job_down.shared)
+    down_parts = lax.psum_scatter(
+        order.last[0].reshape(len(places), -1, width), "seq", scatter_dimension=1, tiled=True
+    )
+    sums = []
+    for turn, part in (
+        (upper, down_parts[:, :, :middle]),
+        (upper[::-1], down_parts[:, :, middle:]),
+    ):
+        sums.append(Halved([part[job_down.whole.index(place)] for place in places_of(turn)], turn))
+    order.send(job_gate)
+    flow.holds(order.last)
+    job_up.first_receive(exchange(flow, [job_gate], [job_up.first_move()])[0])
+
+    grad_normed_two = order(
+        lambda *lefts: back_by_rows(lefts, full_two, jnp.float32), grad_gate, grad_up
+    )
     back_mid, gain_two_term = norm_back(grad_normed_two, mid, scale_two, gain_b)
     grad_mid = grad_out.astype(jnp.float32) + back_mid
     grad_branch = grad_mid.astype(half_type)
-    one_b = Scattered(mixed.T, grad_branch, orders[1])
-    sent = one_b.send()
-    grad_branch = after(grad_branch, sent)
-    grad_mixed = back_by_rows([grad_branch], full_one[1:], half_type).reshape(batch, group, HEADS, HEAD)
-    probs_full = jnp.exp(scores_of() - log_total)
-    grad_probs = jnp.einsum(
-        "bqhe,bke->bhqk", grad_mixed, values_seen, preferred_element_type=jnp.float32
-    )
-    grad_values = jnp.einsum(
-        "bhqk,bqhe->bke", probs, grad_mixed, preferred_element_type=jnp.float32
-    )
-    centre = jnp.sum(probs_full * grad_probs, axis=-1, keepdims=True)
-    grad_scores = (probs_full * (grad_probs - centre)).astype(half_type)
-    flow.holds(grad_scores)
-    for step in range(len(upper) - 1):
-        sent = send(two)
-        grad_scores = after(grad_scores, sent)
-        if step == 0:
-            one_b.receive(exchange(two, [one_b.move()])[0])
-        else:
-            exchange(two)
-    grad_query = (
-        jnp.einsum("bhqk,bke->bqhe", grad_scores, keys_seen, preferred_element_type=jnp.float32)
-        * factor
-    )
-    grad_keys = (
-        jnp.einsum("bhqk,bqhe->bke", grad_scores, query_turned, preferred_element_type=jnp.float32)
-        * factor
-    )
-    grad_seen = jnp.concatenate([grad_keys, grad_values], axis=-1)
-    own = grad_seen[:, reach * group :]
+    job_out = Pair(turned_mixed, grad_branch, upper)
+    order.last = [grad_branch]
+    order.first(job_out)
+    order.send(job_up)
+    flow.holds(order.last)
+    job_out.first_receive(exchange(flow, [job_up], [job_out.first_move()])[0])
+
+    rest(job_gate)
+    order.send(job_gate)
+    grad_mixed = order(lambda left: back_by_rows([left], full_one[1:], half_type), grad_branch)
+    grad_q, grad_keys, grad_values = order(
+        lambda left: attend_back(
+            bias, cosine[0].T, sine[0].T, query_turned, left, log_total, keys_seen, values_seen
+        ),
+        grad_mixed,
+    )
+    flow.holds(order.last)
+    exchange(flow, [job_gate])
+
+    grad_seen = jnp.concatenate([grad_keys, grad_values], axis=-1)[None]
+    own, arrived = grad_seen[:, reach * group :], []
     for step in range(1, reach + 1):
         part = grad_seen[:, (reach - step) * group : (reach - step + 1) * group]
-        own = own + shifted(part.astype(jnp.bfloat16), "seq", -step).astype(part.dtype)
+        part = shifted(part.astype(jnp.bfloat16), "seq", -step)
+        arrived.append(part)
+        own = own + part.astype(own.dtype)
     grad_key = rotate(own[..., :HEAD], cosine, -sine).astype(half_type).reshape(count, HEAD)
     grad_value = own[..., HEAD:].astype(half_type).reshape(count, HEAD)
-    grad_q = (
-        rotate(grad_query, cosine[:, :, None, :], -sine[:, :, None, :])
-        .astype(half_type)
-        .reshape(count, HEADS * HEAD)
-    )
+    rest(job_up)
+    order.send(job_up)
+    output = order(
+        lambda *operands: with_down(operands, early, full_three, False), hidden, mid
+    ).reshape(batch, group, width)
+    flow.holds(order.last)
+    exchange(flow, [job_up])
+
+    gate_done = finish(order.line(job_gate))
+    order.send(job_out)
+    flow.holds(order.last, down_parts, arrived)
+    exchange(flow, [job_out])
+
     grad_first = jnp.concatenate([grad_q, grad_key, grad_value], axis=1)
-    one_a = Scattered(normed.T, grad_first, orders[0])
-    sent = one_a.send()
-    one = [one_a, one_b]
-    done = [job.line() for job in two]
-    gate_done, up_done = [finish([job]) for job in two]
-    grad_first = after(grad_first, sent, done)
-    grad_normed = back_by_rows([grad_first], full_one[:1], jnp.float32)
+    job_first = Pair(turned_one, after(grad_first, flow.fence), upper)
+    order.first(job_first)
+    job_first.first_receive(partner(*job_first.first_move()))
+    up_done = finish(order.line(job_up))
+    flow.holds(order.last)
+    exchange(flow, sums)
+
+    order.send(job_first)
+    flow.holds(order.last)
+    exchange(flow, [job_first])
+
+    rest(job_out)
+    order.send(job_out)
+    grad_normed = order(
+        lambda left: back_by_rows([left], full_one[:1], jnp.float32), grad_first
+    )
+    flow.holds(order.last)
+    exchange(flow, [job_out])
+
+    rest(job_first)
+    order.send(job_first)
+    flow.holds(order.last)
+    exchange(flow, [job_first])
     back_rows, gain_one_term = norm_back(grad_normed, rows, scale_one, gain_a)
     grad_rows = (grad_mid + back_rows).astype(half_type).reshape(batch, group, width)
     gain_terms = jnp.stack([gain_one_term, gain_two_term])
-    one_a.receive(flow.round([one_a.move()])[0])
-    bits = [0] + list(upper)
-    for step in range(len(upper)):
-        send(one)
-        got = exchange(one, [(gain_terms, bits.pop(0))])
-        gain_terms = gain_terms + got[0]
-    done = [job.line() for job in one]
-    one_done = finish(one)
-    first_done, out_done = one_done[:, : one_done.shape[1] - width], one_done[:, -width:]
+
+    out_done = finish(order.line(job_out))
+    first_done = finish(order.line(job_first))
+    while sums[0].left():
+        exchange(flow, sums)
+    down_done = jnp.concatenate([part.kept[0] for part in sums], axis=1)
+    bits = range(dp_bits())
     for bit in bits:
         gain_terms = gain_terms + partner(gain_terms, bit)
     gain_terms = sum(

time: 1080 us -> 904 us (0.84)
  matrix products: 228 us -> 0 us
  Pallas kernels: 190 us -> 405 us
  waiting for transfers between devices: 432 us -> 313 us
  other arithmetic: 105 us -> 63.9 us
    dot_general x30 -> x0, matrix products: 228 us -> none  [the longest x24 132 us: matmul(): return jnp.dot(left, right, preferred_element_type=jnp.float32)]
    pallas_call x1 -> x25, Pallas kernels: 58.5 us -> 274 us  [the longest x18 151 us: summed_rows(): pl.pallas_call(functools.partial(sum_kernel, len(shared), each), out_shap...]
    all_gather x6 -> x5, waiting for transfers between devices: 103 us -> 32.6 us  [along(): return lax.all_gather(shard, 'seq', axis=0, tiled=True)]
    ppermute x63 -> x74, waiting for transfers between devices: 300 us -> 267 us  [partner(): lax.ppermute(value, 'dp', [(source, source ^ 1 << bit) for source in rang...]
    convert_element_type x6 -> x5, other arithmetic: 37.8 us -> 9.53 us  [the longest x3 6.39 us: finish(): lax.psum_scatter(line, 'seq', scatter_dimension=0, tiled=True)]
    reduce_scatter x4 -> x5, waiting for transfers between devices: 22 us -> 7.18 us  [the longest x4 7.18 us: finish(): lax.psum_scatter(line, 'seq', scatter_dimension=0, tiled=True)]
    reduce_sum x1, other arithmetic: 14.4 us -> 0.1 us  [documents(): before = jnp.sum(passed * doc_lengths[:, None, :], axis=-1)]
    ppermute x63 -> x74, starting transfers between devices: 37.6 us -> 49.6 us  [partner(): lax.ppermute(value, 'dp', [(source, source ^ 1 << bit) for source in rang...]
  transfers between devices with their start and end apart: 78 -> 90, of which waited for: 36 -> 41; matrix products, arithmetic and copies ran while one was open for 33% -> 9% of each run, Pallas kernels for 18% -> 45%
where the time goes in v2:
time: 904 us; the launch traced here: 893 us
  Pallas kernels  405 us (45%)
  waiting for transfers between devices  313 us (35%)
  other arithmetic  63.9 us (7%)
  starting transfers between devices  61.2 us (7%)
  local copies, waits for them, and re-layouts  33.5 us (4%)
  between operations  15.3 us (2%)
    ppermute x74, waiting for transfers between devices, partner(): lax.ppermute(value, 'dp', [(source, source ^ 1 << bit) for source in rang...  267 us
    pallas_call x18, Pallas kernels, summed_rows(): pl.pallas_call(functools.partial(sum_kernel, len(shared), each), out_shap...  151 us
    pallas_call x3, Pallas kernels, back_by_rows(): pl.pallas_call(functools.partial(back_kernel, count, many), out_shape=jax...  64 us
    pallas_call x2, Pallas kernels, with_down(): pl.pallas_call(functools.partial(down_kernel, count, together, sides, bac...  50.5 us
    ppermute x74, starting transfers between devices, partner(): lax.ppermute(value, 'dp', [(source, source ^ 1 << bit) for source in rang...  49.6 us
    pallas_call x1, Pallas kernels, gate_up(): pl.pallas_call(functools.partial(gate_kernel, count), out_shape=[jax.Shap...  36.1 us
    pallas_call x1, Pallas kernels, attend_back(): pl.pallas_call(attend_back_kernel, out_shape=[jax.ShapeDtypeStruct(query....  32.9 us
    all_gather x5, waiting for transfers between devices, along(): return lax.all_gather(shard, 'seq', axis=0, tiled=True)  32.6 us
  transfers between devices with their start and end apart: 90, of which 41 were waited for; matrix products, arithmetic and copies ran while one was open for 9% of the time, Pallas kernels for 45%

profile of v2, /device:TPU:0, one launch (start us, length us, event | category | flops | bytes accessed | tf_op | source)
XLA Modules:
  0.0 892.8 jit_solution(11747485237062296731)
XLA Ops:
  13.4 32.6 %all-gather.7.cloned.1.call-done.refs_0_.refs_1_ = bf16[256,2432]{1,0:T(8,128)(2,1)} async-done(((bf16[64,2432]{1,0:T(8,128)(2,1)}), bf16[256,2432]{1,0:T(8,128)(2,1)}) %all-gather.7.cloned.1.call-update) | async-done | bytes 1245200 | tf_op jit(solution)/shard_map/all_gather | solution.py:833
  50.1 24.9 %collective-permute-done.1.refs_2_.refs_3_ = bf16[256,2432]{1,0:T(8,128)(2,1)} collective-permute-done((bf16[256,2432]{1,0:T(8,128)(2,1)}, bf16[256,2432]{1,0:T(8,128)(2,1)}, u32[]{:S(2)}, u32[]{:S(2)}) %collective-permute-start.1) | collective-permute-done | bytes 1245216 | tf_op jit(solution)/shard_map/ppermute | solution.py:68
  81.7 27.4 %collective-permute-done.7 = bf16[176,1024]{1,0:T(8,128)(2,1)S(1)} collective-permute-done((bf16[176,1024]{1,0:T(8,128)(2,1)S(1)}, bf16[176,1024]{1,0:T(8,128)(2,1)S(1)}, u32[]{:S(2)}, u32[]{:S(2)}) %collective-permute-start.7) | collective-permute-done | bytes 360480 | tf_op jit(solution)/shard_map/ppermute | solution.py:68
  114.7 21.0 %collective-permute-done.11.refs_6_.refs_7_ = bf16[256,2048]{1,0:T(8,128)(2,1)} collective-permute-done((bf16[256,2048]{1,0:T(8,128)(2,1)}, bf16[256,2048]{1,0:T(8,128)(2,1)}, u32[]{:S(2)}, u32[]{:S(2)}) %collective-permute-start.11) | collective-permute-done | bytes 1048608 | tf_op jit(solution)/shard_map/ppermute | solution.py:68
  151.0 17.1 %shard_map.365 = (f32[512,2304]{1,0:T(8,128)}, bf16[512,2048]{1,0:T(8,128)(2,1)}, f32[8,2048]{1,0:T(8,128)}) custom-call(s32[8]{0:T(128)} %iota_xor_fusion.near, f32[512,2048]{1,0:T(8,128)} %convert_multiply_fusion.3.left, bf16[256,2432]{1,0:T(8,128)(2,1)} %all-gather.7.cloned.1.call-done.refs_0_.refs_1_, ...), custom_call_target="tpu_custom_call" | custom-call | flops 4831838208 | bytes 9437184 | tf_op jit(solution)/shard_map/pallas_call | solution.py:160
  187.8 22.5 %collective-permute-done.18.refs_2_.refs_4_ = bf16[256,5632]{1,0:T(8,128)(2,1)} collective-permute-done((bf16[256,5632]{1,0:T(8,128)(2,1)}, bf16[256,5632]{1,0:T(8,128)(2,1)}, u32[]{:S(2)}, u32[]{:S(2)}) %collective-permute-start.18) | collective-permute-done | bytes 2883616 | tf_op jit(solution)/shard_map/ppermute | solution.py:68
  217.2 26.6 %shard_map.366 = (bf16[512,2048]{1,0:T(8,128)(2,1)}, f32[16,1,512]{2,1,0:T(1,128)}) custom-call(f32[1024,512]{1,0:T(8,128)} %fusion.11.bias, bf16[512,2048]{1,0:T(8,128)(2,1)} %bitcast.102, bf16[1024,128]{1,0:T(8,128)(2,1)} %get-tuple-element.521.keys, bf16[128,1024]{1,0:T(8,128)(2,1)} %copy.49.values_turned), custom_call_target="tpu_custom_call" | custom-call | flops 4294967296 | bytes 8388608 | tf_op jit(solution)/shard_map/pallas_call | solution.py:268
  247.9 14.6 %shard_map.367 = f32[512,2048]{1,0:T(8,128)} custom-call(s32[8]{0:T(128)} %iota_xor_fusion.near, bf16[512,2048]{1,0:T(8,128)(2,1)} %get-tuple-element.377.left.source, bf16[256,2048]{1,0:T(8,128)(2,1)} %all-gather.9.cloned.1.call-done.refs_0_.refs_1_, bf16[256,2048]{1,0:T(8,128)(2,1)} %copy-done.69, bf16[256,2048]{1,0:T(8,128)(2,1)} %copy-done.68, ...), custom_call_target="tpu_custom_call" | custom-call | flops 4294967296 | bytes 8388608 | tf_op jit(solution)/shard_map/pallas_call | solution.py:160
  273.4 9.4 %collective-permute-done.23 = bf16[176,1024]{1,0:T(8,128)(2,1)S(1)} collective-permute-done((bf16[176,1024]{1,0:T(8,128)(2,1)S(1)}, bf16[176,1024]{1,0:T(8,128)(2,1)S(1)}, u32[]{:S(2)}, u32[]{:S(2)}) %collective-permute-start.23) | collective-permute-done | bytes 360480 | tf_op jit(solution)/shard_map/ppermute | solution.py:68
  292.5 57.0 %collective-permute-done.26.refs_6_.refs_8_ = bf16[256,5632]{1,0:T(8,128)(2,1)S(1)} collective-permute-done((bf16[256,5632]{1,0:T(8,128)(2,1)}, bf16[256,5632]{1,0:T(8,128)(2,1)S(1)}, u32[]{:S(2)}, u32[]{:S(2)}) %collective-permute-start.26) | collective-permute-done | bytes 2883616 | tf_op jit(solution)/shard_map/ppermute | solution.py:68
  366.4 36.1 %shard_map.371 = (f32[512,5632]{1,0:T(8,128)}, f32[512,5632]{1,0:T(8,128)}, bf16[512,5632]{1,0:T(8,128)(2,1)}, bf16[5632,512]{1,0:T(8,128)(2,1)}) custom-call(bf16[512,2048]{1,0:T(8,128)(2,1)} %multiply_convert_fusion.source.left, bf16[256,5632]{1,0:T(8,128)(2,1)} %all-gather.11.cloned.1.call-done.refs_0_.refs_2_, ...), custom_call_target="tpu_custom_call" | custom-call | flops 23622320128 | bytes 80740352 | tf_op jit(solution)/shard_map/pallas_call | solution.py:375
  406.6 10.9 %shard_map.372 = bf16[2816,2048]{1,0:T(8,128)(2,1)} custom-call(s32[1,4]{1,0:T(1,128)} %broadcast_xor_fusion.2.table, bf16[5632,512]{1,0:T(8,128)(2,1)} %get-tuple-element.401.turned, bf16[512,2048]{1,0:T(8,128)(2,1)} %bitcast.98), custom_call_target="tpu_custom_call" | custom-call | flops 5905580032 | bytes 11534336 | tf_op jit(solution)/shard_map/pallas_call | solution.py:707
  432.1 27.2 %shard_map.373 = (bf16[512,5632]{1,0:T(8,128)(2,1)}, bf16[512,5632]{1,0:T(8,128)(2,1)}) custom-call(s32[4]{0:T(128)} %iota_xor_fusion.1.near, f32[512,5632]{1,0:T(8,128)} %get-tuple-element.403.refs_0_, f32[512,5632]{1,0:T(8,128)} %get-tuple-element.404.refs_1_, bf16[512,2048]{1,0:T(8,128)(2,1)} %bitcast.99, ...), custom_call_target="tpu_custom_call" | custom-call | flops 11811160064 | bytes 51904512 | tf_op jit(solution)/shard_map/pallas_call | solution.py:499
  459.3 11.9 %shard_map.374 = bf16[1024,5632]{1,0:T(8,128)(2,1)} custom-call(s32[1,4]{1,0:T(1,128)} %broadcast_xor_fusion.2.table, bf16[2048,512]{1,0:T(8,128)(2,1)} %shard_map.370.turned, bf16[512,5632]{1,0:T(8,128)(2,1)} %get-tuple-element.455.right.refs_0_), custom_call_target="tpu_custom_call" | custom-call | flops 5905580032 | bytes 11534336 | tf_op jit(solution)/shard_map/pallas_call | solution.py:707
  471.7 11.8 %shard_map.375 = bf16[1024,5632]{1,0:T(8,128)(2,1)} custom-call(s32[1,4]{1,0:T(1,128)} %broadcast_xor_fusion.2.table, bf16[2048,512]{1,0:T(8,128)(2,1)} %shard_map.370.turned, bf16[512,5632]{1,0:T(8,128)(2,1)} %get-tuple-element.468.right.refs_1_), custom_call_target="tpu_custom_call" | custom-call | flops 5905580032 | bytes 11534336 | tf_op jit(solution)/shard_map/pallas_call | solution.py:707
  483.5 14.2 %shard_map.376 = bf16[2816,2048]{1,0:T(8,128)(2,1)} custom-call(s32[2,4]{1,0:T(2,128)} %copy-done.54, bf16[5632,512]{1,0:T(8,128)(2,1)} %get-tuple-element.401.turned, bf16[512,2048]{1,0:T(8,128)(2,1)} %bitcast.100, bf16[2816,2048]{1,0:T(8,128)(2,1)} %collective-permute-done.47.refs_0_), custom_call_target="tpu_custom_call" | custom-call | flops 5905580032 | bytes 23068672 | tf_op jit(solution)/shard_map/pallas_call | solution.py:707
  498.9 10.9 %shard_map.377 = (bf16[512,2816]{1,0:T(8,128)(2,1)}, bf16[512,2816]{1,0:T(8,128)(2,1)}) custom-call(s32[2,4]{1,0:T(2,128)} %copy-done.51, bf16[2048,512]{1,0:T(8,128)(2,1)} %shard_map.370.turned, bf16[512,5632]{1,0:T(8,128)(2,1)} %get-tuple-element.455.right.refs_0_, bf16[1024,5632]{1,0:T(8,128)(2,1)} %collective-permute-done.48.refs_0_), custom_call_target="tpu_custom_call" | custom-call | flops 2952790016 | bytes 11534336 | tf_op jit(solution)/shard_map/pallas_call | solution.py:707
  512.8 38.2 %shard_map.378 = f32[512,2048]{1,0:T(8,128)} custom-call(s32[8]{0:T(128)} %iota_xor_fusion.near, bf16[512,5632]{1,0:T(8,128)(2,1)} %get-tuple-element.455.right.refs_0_, bf16[512,5632]{1,0:T(8,128)(2,1)} %get-tuple-element.468.right.refs_1_, bf16[256,5632]{1,0:T(8,128)(2,1)} %all-gather.11.cloned.1.call-done.refs_0_.refs_2_, ...), custom_call_target="tpu_custom_call" | custom-call | flops 23622320128 | bytes 46137344 | tf_op jit(solution)/shard_map/pallas_call | solution.py:214
  565.4 10.9 %shard_map.380 = (bf16[512,2816]{1,0:T(8,128)(2,1)}, bf16[512,2816]{1,0:T(8,128)(2,1)}) custom-call(s32[2,4]{1,0:T(2,128)} %copy-done.51, bf16[2048,512]{1,0:T(8,128)(2,1)} %shard_map.370.turned, bf16[512,5632]{1,0:T(8,128)(2,1)} %get-tuple-element.468.right.refs_1_, bf16[1024,5632]{1,0:T(8,128)(2,1)} %collective-permute-done.49.refs_0_), custom_call_target="tpu_custom_call" | custom-call | flops 2952790016 | bytes 11534336 | tf_op jit(solution)/shard_map/pallas_call | solution.py:707
  589.1 12.5 %shard_map.382.grad_mixed = bf16[512,2048]{1,0:T(8,128)(2,1)} custom-call(s32[8]{0:T(128)} %iota_xor_fusion.near, bf16[512,2048]{1,0:T(8,128)(2,1)} %get-tuple-element.483.right.refs_0_, bf16[256,2048]{1,0:T(8,128)(2,1)} %all-gather.9.cloned.1.call-done.refs_0_.refs_1_, bf16[256,2048]{1,0:T(8,128)(2,1)} %copy-done.69, bf16[256,2048]{1,0:T(8,128)(2,1)} %copy-done.68, ...), custom_call_target="tpu_custom_call" | custom-call | flops 4294967296 | bytes 8388608 | tf_op jit(solution)/shard_map/pallas_call | solution.py:214
  601.5 32.9 %shard_map.383 = (bf16[512,2048]{1,0:T(8,128)(2,1)}, f32[1024,128]{1,0:T(8,128)}, f32[1024,128]{1,0:T(8,128)}) custom-call(f32[1024,512]{1,0:T(8,128)} %fusion.11.bias, f32[64,512]{1,0:T(8,128)} %get-tuple-element.529.cosine, f32[64,512]{1,0:T(8,128)} %get-tuple-element.528.sine, bf16[512,2048]{1,0:T(8,128)(2,1)} %bitcast.103, ...), custom_call_target="tpu_custom_call" | custom-call | flops 10737418240 | bytes 12582912 | tf_op jit(solution)/shard_map/pallas_call | solution.py:316
  652.3 23.3 %shard_map.385 = bf16[512,2048]{1,0:T(8,128)(2,1)} custom-call(s32[4]{0:T(128)} %iota_xor_fusion.1.near, bf16[512,5632]{1,0:T(8,128)(2,1)} %get-tuple-element.453.refs_0_, f32[512,2048]{1,0:T(8,128)} %copy-done, bf16[4,704,1024]{2,1,0:T(8,128)(2,1)} %all-gather.17.cloned.1.call-done.refs_3_.refs_2_, ...), custom_call_target="tpu_custom_call" | custom-call | flops 11811160064 | bytes 51904512 | tf_op jit(solution)/shard_map/pallas_call | solution.py:499
  738.6 22.2 %collective-permute-done.61.refs_1_ = bf16[512,1024]{1,0:T(8,128)(2,1)S(1)} collective-permute-done((bf16[512,1024]{1,0:T(8,128)(2,1)}, bf16[512,1024]{1,0:T(8,128)(2,1)S(1)}, u32[]{:S(2)}, u32[]{:S(2)}) %collective-permute-start.61) | collective-permute-done | bytes 1048608 | tf_op jit(solution)/shard_map/ppermute | solution.py:68
  787.4 13.4 %shard_map.392 = f32[512,2048]{1,0:T(8,128)} custom-call(s32[8]{0:T(128)} %iota_xor_fusion.near, bf16[512,2304]{1,0:T(8,128)(2,1)} %concatenate.97.right.refs_0_, bf16[256,2432]{1,0:T(8,128)(2,1)} %all-gather.7.cloned.1.call-done.refs_0_.refs_1_, bf16[256,2432]{1,0:T(8,128)(2,1)} %collective-permute-done.refs_1_.refs_2_, ...), custom_call_target="tpu_custom_call" | custom-call | flops 4831838208 | bytes 9437184 | tf_op jit(solution)/shard_map/pallas_call | solution.py:214
  (434 shorter events, 348.1 us)
Async XLA Ops:
  11.6 64.6 %all-gather.9.cloned.1.call-start = ((), (), s32[]{:S(2)}) async-start(), calls=%async_computation.6 | async-start | bytes 1310720 | tf_op jit(solution)/shard_map/all_gather | solution.py:833
  46.1 92.3 %all-gather.11.cloned.1.call-start = ((), (), s32[]{:S(2)}) async-start(), calls=%async_computation.7 | async-start | bytes 3604480 | tf_op jit(solution)/shard_map/all_gather | solution.py:833
  76.2 135.0 %all-gather.13.cloned.1.call-start = ((), (), s32[]{:S(2)}) async-start(), calls=%async_computation.8 | async-start | bytes 3604480 | tf_op jit(solution)/shard_map/all_gather | solution.py:833
  138.4 144.4 %all-gather.15.cloned.1.call-start = ((), (), s32[]{:S(2)}) async-start(), calls=%async_computation.9 | async-start | bytes 1802240 | tf_op jit(solution)/shard_map/all_gather | solution.py:833
  145.6 64.7 %collective-permute-start.18 = (bf16[256,5632]{1,0:T(8,128)(2,1)}, bf16[256,5632]{1,0:T(8,128)(2,1)}, u32[]{:S(2)}, u32[]{:S(2)}) collective-permute-start(bf16[256,5632]{1,0:T(8,128)(2,1)} %all-gather.11.cloned.1.call-done.refs_0_.refs_2_), channel_id=1, source_target_pairs={{0,8},{4,12},{8,0},{12,4},{16,24},{20,28},{24,16},{28,20},{1,9},{5... | collective-permute-start | bytes 8650760 | tf_op jit(solution)/shard_map/ppermute | solution.py:68
  146.8 64.4 %collective-permute-start.19 = (bf16[256,5632]{1,0:T(8,128)(2,1)}, bf16[256,5632]{1,0:T(8,128)(2,1)}, u32[]{:S(2)}, u32[]{:S(2)}) collective-permute-start(bf16[256,5632]{1,0:T(8,128)(2,1)} %all-gather.11.cloned.1.call-done.refs_0_.refs_2_), channel_id=1, source_target_pairs={{0,16},{4,20},{8,24},{12,28},{16,0},{20,4},{24,8},{28,12},{1,17},{... | collective-permute-start | bytes 8650760 | tf_op jit(solution)/shard_map/ppermute | solution.py:68
  211.3 71.5 %collective-permute-start.20 = (bf16[256,5632]{1,0:T(8,128)(2,1)}, bf16[256,5632]{1,0:T(8,128)(2,1)}, u32[]{:S(2)}, u32[]{:S(2)}) collective-permute-start(bf16[256,5632]{1,0:T(8,128)(2,1)} %all-gather.13.cloned.1.call-done.refs_8_.refs_10_), channel_id=1, source_target_pairs={{0,16},{4,20},{8,24},{12,28},{16,0},{20,4},{24,8},{28,12},{1,17},{... | collective-permute-start | bytes 8650760 | tf_op jit(solution)/shard_map/ppermute | solution.py:68
  211.9 70.9 %collective-permute-start.21 = (bf16[256,5632]{1,0:T(8,128)(2,1)}, bf16[256,5632]{1,0:T(8,128)(2,1)}, u32[]{:S(2)}, u32[]{:S(2)}) collective-permute-start(bf16[256,5632]{1,0:T(8,128)(2,1)} %all-gather.13.cloned.1.call-done.refs_8_.refs_10_), channel_id=1, source_target_pairs={{0,8},{4,12},{8,0},{12,4},{16,24},{20,28},{24,16},{28,20},{1,9},{5... | collective-permute-start | bytes 8650760 | tf_op jit(solution)/shard_map/ppermute | solution.py:68
  212.7 70.1 %collective-permute-start.22 = (bf16[256,5632]{1,0:T(8,128)(2,1)}, bf16[256,5632]{1,0:T(8,128)(2,1)}, u32[]{:S(2)}, u32[]{:S(2)}) collective-permute-start(bf16[256,5632]{1,0:T(8,128)(2,1)} %all-gather.13.cloned.1.call-done.refs_8_.refs_10_), channel_id=1, source_target_pairs={{0,4},{4,0},{8,12},{12,8},{16,20},{20,16},{24,28},{28,24},{1,5},{5... | collective-permute-start | bytes 8650760 | tf_op jit(solution)/shard_map/ppermute | solution.py:68
  215.4 189.3 %all-gather.17.cloned.1.call-start = ((), (), s32[]{:S(2)}) async-start(), calls=%async_computation.10 | async-start | bytes 7208960 | tf_op jit(solution)/shard_map/all_gather | solution.py:901
  284.2 434.6 %reduce-scatter.6.cloned.1.call-start = ((), (), s32[]{:S(2)}) async-start(), calls=%async_computation.11 | async-start | bytes 14417920 | tf_op jit(solution)/shard_map/reduce_scatter | solution.py:949
  284.8 64.7 %collective-permute-start.26 = (bf16[256,5632]{1,0:T(8,128)(2,1)}, bf16[256,5632]{1,0:T(8,128)(2,1)S(1)}, u32[]{:S(2)}, u32[]{:S(2)}) collective-permute-start(bf16[256,5632]{1,0:T(8,128)(2,1)} %collective-permute-done.18.refs_2_.refs_4_), channel_id=1, source_target_pairs={{0,16},{4,20},{8,24},{12,28},{16,0},{20,4},{24,8},{28,12},{1,17},{... | collective-permute-start | bytes 8650760 | tf_op jit(solution)/shard_map/ppermute | solution.py:68
  286.2 64.4 %collective-permute-start.27 = (bf16[256,5632]{1,0:T(8,128)(2,1)}, bf16[256,5632]{1,0:T(8,128)(2,1)S(1)}, u32[]{:S(2)}, u32[]{:S(2)}) collective-permute-start(bf16[256,5632]{1,0:T(8,128)(2,1)} %collective-permute-done.20.refs_12_.refs_14_), channel_id=1, source_target_pairs={{0,8},{4,12},{8,0},{12,4},{16,24},{20,28},{24,16},{28,20},{1,9},{5... | collective-permute-start | bytes 8650760 | tf_op jit(solution)/shard_map/ppermute | solution.py:68
  287.0 63.6 %collective-permute-start.28 = (bf16[256,5632]{1,0:T(8,128)(2,1)}, bf16[256,5632]{1,0:T(8,128)(2,1)S(1)}, u32[]{:S(2)}, u32[]{:S(2)}) collective-permute-start(bf16[256,5632]{1,0:T(8,128)(2,1)} %collective-permute-done.21.refs_10_.refs_12_), channel_id=1, source_target_pairs={{0,4},{4,0},{8,12},{12,8},{16,20},{20,16},{24,28},{28,24},{1,5},{5... | collective-permute-start | bytes 8650760 | tf_op jit(solution)/shard_map/ppermute | solution.py:68
  288.5 62.1 %collective-permute-start.29 = (bf16[256,5632]{1,0:T(8,128)(2,1)}, bf16[256,5632]{1,0:T(8,128)(2,1)S(1)}, u32[]{:S(2)}, u32[]{:S(2)}) collective-permute-start(bf16[256,5632]{1,0:T(8,128)(2,1)} %collective-permute-done.20.refs_12_.refs_14_), channel_id=1, source_target_pairs={{0,4},{4,0},{8,12},{12,8},{16,20},{20,16},{24,28},{28,24},{1,5},{5... | collective-permute-start | bytes 8650760 | tf_op jit(solution)/shard_map/ppermute | solution.py:68
  497.7 334.3 %reduce-scatter.12.cloned.1.call-start = ((), (), s32[]{:S(2)}) async-start(), calls=%async_computation.14 | async-start | bytes 3604480 | tf_op jit(solution)/shard_map/reduce_scatter | solution.py:784
  510.1 66.2 %collective-permute-start.50 = (bf16[512,2816]{1,0:T(8,128)(2,1)}, bf16[512,2816]{1,0:T(8,128)(2,1)}, u32[]{:S(2)}, u32[]{:S(2)}) collective-permute-start(bf16[512,2816]{1,0:T(8,128)(2,1)} %get-tuple-element.439), channel_id=1, source_target_pairs={{0,8},{4,12},{8,0},{12,4},{16,24},{20,28},{24,16},{28,20},{1,9},{5... | collective-permute-start | bytes 8650760 | tf_op jit(solution)/shard_map/ppermute | solution.py:68
  511.4 65.0 %collective-permute-start.51 = (bf16[512,2816]{1,0:T(8,128)(2,1)}, bf16[512,2816]{1,0:T(8,128)(2,1)}, u32[]{:S(2)}, u32[]{:S(2)}) collective-permute-start(bf16[512,2816]{1,0:T(8,128)(2,1)} %get-tuple-element.440), channel_id=1, source_target_pairs={{0,16},{4,20},{8,24},{12,28},{16,0},{20,4},{24,8},{28,12},{1,17},{... | collective-permute-start | bytes 8650760 | tf_op jit(solution)/shard_map/ppermute | solution.py:68
  576.3 65.9 %collective-permute-start.55 = (bf16[1024,2048]{1,0:T(8,128)(2,1)}, bf16[1024,2048]{1,0:T(8,128)(2,1)}, u32[]{:S(2)}, u32[]{:S(2)}) collective-permute-start(bf16[1024,2048]{1,0:T(8,128)(2,1)} %shard_map.379), channel_id=1, source_target_pairs={{0,4},{4,0},{8,12},{12,8},{16,20},{20,16},{24,28},{28,24},{1,5},{5... | collective-permute-start | bytes 12582920 | tf_op jit(solution)/shard_map/ppermute | solution.py:68
  576.4 65.1 %collective-permute-start.52 = (bf16[512,2816]{1,0:T(8,128)(2,1)}, bf16[512,2816]{1,0:T(8,128)(2,1)S(1)}, u32[]{:S(2)}, u32[]{:S(2)}) collective-permute-start(bf16[512,2816]{1,0:T(8,128)(2,1)} %get-tuple-element.449), channel_id=1, source_target_pairs={{0,8},{4,12},{8,0},{12,4},{16,24},{20,28},{24,16},{28,20},{1,9},{5... | collective-permute-start | bytes 8650760 | tf_op jit(solution)/shard_map/ppermute | solution.py:68
  577.4 64.9 %collective-permute-start.53 = (bf16[512,2816]{1,0:T(8,128)(2,1)}, bf16[512,2816]{1,0:T(8,128)(2,1)}, u32[]{:S(2)}, u32[]{:S(2)}) collective-permute-start(bf16[512,2816]{1,0:T(8,128)(2,1)} %get-tuple-element.450), channel_id=1, source_target_pairs={{0,16},{4,20},{8,24},{12,28},{16,0},{20,4},{24,8},{28,12},{1,17},{... | collective-permute-start | bytes 8650760 | tf_op jit(solution)/shard_map/ppermute | solution.py:68
  685.6 182.9 %reduce-scatter.14.cloned.1.call-start = ((), (), s32[]{:S(2)}) async-start(), calls=%async_computation.15 | async-start | bytes 3604480 | tf_op jit(solution)/shard_map/reduce_scatter | solution.py:784
  734.9 138.9 %reduce-scatter.10.cloned.1.call-start = ((), (), s32[]{:S(2)}) async-start(), calls=%async_computation.13 | async-start | bytes 1310720 | tf_op jit(solution)/shard_map/reduce_scatter | solution.py:784
  825.7 57.0 %reduce-scatter.8.cloned.1.call-start = ((), (), s32[]{:S(2)}) async-start(), calls=%async_computation.12 | async-start | bytes 1474560 | tf_op jit(solution)/shard_map/reduce_scatter | solution.py:784
  (140 other events, 3023.6 us)
Sparse Core Ops, SparseCore 0:
  11.7 34.2 all-gather.6
  48.2 26.9 all-gather.8
  77.4 58.6 all-gather.10
  138.5 60.4 all-gather.12
  215.5 34.4 all-gather.14
  284.4 105.7 all-gather.16
  497.9 193.8 reduce-scatter.5
  694.0 57.5 reduce-scatter.11
  753.9 56.0 reduce-scatter.13
  825.9 26.5 reduce-scatter.9
  854.9 27.8 reduce-scatter.7

commit v3 on v2

--- a/solution.py
+++ b/solution.py
@@ -1002,20 +1002,17 @@
     exchange(flow, [job_up])
 
     gate_done = finish(order.line(job_gate))
-    order.send(job_out)
-    flow.holds(order.last, down_parts, arrived)
-    exchange(flow, [job_out])
-
     grad_first = jnp.concatenate([grad_q, grad_key, grad_value], axis=1)
-    job_first = Pair(turned_one, after(grad_first, flow.fence), upper)
+    job_first = Pair(turned_one, grad_first, upper)
     order.first(job_first)
     job_first.first_receive(partner(*job_first.first_move()))
+    order.send(job_out)
+    flow.holds(order.last)
+    exchange(flow, [job_out])
+
     up_done = finish(order.line(job_up))
-    flow.holds(order.last)
-    exchange(flow, sums)
-
     order.send(job_first)
-    flow.holds(order.last)
+    flow.holds(order.last, down_parts)
     exchange(flow, [job_first])
 
     rest(job_out)
@@ -1030,12 +1027,14 @@
     order.send(job_first)
     flow.holds(order.last)
     exchange(flow, [job_first])
+    grad_normed = after(grad_normed, flow.fence)
     back_rows, gain_one_term = norm_back(grad_normed, rows, scale_one, gain_a)
     grad_rows = (grad_mid + back_rows).astype(half_type).reshape(batch, group, width)
     gain_terms = jnp.stack([gain_one_term, gain_two_term])
 
     out_done = finish(order.line(job_out))
     first_done = finish(order.line(job_first))
+    flow.holds(order.last)
     while sums[0].left():
         exchange(flow, sums)
     down_done = jnp.concatenate([part.kept[0] for part in sums], axis=1)

time: 904 us -> 892 us (0.987)
  waiting for transfers between devices: 313 us -> 298 us
    ppermute x74, waiting for transfers between devices: 267 us -> 249 us  [partner(): lax.ppermute(value, 'dp', [(source, source ^ 1 << bit) for source in rang...]
  transfers between devices with their start and end apart: 90 -> 90, of which waited for: 41 -> 41; matrix products, arithmetic and copies ran while one was open for 9% -> 9% of each run, Pallas kernels for 45% -> 46%
where the time goes in v3:
time: 892 us; the launch traced here: 881 us
  Pallas kernels  406 us (46%)
  waiting for transfers between devices  298 us (33%)
  other arithmetic  64.9 us (7%)
  starting transfers between devices  62.1 us (7%)
  local copies, waits for them, and re-layouts  35.2 us (4%)
  between operations  15.2 us (2%)
    ppermute x74, waiting for transfers between devices, partner(): lax.ppermute(value, 'dp', [(source, source ^ 1 << bit) for source in rang...  249 us
    pallas_call x18, Pallas kernels, summed_rows(): pl.pallas_call(functools.partial(sum_kernel, len(shared), each), out_shap...  151 us
    pallas_call x3, Pallas kernels, back_by_rows(): pl.pallas_call(functools.partial(back_kernel, count, many), out_shape=jax...  64.1 us
    pallas_call x2, Pallas kernels, with_down(): pl.pallas_call(functools.partial(down_kernel, count, together, sides, bac...  50.5 us
    ppermute x74, starting transfers between devices, partner(): lax.ppermute(value, 'dp', [(source, source ^ 1 << bit) for source in rang...  50.1 us
    pallas_call x1, Pallas kernels, gate_up(): pl.pallas_call(functools.partial(gate_kernel, count), out_shape=[jax.Shap...  36.2 us
    pallas_call x1, Pallas kernels, attend_back(): pl.pallas_call(attend_back_kernel, out_shape=[jax.ShapeDtypeStruct(query....  32.9 us
    all_gather x5, waiting for transfers between devices, along(): return lax.all_gather(shard, 'seq', axis=0, tiled=True)  32.6 us
  transfers between devices with their start and end apart: 90, of which 41 were waited for; matrix products, arithmetic and copies ran while one was open for 9% of the time, Pallas kernels for 46%

profile of v3, /device:TPU:0, one launch (start us, length us, event | category | flops | bytes accessed | tf_op | source)
XLA Modules:
  0.0 881.2 jit_solution(5724701929922510360)
XLA Ops:
  13.4 32.6 %all-gather.7.cloned.1.call-done.refs_0_.refs_1_ = bf16[256,2432]{1,0:T(8,128)(2,1)} async-done(((bf16[64,2432]{1,0:T(8,128)(2,1)}), bf16[256,2432]{1,0:T(8,128)(2,1)}) %all-gather.7.cloned.1.call-update) | async-done | bytes 1245200 | tf_op jit(solution)/shard_map/all_gather | solution.py:833
  50.1 24.9 %collective-permute-done.1.refs_2_.refs_3_ = bf16[256,2432]{1,0:T(8,128)(2,1)} collective-permute-done((bf16[256,2432]{1,0:T(8,128)(2,1)}, bf16[256,2432]{1,0:T(8,128)(2,1)}, u32[]{:S(2)}, u32[]{:S(2)}) %collective-permute-start.1) | collective-permute-done | bytes 1245216 | tf_op jit(solution)/shard_map/ppermute | solution.py:68
  81.7 27.4 %collective-permute-done.7 = bf16[176,1024]{1,0:T(8,128)(2,1)S(1)} collective-permute-done((bf16[176,1024]{1,0:T(8,128)(2,1)S(1)}, bf16[176,1024]{1,0:T(8,128)(2,1)S(1)}, u32[]{:S(2)}, u32[]{:S(2)}) %collective-permute-start.7) | collective-permute-done | bytes 360480 | tf_op jit(solution)/shard_map/ppermute | solution.py:68
  114.7 21.0 %collective-permute-done.11.refs_6_.refs_7_ = bf16[256,2048]{1,0:T(8,128)(2,1)} collective-permute-done((bf16[256,2048]{1,0:T(8,128)(2,1)}, bf16[256,2048]{1,0:T(8,128)(2,1)}, u32[]{:S(2)}, u32[]{:S(2)}) %collective-permute-start.11) | collective-permute-done | bytes 1048608 | tf_op jit(solution)/shard_map/ppermute | solution.py:68
  150.9 17.1 %shard_map.365 = (f32[512,2304]{1,0:T(8,128)}, bf16[512,2048]{1,0:T(8,128)(2,1)}, f32[8,2048]{1,0:T(8,128)}) custom-call(s32[8]{0:T(128)} %iota_xor_fusion.near, f32[512,2048]{1,0:T(8,128)} %convert_multiply_fusion.3.left, bf16[256,2432]{1,0:T(8,128)(2,1)} %all-gather.7.cloned.1.call-done.refs_0_.refs_1_, ...), custom_call_target="tpu_custom_call" | custom-call | flops 4831838208 | bytes 9437184 | tf_op jit(solution)/shard_map/pallas_call | solution.py:160
  187.8 22.5 %collective-permute-done.18.refs_2_.refs_4_ = bf16[256,5632]{1,0:T(8,128)(2,1)} collective-permute-done((bf16[256,5632]{1,0:T(8,128)(2,1)}, bf16[256,5632]{1,0:T(8,128)(2,1)}, u32[]{:S(2)}, u32[]{:S(2)}) %collective-permute-start.18) | collective-permute-done | bytes 2883616 | tf_op jit(solution)/shard_map/ppermute | solution.py:68
  217.2 26.6 %shard_map.366 = (bf16[512,2048]{1,0:T(8,128)(2,1)}, f32[16,1,512]{2,1,0:T(1,128)}) custom-call(f32[1024,512]{1,0:T(8,128)} %fusion.11.bias, bf16[512,2048]{1,0:T(8,128)(2,1)} %bitcast.102, bf16[1024,128]{1,0:T(8,128)(2,1)} %get-tuple-element.521.keys, bf16[128,1024]{1,0:T(8,128)(2,1)} %copy.49.values_turned), custom_call_target="tpu_custom_call" | custom-call | flops 4294967296 | bytes 8388608 | tf_op jit(solution)/shard_map/pallas_call | solution.py:268
  247.9 14.6 %shard_map.367 = f32[512,2048]{1,0:T(8,128)} custom-call(s32[8]{0:T(128)} %iota_xor_fusion.near, bf16[512,2048]{1,0:T(8,128)(2,1)} %get-tuple-element.377.left.source, bf16[256,2048]{1,0:T(8,128)(2,1)} %all-gather.9.cloned.1.call-done.refs_0_.refs_1_, bf16[256,2048]{1,0:T(8,128)(2,1)} %copy-done.68, bf16[256,2048]{1,0:T(8,128)(2,1)} %copy-done.67, ...), custom_call_target="tpu_custom_call" | custom-call | flops 4294967296 | bytes 8388608 | tf_op jit(solution)/shard_map/pallas_call | solution.py:160
  292.5 57.0 %collective-permute-done.26.refs_6_.refs_8_ = bf16[256,5632]{1,0:T(8,128)(2,1)S(1)} collective-permute-done((bf16[256,5632]{1,0:T(8,128)(2,1)}, bf16[256,5632]{1,0:T(8,128)(2,1)S(1)}, u32[]{:S(2)}, u32[]{:S(2)}) %collective-permute-start.26) | collective-permute-done | bytes 2883616 | tf_op jit(solution)/shard_map/ppermute | solution.py:68
  366.4 36.2 %shard_map.371 = (f32[512,5632]{1,0:T(8,128)}, f32[512,5632]{1,0:T(8,128)}, bf16[512,5632]{1,0:T(8,128)(2,1)}, bf16[5632,512]{1,0:T(8,128)(2,1)}) custom-call(bf16[512,2048]{1,0:T(8,128)(2,1)} %multiply_convert_fusion.source.left, bf16[256,5632]{1,0:T(8,128)(2,1)} %all-gather.11.cloned.1.call-done.refs_0_.refs_2_, ...), custom_call_target="tpu_custom_call" | custom-call | flops 23622320128 | bytes 80740352 | tf_op jit(solution)/shard_map/pallas_call | solution.py:375
  406.7 10.9 %shard_map.372 = bf16[2816,2048]{1,0:T(8,128)(2,1)} custom-call(s32[1,4]{1,0:T(1,128)} %broadcast_xor_fusion.2.table, bf16[5632,512]{1,0:T(8,128)(2,1)} %get-tuple-element.401.turned, bf16[512,2048]{1,0:T(8,128)(2,1)} %bitcast.98), custom_call_target="tpu_custom_call" | custom-call | flops 5905580032 | bytes 11534336 | tf_op jit(solution)/shard_map/pallas_call | solution.py:707
  432.1 27.3 %shard_map.373 = (bf16[512,5632]{1,0:T(8,128)(2,1)}, bf16[512,5632]{1,0:T(8,128)(2,1)}) custom-call(s32[4]{0:T(128)} %iota_xor_fusion.1.near, f32[512,5632]{1,0:T(8,128)} %get-tuple-element.403.refs_0_, f32[512,5632]{1,0:T(8,128)} %get-tuple-element.404.refs_1_, bf16[512,2048]{1,0:T(8,128)(2,1)} %bitcast.99, ...), custom_call_target="tpu_custom_call" | custom-call | flops 11811160064 | bytes 51904512 | tf_op jit(solution)/shard_map/pallas_call | solution.py:499
  459.5 11.9 %shard_map.374 = bf16[1024,5632]{1,0:T(8,128)(2,1)} custom-call(s32[1,4]{1,0:T(1,128)} %broadcast_xor_fusion.2.table, bf16[2048,512]{1,0:T(8,128)(2,1)} %shard_map.370.turned, bf16[512,5632]{1,0:T(8,128)(2,1)} %get-tuple-element.455.right.refs_0_), custom_call_target="tpu_custom_call" | custom-call | flops 5905580032 | bytes 11534336 | tf_op jit(solution)/shard_map/pallas_call | solution.py:707
  471.8 11.7 %shard_map.375 = bf16[1024,5632]{1,0:T(8,128)(2,1)} custom-call(s32[1,4]{1,0:T(1,128)} %broadcast_xor_fusion.2.table, bf16[2048,512]{1,0:T(8,128)(2,1)} %shard_map.370.turned, bf16[512,5632]{1,0:T(8,128)(2,1)} %get-tuple-element.463.right.refs_1_), custom_call_target="tpu_custom_call" | custom-call | flops 5905580032 | bytes 11534336 | tf_op jit(solution)/shard_map/pallas_call | solution.py:707
  483.6 14.2 %shard_map.376 = bf16[2816,2048]{1,0:T(8,128)(2,1)} custom-call(s32[2,4]{1,0:T(2,128)} %copy-done.53, bf16[5632,512]{1,0:T(8,128)(2,1)} %get-tuple-element.401.turned, bf16[512,2048]{1,0:T(8,128)(2,1)} %bitcast.100, bf16[2816,2048]{1,0:T(8,128)(2,1)} %collective-permute-done.47.refs_0_), custom_call_target="tpu_custom_call" | custom-call | flops 5905580032 | bytes 23068672 | tf_op jit(solution)/shard_map/pallas_call | solution.py:707
  499.1 10.9 %shard_map.377 = (bf16[512,2816]{1,0:T(8,128)(2,1)}, bf16[512,2816]{1,0:T(8,128)(2,1)}) custom-call(s32[2,4]{1,0:T(2,128)} %copy-done.50, bf16[2048,512]{1,0:T(8,128)(2,1)} %shard_map.370.turned, bf16[512,5632]{1,0:T(8,128)(2,1)} %get-tuple-element.455.right.refs_0_, bf16[1024,5632]{1,0:T(8,128)(2,1)} %collective-permute-done.48.refs_0_), custom_call_target="tpu_custom_call" | custom-call | flops 2952790016 | bytes 11534336 | tf_op jit(solution)/shard_map/pallas_call | solution.py:707
  512.9 38.2 %shard_map.378 = f32[512,2048]{1,0:T(8,128)} custom-call(s32[8]{0:T(128)} %iota_xor_fusion.near, bf16[512,5632]{1,0:T(8,128)(2,1)} %get-tuple-element.455.right.refs_0_, bf16[512,5632]{1,0:T(8,128)(2,1)} %get-tuple-element.463.right.refs_1_, bf16[256,5632]{1,0:T(8,128)(2,1)} %all-gather.11.cloned.1.call-done.refs_0_.refs_2_, ...), custom_call_target="tpu_custom_call" | custom-call | flops 23622320128 | bytes 46137344 | tf_op jit(solution)/shard_map/pallas_call | solution.py:214
  565.6 10.9 %shard_map.380 = (bf16[512,2816]{1,0:T(8,128)(2,1)}, bf16[512,2816]{1,0:T(8,128)(2,1)}) custom-call(s32[2,4]{1,0:T(2,128)} %copy-done.50, bf16[2048,512]{1,0:T(8,128)(2,1)} %shard_map.370.turned, bf16[512,5632]{1,0:T(8,128)(2,1)} %get-tuple-element.463.right.refs_1_, bf16[1024,5632]{1,0:T(8,128)(2,1)} %collective-permute-done.49.refs_0_), custom_call_target="tpu_custom_call" | custom-call | flops 2952790016 | bytes 11534336 | tf_op jit(solution)/shard_map/pallas_call | solution.py:707
  589.2 12.5 %shard_map.382.grad_mixed = bf16[512,2048]{1,0:T(8,128)(2,1)} custom-call(s32[8]{0:T(128)} %iota_xor_fusion.near, bf16[512,2048]{1,0:T(8,128)(2,1)} %get-tuple-element.485.right.refs_0_, bf16[256,2048]{1,0:T(8,128)(2,1)} %all-gather.9.cloned.1.call-done.refs_0_.refs_1_, bf16[256,2048]{1,0:T(8,128)(2,1)} %copy-done.68, bf16[256,2048]{1,0:T(8,128)(2,1)} %copy-done.67, ...), custom_call_target="tpu_custom_call" | custom-call | flops 4294967296 | bytes 8388608 | tf_op jit(solution)/shard_map/pallas_call | solution.py:214
  601.7 32.9 %shard_map.383 = (bf16[512,2048]{1,0:T(8,128)(2,1)}, f32[1024,128]{1,0:T(8,128)}, f32[1024,128]{1,0:T(8,128)}) custom-call(f32[1024,512]{1,0:T(8,128)} %fusion.11.bias, f32[64,512]{1,0:T(8,128)} %get-tuple-element.529.cosine, f32[64,512]{1,0:T(8,128)} %get-tuple-element.528.sine, bf16[512,2048]{1,0:T(8,128)(2,1)} %bitcast.103, ...), custom_call_target="tpu_custom_call" | custom-call | flops 10737418240 | bytes 12582912 | tf_op jit(solution)/shard_map/pallas_call | solution.py:316
  652.5 23.3 %shard_map.385 = bf16[512,2048]{1,0:T(8,128)(2,1)} custom-call(s32[4]{0:T(128)} %iota_xor_fusion.1.near, bf16[512,5632]{1,0:T(8,128)(2,1)} %get-tuple-element.453.refs_0_, f32[512,2048]{1,0:T(8,128)} %copy-done, bf16[4,704,1024]{2,1,0:T(8,128)(2,1)} %all-gather.17.cloned.1.call-done.refs_3_.refs_2_, ...), custom_call_target="tpu_custom_call" | custom-call | flops 11811160064 | bytes 51904512 | tf_op jit(solution)/shard_map/pallas_call | solution.py:499
  739.8 14.5 %collective-permute-done.61.refs_1_ = bf16[512,1024]{1,0:T(8,128)(2,1)S(1)} collective-permute-done((bf16[512,1024]{1,0:T(8,128)(2,1)}, bf16[512,1024]{1,0:T(8,128)(2,1)S(1)}, u32[]{:S(2)}, u32[]{:S(2)}) %collective-permute-start.61) | collective-permute-done | bytes 1048608 | tf_op jit(solution)/shard_map/ppermute | solution.py:68
  761.5 13.5 %shard_map.392 = f32[512,2048]{1,0:T(8,128)} custom-call(s32[8]{0:T(128)} %iota_xor_fusion.near, bf16[512,2304]{1,0:T(8,128)(2,1)} %concatenate.97.right.refs_0_, bf16[256,2432]{1,0:T(8,128)(2,1)} %all-gather.7.cloned.1.call-done.refs_0_.refs_1_, bf16[256,2432]{1,0:T(8,128)(2,1)} %collective-permute-done.refs_1_.refs_2_, ...), custom_call_target="tpu_custom_call" | custom-call | flops 4831838208 | bytes 9437184 | tf_op jit(solution)/shard_map/pallas_call | solution.py:214
  859.9 11.2 %reduce-scatter.8.cloned.1.call-done = bf16[64,2304]{1,0:T(8,128)(2,1)} async-done(((bf16[256,2304]{1,0:T(8,128)(2,1)}), bf16[64,2304]{1,0:T(8,128)(2,1)}) %reduce-scatter.8.cloned.1.call-update) | async-done | bytes 294928 | tf_op jit(solution)/shard_map/reduce_scatter | solution.py:784
  (442 shorter events, 342.3 us)
Async XLA Ops:
  11.6 64.6 %all-gather.9.cloned.1.call-start = ((), (), s32[]{:S(2)}) async-start(), calls=%async_computation.6 | async-start | bytes 1310720 | tf_op jit(solution)/shard_map/all_gather | solution.py:833
  46.1 92.3 %all-gather.11.cloned.1.call-start = ((), (), s32[]{:S(2)}) async-start(), calls=%async_computation.7 | async-start | bytes 3604480 | tf_op jit(solution)/shard_map/all_gather | solution.py:833
  76.2 135.0 %all-gather.13.cloned.1.call-start = ((), (), s32[]{:S(2)}) async-start(), calls=%async_computation.8 | async-start | bytes 3604480 | tf_op jit(solution)/shard_map/all_gather | solution.py:833
  138.4 144.4 %all-gather.15.cloned.1.call-start = ((), (), s32[]{:S(2)}) async-start(), calls=%async_computation.9 | async-start | bytes 1802240 | tf_op jit(solution)/shard_map/all_gather | solution.py:833
  145.6 64.7 %collective-permute-start.18 = (bf16[256,5632]{1,0:T(8,128)(2,1)}, bf16[256,5632]{1,0:T(8,128)(2,1)}, u32[]{:S(2)}, u32[]{:S(2)}) collective-permute-start(bf16[256,5632]{1,0:T(8,128)(2,1)} %all-gather.11.cloned.1.call-done.refs_0_.refs_2_), channel_id=1, source_target_pairs={{0,8},{4,12},{8,0},{12,4},{16,24},{20,28},{24,16},{28,20},{1,9},{5... | collective-permute-start | bytes 8650760 | tf_op jit(solution)/shard_map/ppermute | solution.py:68
  146.8 64.4 %collective-permute-start.19 = (bf16[256,5632]{1,0:T(8,128)(2,1)}, bf16[256,5632]{1,0:T(8,128)(2,1)}, u32[]{:S(2)}, u32[]{:S(2)}) collective-permute-start(bf16[256,5632]{1,0:T(8,128)(2,1)} %all-gather.11.cloned.1.call-done.refs_0_.refs_2_), channel_id=1, source_target_pairs={{0,16},{4,20},{8,24},{12,28},{16,0},{20,4},{24,8},{28,12},{1,17},{... | collective-permute-start | bytes 8650760 | tf_op jit(solution)/shard_map/ppermute | solution.py:68
  211.3 71.5 %collective-permute-start.20 = (bf16[256,5632]{1,0:T(8,128)(2,1)}, bf16[256,5632]{1,0:T(8,128)(2,1)}, u32[]{:S(2)}, u32[]{:S(2)}) collective-permute-start(bf16[256,5632]{1,0:T(8,128)(2,1)} %all-gather.13.cloned.1.call-done.refs_8_.refs_10_), channel_id=1, source_target_pairs={{0,16},{4,20},{8,24},{12,28},{16,0},{20,4},{24,8},{28,12},{1,17},{... | collective-permute-start | bytes 8650760 | tf_op jit(solution)/shard_map/ppermute | solution.py:68
  211.9 70.9 %collective-permute-start.21 = (bf16[256,5632]{1,0:T(8,128)(2,1)}, bf16[256,5632]{1,0:T(8,128)(2,1)}, u32[]{:S(2)}, u32[]{:S(2)}) collective-permute-start(bf16[256,5632]{1,0:T(8,128)(2,1)} %all-gather.13.cloned.1.call-done.refs_8_.refs_10_), channel_id=1, source_target_pairs={{0,8},{4,12},{8,0},{12,4},{16,24},{20,28},{24,16},{28,20},{1,9},{5... | collective-permute-start | bytes 8650760 | tf_op jit(solution)/shard_map/ppermute | solution.py:68
  212.7 70.1 %collective-permute-start.22 = (bf16[256,5632]{1,0:T(8,128)(2,1)}, bf16[256,5632]{1,0:T(8,128)(2,1)}, u32[]{:S(2)}, u32[]{:S(2)}) collective-permute-start(bf16[256,5632]{1,0:T(8,128)(2,1)} %all-gather.13.cloned.1.call-done.refs_8_.refs_10_), channel_id=1, source_target_pairs={{0,4},{4,0},{8,12},{12,8},{16,20},{20,16},{24,28},{28,24},{1,5},{5... | collective-permute-start | bytes 8650760 | tf_op jit(solution)/shard_map/ppermute | solution.py:68
  215.3 189.4 %all-gather.17.cloned.1.call-start = ((), (), s32[]{:S(2)}) async-start(), calls=%async_computation.10 | async-start | bytes 7208960 | tf_op jit(solution)/shard_map/all_gather | solution.py:901
  284.2 471.0 %reduce-scatter.6.cloned.1.call-start = ((), (), s32[]{:S(2)}) async-start(), calls=%async_computation.11 | async-start | bytes 14417920 | tf_op jit(solution)/shard_map/reduce_scatter | solution.py:949
  284.8 64.7 %collective-permute-start.26 = (bf16[256,5632]{1,0:T(8,128)(2,1)}, bf16[256,5632]{1,0:T(8,128)(2,1)S(1)}, u32[]{:S(2)}, u32[]{:S(2)}) collective-permute-start(bf16[256,5632]{1,0:T(8,128)(2,1)} %collective-permute-done.18.refs_2_.refs_4_), channel_id=1, source_target_pairs={{0,16},{4,20},{8,24},{12,28},{16,0},{20,4},{24,8},{28,12},{1,17},{... | collective-permute-start | bytes 8650760 | tf_op jit(solution)/shard_map/ppermute | solution.py:68
  286.2 64.4 %collective-permute-start.27 = (bf16[256,5632]{1,0:T(8,128)(2,1)}, bf16[256,5632]{1,0:T(8,128)(2,1)S(1)}, u32[]{:S(2)}, u32[]{:S(2)}) collective-permute-start(bf16[256,5632]{1,0:T(8,128)(2,1)} %collective-permute-done.20.refs_12_.refs_14_), channel_id=1, source_target_pairs={{0,8},{4,12},{8,0},{12,4},{16,24},{20,28},{24,16},{28,20},{1,9},{5... | collective-permute-start | bytes 8650760 | tf_op jit(solution)/shard_map/ppermute | solution.py:68
  287.0 63.6 %collective-permute-start.28 = (bf16[256,5632]{1,0:T(8,128)(2,1)}, bf16[256,5632]{1,0:T(8,128)(2,1)S(1)}, u32[]{:S(2)}, u32[]{:S(2)}) collective-permute-start(bf16[256,5632]{1,0:T(8,128)(2,1)} %collective-permute-done.21.refs_10_.refs_12_), channel_id=1, source_target_pairs={{0,4},{4,0},{8,12},{12,8},{16,20},{20,16},{24,28},{28,24},{1,5},{5... | collective-permute-start | bytes 8650760 | tf_op jit(solution)/shard_map/ppermute | solution.py:68
  288.5 62.1 %collective-permute-start.29 = (bf16[256,5632]{1,0:T(8,128)(2,1)}, bf16[256,5632]{1,0:T(8,128)(2,1)S(1)}, u32[]{:S(2)}, u32[]{:S(2)}) collective-permute-start(bf16[256,5632]{1,0:T(8,128)(2,1)} %collective-permute-done.20.refs_12_.refs_14_), channel_id=1, source_target_pairs={{0,4},{4,0},{8,12},{12,8},{16,20},{20,16},{24,28},{28,24},{1,5},{5... | collective-permute-start | bytes 8650760 | tf_op jit(solution)/shard_map/ppermute | solution.py:68
  497.8 326.1 %reduce-scatter.12.cloned.1.call-start = ((), (), s32[]{:S(2)}) async-start(), calls=%async_computation.14 | async-start | bytes 3604480 | tf_op jit(solution)/shard_map/reduce_scatter | solution.py:784
  510.3 66.2 %collective-permute-start.50 = (bf16[512,2816]{1,0:T(8,128)(2,1)}, bf16[512,2816]{1,0:T(8,128)(2,1)}, u32[]{:S(2)}, u32[]{:S(2)}) collective-permute-start(bf16[512,2816]{1,0:T(8,128)(2,1)} %get-tuple-element.439), channel_id=1, source_target_pairs={{0,8},{4,12},{8,0},{12,4},{16,24},{20,28},{24,16},{28,20},{1,9},{5... | collective-permute-start | bytes 8650760 | tf_op jit(solution)/shard_map/ppermute | solution.py:68
  511.5 65.0 %collective-permute-start.51 = (bf16[512,2816]{1,0:T(8,128)(2,1)}, bf16[512,2816]{1,0:T(8,128)(2,1)}, u32[]{:S(2)}, u32[]{:S(2)}) collective-permute-start(bf16[512,2816]{1,0:T(8,128)(2,1)} %get-tuple-element.440), channel_id=1, source_target_pairs={{0,16},{4,20},{8,24},{12,28},{16,0},{20,4},{24,8},{28,12},{1,17},{... | collective-permute-start | bytes 8650760 | tf_op jit(solution)/shard_map/ppermute | solution.py:68
  576.5 65.8 %collective-permute-start.55 = (bf16[1024,2048]{1,0:T(8,128)(2,1)}, bf16[1024,2048]{1,0:T(8,128)(2,1)}, u32[]{:S(2)}, u32[]{:S(2)}) collective-permute-start(bf16[1024,2048]{1,0:T(8,128)(2,1)} %shard_map.379), channel_id=1, source_target_pairs={{0,4},{4,0},{8,12},{12,8},{16,20},{20,16},{24,28},{28,24},{1,5},{5... | collective-permute-start | bytes 12582920 | tf_op jit(solution)/shard_map/ppermute | solution.py:68
  576.6 65.1 %collective-permute-start.52 = (bf16[512,2816]{1,0:T(8,128)(2,1)}, bf16[512,2816]{1,0:T(8,128)(2,1)S(1)}, u32[]{:S(2)}, u32[]{:S(2)}) collective-permute-start(bf16[512,2816]{1,0:T(8,128)(2,1)} %get-tuple-element.449), channel_id=1, source_target_pairs={{0,8},{4,12},{8,0},{12,4},{16,24},{20,28},{24,16},{28,20},{1,9},{5... | collective-permute-start | bytes 8650760 | tf_op jit(solution)/shard_map/ppermute | solution.py:68
  577.5 64.9 %collective-permute-start.53 = (bf16[512,2816]{1,0:T(8,128)(2,1)}, bf16[512,2816]{1,0:T(8,128)(2,1)}, u32[]{:S(2)}, u32[]{:S(2)}) collective-permute-start(bf16[512,2816]{1,0:T(8,128)(2,1)} %get-tuple-element.450), channel_id=1, source_target_pairs={{0,16},{4,20},{8,24},{12,28},{16,0},{20,4},{24,8},{28,12},{1,17},{... | collective-permute-start | bytes 8650760 | tf_op jit(solution)/shard_map/ppermute | solution.py:68
  685.7 140.5 %reduce-scatter.14.cloned.1.call-start = ((), (), s32[]{:S(2)}) async-start(), calls=%async_computation.15 | async-start | bytes 3604480 | tf_op jit(solution)/shard_map/reduce_scatter | solution.py:784
  730.8 127.3 %reduce-scatter.10.cloned.1.call-start = ((), (), s32[]{:S(2)}) async-start(), calls=%async_computation.13 | async-start | bytes 1310720 | tf_op jit(solution)/shard_map/reduce_scatter | solution.py:784
  798.4 72.7 %reduce-scatter.8.cloned.1.call-start = ((), (), s32[]{:S(2)}) async-start(), calls=%async_computation.12 | async-start | bytes 1474560 | tf_op jit(solution)/shard_map/reduce_scatter | solution.py:784
  (144 other events, 3003.8 us)
Sparse Core Ops, SparseCore 0:
  11.7 34.2 all-gather.6
  48.2 26.9 all-gather.8
  77.4 58.6 all-gather.10
  138.5 60.4 all-gather.12
  215.5 34.5 all-gather.14
  284.3 105.8 all-gather.16
  497.9 193.8 reduce-scatter.5
  694.1 58.8 reduce-scatter.11
  755.3 56.0 reduce-scatter.13
  813.6 26.9 reduce-scatter.9
  843.0 28.1 reduce-scatter.7

commit v4 on v3

--- a/solution.py
+++ b/solution.py
@@ -80,6 +80,7 @@
 
 
 MIB = 1 << 20
+STREAMS = 4
 ANYWHERE = pl.BlockSpec(memory_space=pl.ANY)
 
 
@@ -180,22 +181,31 @@
     out, held, sems = refs[many + many * count :]
     step = pl.program_id(0)
 
-    def copy(number, which, slot):
-        return pltpu.make_async_copy(
-            pieces[which * count + number], held.at[slot, which], sems.at[slot, which]
-        )
+    rows = held.shape[2]
+    share = rows // STREAMS
+
+    def copies(number, slot):
+        for which in range(many):
+            for stream in range(STREAMS):
+                part = pl.ds(stream * share, share)
+                yield pltpu.make_async_copy(
+                    pieces[which * count + number].at[part, :],
+                    held.at[slot, which, part, :],
+                    sems.at[slot, which, stream],
+                )
 
     for number in range(count):
 
         @pl.when(step == max(number - 1, 0))
         def _(number=number):
-            for which in range(many):
-                copy(number, which, number % 2).start()
+            for copy in copies(number, number % 2):
+                copy.start()
 
     slot = lax.rem(step, 2)
+    for copy in copies(0, slot):
+        copy.wait()
     total = None
     for which in range(many):
-        copy(0, which, slot).wait()
         part = lax.dot_general(
             lefts[which][...],
             held[slot, which, :, : lefts[which].shape[1]],
@@ -222,7 +232,7 @@
             out_specs=pl.BlockSpec((tokens, rows), lambda step, near: (0, near[step])),
             scratch_shapes=[
                 pltpu.VMEM((2, many, rows, wide), helds[0][0].dtype),
-                pltpu.SemaphoreType.DMA((2, many)),
+                pltpu.SemaphoreType.DMA((2, many, STREAMS)),
             ],
         ),
         **kernel_params(
@@ -652,9 +662,10 @@
     return places
 
 
-def sum_kernel(shared, each, table, turned, right, *refs):
+def sum_kernel(shared, each, table, turned, upper, lower, *refs):
     outs = refs[shared + 2 * each :]
-    total = matmul(turned[...], right[...])
+    half = upper.shape[0]
+    total = matmul(turned[:, :half], upper[...]) + matmul(turned[:, half:], lower[...])
     for part in refs[:shared]:
         total = total + part[...].astype(jnp.float32)
     sides = 2 if len(outs) == 2 or each else 1
@@ -715,7 +726,8 @@
                     (block, tokens),
                     lambda now, step, spots: (spots[0, now * count + step], 0),
                 ),
-                pl.BlockSpec((tokens, columns), lambda now, step, spots: (0, now)),
+                pl.BlockSpec((tokens // 2, columns), lambda now, step, spots: (0, now)),
+                pl.BlockSpec((tokens // 2, columns), lambda now, step, spots: (1, now)),
             ]
             + [shared_spec(1 + number) for number in range(len(shared))]
             + [
@@ -729,7 +741,7 @@
             2 * tokens * sides * count * block * columns,
             2 * sides * count * block * columns * (1 + len(shared) + each),
         ),
-    )(spots, turned, right, *[part for part, _ in shared], *[p for side in parts for p, _ in side])
+    )(spots, turned, right, right, *[part for part, _ in shared], *[p for side in parts for p, _ in side])
 
 
 class Pair:

time: 892 us -> 893 us (level)
  transfers between devices with their start and end apart: 90 -> 90, of which waited for: 41 -> 43; matrix products, arithmetic and copies ran while one was open for 9% -> 9% of each run, Pallas kernels for 46% -> 46%
where the time goes in v4:
time: 893 us; the launch traced here: 882 us
  Pallas kernels  402 us (45%)
  waiting for transfers between devices  301 us (34%)
  other arithmetic  64.7 us (7%)
  starting transfers between devices  62.7 us (7%)
  local copies, waits for them, and re-layouts  35.1 us (4%)
  between operations  15.2 us (2%)
    ppermute x74, waiting for transfers between devices, partner(): lax.ppermute(value, 'dp', [(source, source ^ 1 << bit) for source in rang...  252 us
    pallas_call x18, Pallas kernels, summed_rows(): pl.pallas_call(functools.partial(sum_kernel, len(shared), each), out_shap...  151 us
    pallas_call x3, Pallas kernels, back_by_rows(): pl.pallas_call(functools.partial(back_kernel, count, many), out_shape=jax...  60.7 us
    ppermute x74, starting transfers between devices, partner(): lax.ppermute(value, 'dp', [(source, source ^ 1 << bit) for source in rang...  50.7 us
    pallas_call x2, Pallas kernels, with_down(): pl.pallas_call(functools.partial(down_kernel, count, together, sides, bac...  50.5 us
    pallas_call x1, Pallas kernels, gate_up(): pl.pallas_call(functools.partial(gate_kernel, count), out_shape=[jax.Shap...  36.2 us
    pallas_call x1, Pallas kernels, attend_back(): pl.pallas_call(attend_back_kernel, out_shape=[jax.ShapeDtypeStruct(query....  32.9 us
    all_gather x5, waiting for transfers between devices, along(): return lax.all_gather(shard, 'seq', axis=0, tiled=True)  32.6 us
  transfers between devices with their start and end apart: 90, of which 43 were waited for; matrix products, arithmetic and copies ran while one was open for 9% of the time, Pallas kernels for 46%

profile of v4, /device:TPU:0, one launch (start us, length us, event | category | flops | bytes accessed | tf_op | source)
XLA Modules:
  0.0 881.6 jit_solution(3534591374430056240)
XLA Ops:
  13.4 32.6 %all-gather.7.cloned.1.call-done.refs_0_.refs_1_ = bf16[256,2432]{1,0:T(8,128)(2,1)} async-done(((bf16[64,2432]{1,0:T(8,128)(2,1)}), bf16[256,2432]{1,0:T(8,128)(2,1)}) %all-gather.7.cloned.1.call-update) | async-done | bytes 1245200 | tf_op jit(solution)/shard_map/all_gather | solution.py:845
  50.1 24.9 %collective-permute-done.1.refs_2_.refs_3_ = bf16[256,2432]{1,0:T(8,128)(2,1)} collective-permute-done((bf16[256,2432]{1,0:T(8,128)(2,1)}, bf16[256,2432]{1,0:T(8,128)(2,1)}, u32[]{:S(2)}, u32[]{:S(2)}) %collective-permute-start.1) | collective-permute-done | bytes 1245216 | tf_op jit(solution)/shard_map/ppermute | solution.py:68
  81.7 27.4 %collective-permute-done.7 = bf16[176,1024]{1,0:T(8,128)(2,1)S(1)} collective-permute-done((bf16[176,1024]{1,0:T(8,128)(2,1)S(1)}, bf16[176,1024]{1,0:T(8,128)(2,1)S(1)}, u32[]{:S(2)}, u32[]{:S(2)}) %collective-permute-start.7) | collective-permute-done | bytes 360480 | tf_op jit(solution)/shard_map/ppermute | solution.py:68
  114.7 21.0 %collective-permute-done.11.refs_6_.refs_7_ = bf16[256,2048]{1,0:T(8,128)(2,1)} collective-permute-done((bf16[256,2048]{1,0:T(8,128)(2,1)}, bf16[256,2048]{1,0:T(8,128)(2,1)}, u32[]{:S(2)}, u32[]{:S(2)}) %collective-permute-start.11) | collective-permute-done | bytes 1048608 | tf_op jit(solution)/shard_map/ppermute | solution.py:68
  150.9 17.1 %shard_map.365 = (f32[512,2304]{1,0:T(8,128)}, bf16[512,2048]{1,0:T(8,128)(2,1)}, f32[8,2048]{1,0:T(8,128)}) custom-call(s32[8]{0:T(128)} %iota_xor_fusion.near, f32[512,2048]{1,0:T(8,128)} %convert_multiply_fusion.3.left, bf16[256,2432]{1,0:T(8,128)(2,1)} %all-gather.7.cloned.1.call-done.refs_0_.refs_1_, ...), custom_call_target="tpu_custom_call" | custom-call | flops 4831838208 | bytes 9437184 | tf_op jit(solution)/shard_map/pallas_call | solution.py:161
  187.8 22.5 %collective-permute-done.18.refs_2_.refs_4_ = bf16[256,5632]{1,0:T(8,128)(2,1)} collective-permute-done((bf16[256,5632]{1,0:T(8,128)(2,1)}, bf16[256,5632]{1,0:T(8,128)(2,1)}, u32[]{:S(2)}, u32[]{:S(2)}) %collective-permute-start.18) | collective-permute-done | bytes 2883616 | tf_op jit(solution)/shard_map/ppermute | solution.py:68
  217.2 26.6 %shard_map.366 = (bf16[512,2048]{1,0:T(8,128)(2,1)}, f32[16,1,512]{2,1,0:T(1,128)}) custom-call(f32[1024,512]{1,0:T(8,128)} %fusion.11.bias, bf16[512,2048]{1,0:T(8,128)(2,1)} %bitcast.104, bf16[1024,128]{1,0:T(8,128)(2,1)} %get-tuple-element.521.keys, bf16[128,1024]{1,0:T(8,128)(2,1)} %copy.49.values_turned), custom_call_target="tpu_custom_call" | custom-call | flops 4294967296 | bytes 8388608 | tf_op jit(solution)/shard_map/pallas_call | solution.py:278
  247.9 14.6 %shard_map.367 = f32[512,2048]{1,0:T(8,128)} custom-call(s32[8]{0:T(128)} %iota_xor_fusion.near, bf16[512,2048]{1,0:T(8,128)(2,1)} %get-tuple-element.377.left.source, bf16[256,2048]{1,0:T(8,128)(2,1)} %all-gather.9.cloned.1.call-done.refs_0_.refs_1_, bf16[256,2048]{1,0:T(8,128)(2,1)} %copy-done.68, bf16[256,2048]{1,0:T(8,128)(2,1)} %copy-done.67, ...), custom_call_target="tpu_custom_call" | custom-call | flops 4294967296 | bytes 8388608 | tf_op jit(solution)/shard_map/pallas_call | solution.py:161
  292.5 57.0 %collective-permute-done.26.refs_6_.refs_8_ = bf16[256,5632]{1,0:T(8,128)(2,1)S(1)} collective-permute-done((bf16[256,5632]{1,0:T(8,128)(2,1)}, bf16[256,5632]{1,0:T(8,128)(2,1)S(1)}, u32[]{:S(2)}, u32[]{:S(2)}) %collective-permute-start.26) | collective-permute-done | bytes 2883616 | tf_op jit(solution)/shard_map/ppermute | solution.py:68
  366.4 36.2 %shard_map.371 = (f32[512,5632]{1,0:T(8,128)}, f32[512,5632]{1,0:T(8,128)}, bf16[512,5632]{1,0:T(8,128)(2,1)}, bf16[5632,512]{1,0:T(8,128)(2,1)}) custom-call(bf16[512,2048]{1,0:T(8,128)(2,1)} %multiply_convert_fusion.source.left, bf16[256,5632]{1,0:T(8,128)(2,1)} %all-gather.11.cloned.1.call-done.refs_0_.refs_2_, ...), custom_call_target="tpu_custom_call" | custom-call | flops 23622320128 | bytes 80740352 | tf_op jit(solution)/shard_map/pallas_call | solution.py:385
  406.7 10.9 %shard_map.372 = bf16[2816,2048]{1,0:T(8,128)(2,1)} custom-call(s32[1,4]{1,0:T(1,128)} %broadcast_xor_fusion.2.table, bf16[5632,512]{1,0:T(8,128)(2,1)} %get-tuple-element.401.turned, bf16[512,2048]{1,0:T(8,128)(2,1)} %bitcast.98, bf16[512,2048]{1,0:T(8,128)(2,1)} %bitcast.99), custom_call_target="tpu_custom_call" | custom-call | flops 5905580032 | bytes 11534336 | tf_op jit(solution)/shard_map/pallas_call | solution.py:718
  432.1 27.3 %shard_map.373 = (bf16[512,5632]{1,0:T(8,128)(2,1)}, bf16[512,5632]{1,0:T(8,128)(2,1)}) custom-call(s32[4]{0:T(128)} %iota_xor_fusion.1.near, f32[512,5632]{1,0:T(8,128)} %get-tuple-element.403.refs_0_, f32[512,5632]{1,0:T(8,128)} %get-tuple-element.404.refs_1_, bf16[512,2048]{1,0:T(8,128)(2,1)} %bitcast.100, ...), custom_call_target="tpu_custom_call" | custom-call | flops 11811160064 | bytes 51904512 | tf_op jit(solution)/shard_map/pallas_call | solution.py:509
  459.5 12.0 %shard_map.374 = bf16[1024,5632]{1,0:T(8,128)(2,1)} custom-call(s32[1,4]{1,0:T(1,128)} %broadcast_xor_fusion.2.table, bf16[2048,512]{1,0:T(8,128)(2,1)} %shard_map.370.turned, bf16[512,5632]{1,0:T(8,128)(2,1)} %get-tuple-element.455.upper.lower.refs_0_, bf16[512,5632]{1,0:T(8,128)(2,1)} %get-tuple-element.455.upper.lower.refs_0_), custom_call_target="tpu_custom_call" | custom-call | flops 5905580032 | bytes 11534336 | tf_op jit(solution)/shard_map/pallas_call | solution.py:718
  471.9 11.8 %shard_map.375 = bf16[1024,5632]{1,0:T(8,128)(2,1)} custom-call(s32[1,4]{1,0:T(1,128)} %broadcast_xor_fusion.2.table, bf16[2048,512]{1,0:T(8,128)(2,1)} %shard_map.370.turned, bf16[512,5632]{1,0:T(8,128)(2,1)} %get-tuple-element.463.upper.lower.refs_1_, bf16[512,5632]{1,0:T(8,128)(2,1)} %get-tuple-element.463.upper.lower.refs_1_), custom_call_target="tpu_custom_call" | custom-call | flops 5905580032 | bytes 11534336 | tf_op jit(solution)/shard_map/pallas_call | solution.py:718
  483.7 14.2 %shard_map.376 = bf16[2816,2048]{1,0:T(8,128)(2,1)} custom-call(s32[2,4]{1,0:T(2,128)} %copy-done.53, bf16[5632,512]{1,0:T(8,128)(2,1)} %get-tuple-element.401.turned, bf16[512,2048]{1,0:T(8,128)(2,1)} %bitcast.101, bf16[512,2048]{1,0:T(8,128)(2,1)} %bitcast.102, bf16[2816,2048]{1,0:T(8,128)(2,1)} %collective-permute-done.47.refs_0_), custom_call_target="tpu_custom_call" | custom-call | flops 5905580032 | bytes 23068672 | tf_op jit(solution)/shard_map/pallas_call | solution.py:718
  499.2 10.9 %shard_map.377 = (bf16[512,2816]{1,0:T(8,128)(2,1)}, bf16[512,2816]{1,0:T(8,128)(2,1)}) custom-call(s32[2,4]{1,0:T(2,128)} %copy-done.50, bf16[2048,512]{1,0:T(8,128)(2,1)} %shard_map.370.turned, bf16[512,5632]{1,0:T(8,128)(2,1)} %get-tuple-element.455.upper.lower.refs_0_, bf16[512,5632]{1,0:T(8,128)(2,1)} %get-tuple-element.455.upper.lower.refs_0_, ...), custom_call_target="tpu_custom_call" | custom-call | flops 2952790016 | bytes 11534336 | tf_op jit(solution)/shard_map/pallas_call | solution.py:718
  513.0 34.9 %shard_map.378 = f32[512,2048]{1,0:T(8,128)} custom-call(s32[8]{0:T(128)} %iota_xor_fusion.near, bf16[512,5632]{1,0:T(8,128)(2,1)} %get-tuple-element.455.upper.lower.refs_0_, bf16[512,5632]{1,0:T(8,128)(2,1)} %get-tuple-element.463.upper.lower.refs_1_, bf16[256,5632]{1,0:T(8,128)(2,1)} %all-gather.11.cloned.1.call-done.refs_0_.refs_2_, ...), custom_call_target="tpu_custom_call" | custom-call | flops 23622320128 | bytes 46137344 | tf_op jit(solution)/shard_map/pallas_call | solution.py:224
  562.4 10.9 %shard_map.380 = (bf16[512,2816]{1,0:T(8,128)(2,1)}, bf16[512,2816]{1,0:T(8,128)(2,1)}) custom-call(s32[2,4]{1,0:T(2,128)} %copy-done.50, bf16[2048,512]{1,0:T(8,128)(2,1)} %shard_map.370.turned, bf16[512,5632]{1,0:T(8,128)(2,1)} %get-tuple-element.463.upper.lower.refs_1_, bf16[512,5632]{1,0:T(8,128)(2,1)} %get-tuple-element.463.upper.lower.refs_1_, ...), custom_call_target="tpu_custom_call" | custom-call | flops 2952790016 | bytes 11534336 | tf_op jit(solution)/shard_map/pallas_call | solution.py:718
  589.2 12.4 %shard_map.382.grad_mixed = bf16[512,2048]{1,0:T(8,128)(2,1)} custom-call(s32[8]{0:T(128)} %iota_xor_fusion.near, bf16[512,2048]{1,0:T(8,128)(2,1)} %get-tuple-element.485.upper.lower.refs_0_, bf16[256,2048]{1,0:T(8,128)(2,1)} %all-gather.9.cloned.1.call-done.refs_0_.refs_1_, bf16[256,2048]{1,0:T(8,128)(2,1)} %copy-done.68, bf16[256,2048]{1,0:T(8,128)(2,1)} %copy-done.67, ...), custom_call_target="tpu_custom_call" | custom-call | flops 4294967296 | bytes 8388608 | tf_op jit(solution)/shard_map/pallas_call | solution.py:224
  601.7 32.9 %shard_map.383 = (bf16[512,2048]{1,0:T(8,128)(2,1)}, f32[1024,128]{1,0:T(8,128)}, f32[1024,128]{1,0:T(8,128)}) custom-call(f32[1024,512]{1,0:T(8,128)} %fusion.11.bias, f32[64,512]{1,0:T(8,128)} %get-tuple-element.529.cosine, f32[64,512]{1,0:T(8,128)} %get-tuple-element.528.sine, bf16[512,2048]{1,0:T(8,128)(2,1)} %bitcast.105, ...), custom_call_target="tpu_custom_call" | custom-call | flops 10737418240 | bytes 12582912 | tf_op jit(solution)/shard_map/pallas_call | solution.py:326
  652.6 23.3 %shard_map.385 = bf16[512,2048]{1,0:T(8,128)(2,1)} custom-call(s32[4]{0:T(128)} %iota_xor_fusion.1.near, bf16[512,5632]{1,0:T(8,128)(2,1)} %get-tuple-element.453.refs_0_, f32[512,2048]{1,0:T(8,128)} %copy-done, bf16[4,704,1024]{2,1,0:T(8,128)(2,1)} %all-gather.17.cloned.1.call-done.refs_3_.refs_2_, ...), custom_call_target="tpu_custom_call" | custom-call | flops 11811160064 | bytes 51904512 | tf_op jit(solution)/shard_map/pallas_call | solution.py:509
  739.7 14.6 %collective-permute-done.61.refs_1_ = bf16[512,1024]{1,0:T(8,128)(2,1)S(1)} collective-permute-done((bf16[512,1024]{1,0:T(8,128)(2,1)}, bf16[512,1024]{1,0:T(8,128)(2,1)S(1)}, u32[]{:S(2)}, u32[]{:S(2)}) %collective-permute-start.61) | collective-permute-done | bytes 1048608 | tf_op jit(solution)/shard_map/ppermute | solution.py:68
  761.5 13.4 %shard_map.392 = f32[512,2048]{1,0:T(8,128)} custom-call(s32[8]{0:T(128)} %iota_xor_fusion.near, bf16[512,2304]{1,0:T(8,128)(2,1)} %concatenate.97.upper.lower.refs_0_, bf16[256,2432]{1,0:T(8,128)(2,1)} %all-gather.7.cloned.1.call-done.refs_0_.refs_1_, bf16[256,2432]{1,0:T(8,128)(2,1)} %collective-permute-done.refs_1_.refs_2_, ...), custom_call_target="tpu_custom_call" | custom-call | flops 4831838208 | bytes 9437184 | tf_op jit(solution)/shard_map/pallas_call | solution.py:224
  859.9 11.6 %reduce-scatter.8.cloned.1.call-done = bf16[64,2304]{1,0:T(8,128)(2,1)} async-done(((bf16[256,2304]{1,0:T(8,128)(2,1)}), bf16[64,2304]{1,0:T(8,128)(2,1)}) %reduce-scatter.8.cloned.1.call-update) | async-done | bytes 294928 | tf_op jit(solution)/shard_map/reduce_scatter | solution.py:796
  (442 shorter events, 345.4 us)
Async XLA Ops:
  11.6 64.6 %all-gather.9.cloned.1.call-start = ((), (), s32[]{:S(2)}) async-start(), calls=%async_computation.6 | async-start | bytes 1310720 | tf_op jit(solution)/shard_map/all_gather | solution.py:845
  46.1 92.3 %all-gather.11.cloned.1.call-start = ((), (), s32[]{:S(2)}) async-start(), calls=%async_computation.7 | async-start | bytes 3604480 | tf_op jit(solution)/shard_map/all_gather | solution.py:845
  76.2 135.0 %all-gather.13.cloned.1.call-start = ((), (), s32[]{:S(2)}) async-start(), calls=%async_computation.8 | async-start | bytes 3604480 | tf_op jit(solution)/shard_map/all_gather | solution.py:845
  138.4 144.4 %all-gather.15.cloned.1.call-start = ((), (), s32[]{:S(2)}) async-start(), calls=%async_computation.9 | async-start | bytes 1802240 | tf_op jit(solution)/shard_map/all_gather | solution.py:845
  145.6 64.7 %collective-permute-start.18 = (bf16[256,5632]{1,0:T(8,128)(2,1)}, bf16[256,5632]{1,0:T(8,128)(2,1)}, u32[]{:S(2)}, u32[]{:S(2)}) collective-permute-start(bf16[256,5632]{1,0:T(8,128)(2,1)} %all-gather.11.cloned.1.call-done.refs_0_.refs_2_), channel_id=1, source_target_pairs={{0,8},{4,12},{8,0},{12,4},{16,24},{20,28},{24,16},{28,20},{1,9},{5... | collective-permute-start | bytes 8650760 | tf_op jit(solution)/shard_map/ppermute | solution.py:68
  146.8 64.4 %collective-permute-start.19 = (bf16[256,5632]{1,0:T(8,128)(2,1)}, bf16[256,5632]{1,0:T(8,128)(2,1)}, u32[]{:S(2)}, u32[]{:S(2)}) collective-permute-start(bf16[256,5632]{1,0:T(8,128)(2,1)} %all-gather.11.cloned.1.call-done.refs_0_.refs_2_), channel_id=1, source_target_pairs={{0,16},{4,20},{8,24},{12,28},{16,0},{20,4},{24,8},{28,12},{1,17},{... | collective-permute-start | bytes 8650760 | tf_op jit(solution)/shard_map/ppermute | solution.py:68
  211.3 71.5 %collective-permute-start.20 = (bf16[256,5632]{1,0:T(8,128)(2,1)}, bf16[256,5632]{1,0:T(8,128)(2,1)}, u32[]{:S(2)}, u32[]{:S(2)}) collective-permute-start(bf16[256,5632]{1,0:T(8,128)(2,1)} %all-gather.13.cloned.1.call-done.refs_8_.refs_10_), channel_id=1, source_target_pairs={{0,16},{4,20},{8,24},{12,28},{16,0},{20,4},{24,8},{28,12},{1,17},{... | collective-permute-start | bytes 8650760 | tf_op jit(solution)/shard_map/ppermute | solution.py:68
  211.9 70.9 %collective-permute-start.21 = (bf16[256,5632]{1,0:T(8,128)(2,1)}, bf16[256,5632]{1,0:T(8,128)(2,1)}, u32[]{:S(2)}, u32[]{:S(2)}) collective-permute-start(bf16[256,5632]{1,0:T(8,128)(2,1)} %all-gather.13.cloned.1.call-done.refs_8_.refs_10_), channel_id=1, source_target_pairs={{0,8},{4,12},{8,0},{12,4},{16,24},{20,28},{24,16},{28,20},{1,9},{5... | collective-permute-start | bytes 8650760 | tf_op jit(solution)/shard_map/ppermute | solution.py:68
  212.7 70.1 %collective-permute-start.22 = (bf16[256,5632]{1,0:T(8,128)(2,1)}, bf16[256,5632]{1,0:T(8,128)(2,1)}, u32[]{:S(2)}, u32[]{:S(2)}) collective-permute-start(bf16[256,5632]{1,0:T(8,128)(2,1)} %all-gather.13.cloned.1.call-done.refs_8_.refs_10_), channel_id=1, source_target_pairs={{0,4},{4,0},{8,12},{12,8},{16,20},{20,16},{24,28},{28,24},{1,5},{5... | collective-permute-start | bytes 8650760 | tf_op jit(solution)/shard_map/ppermute | solution.py:68
  215.3 189.4 %all-gather.17.cloned.1.call-start = ((), (), s32[]{:S(2)}) async-start(), calls=%async_computation.10 | async-start | bytes 7208960 | tf_op jit(solution)/shard_map/all_gather | solution.py:913
  284.2 470.9 %reduce-scatter.6.cloned.1.call-start = ((), (), s32[]{:S(2)}) async-start(), calls=%async_computation.11 | async-start | bytes 14417920 | tf_op jit(solution)/shard_map/reduce_scatter | solution.py:961
  284.8 64.7 %collective-permute-start.26 = (bf16[256,5632]{1,0:T(8,128)(2,1)}, bf16[256,5632]{1,0:T(8,128)(2,1)S(1)}, u32[]{:S(2)}, u32[]{:S(2)}) collective-permute-start(bf16[256,5632]{1,0:T(8,128)(2,1)} %collective-permute-done.18.refs_2_.refs_4_), channel_id=1, source_target_pairs={{0,16},{4,20},{8,24},{12,28},{16,0},{20,4},{24,8},{28,12},{1,17},{... | collective-permute-start | bytes 8650760 | tf_op jit(solution)/shard_map/ppermute | solution.py:68
  286.2 64.4 %collective-permute-start.27 = (bf16[256,5632]{1,0:T(8,128)(2,1)}, bf16[256,5632]{1,0:T(8,128)(2,1)S(1)}, u32[]{:S(2)}, u32[]{:S(2)}) collective-permute-start(bf16[256,5632]{1,0:T(8,128)(2,1)} %collective-permute-done.20.refs_12_.refs_14_), channel_id=1, source_target_pairs={{0,8},{4,12},{8,0},{12,4},{16,24},{20,28},{24,16},{28,20},{1,9},{5... | collective-permute-start | bytes 8650760 | tf_op jit(solution)/shard_map/ppermute | solution.py:68
  287.0 63.6 %collective-permute-start.28 = (bf16[256,5632]{1,0:T(8,128)(2,1)}, bf16[256,5632]{1,0:T(8,128)(2,1)S(1)}, u32[]{:S(2)}, u32[]{:S(2)}) collective-permute-start(bf16[256,5632]{1,0:T(8,128)(2,1)} %collective-permute-done.21.refs_10_.refs_12_), channel_id=1, source_target_pairs={{0,4},{4,0},{8,12},{12,8},{16,20},{20,16},{24,28},{28,24},{1,5},{5... | collective-permute-start | bytes 8650760 | tf_op jit(solution)/shard_map/ppermute | solution.py:68
  288.5 62.1 %collective-permute-start.29 = (bf16[256,5632]{1,0:T(8,128)(2,1)}, bf16[256,5632]{1,0:T(8,128)(2,1)S(1)}, u32[]{:S(2)}, u32[]{:S(2)}) collective-permute-start(bf16[256,5632]{1,0:T(8,128)(2,1)} %collective-permute-done.20.refs_12_.refs_14_), channel_id=1, source_target_pairs={{0,4},{4,0},{8,12},{12,8},{16,20},{20,16},{24,28},{28,24},{1,5},{5... | collective-permute-start | bytes 8650760 | tf_op jit(solution)/shard_map/ppermute | solution.py:68
  497.9 326.0 %reduce-scatter.12.cloned.1.call-start = ((), (), s32[]{:S(2)}) async-start(), calls=%async_computation.14 | async-start | bytes 3604480 | tf_op jit(solution)/shard_map/reduce_scatter | solution.py:796
  510.4 64.9 %collective-permute-start.50 = (bf16[512,2816]{1,0:T(8,128)(2,1)}, bf16[512,2816]{1,0:T(8,128)(2,1)}, u32[]{:S(2)}, u32[]{:S(2)}) collective-permute-start(bf16[512,2816]{1,0:T(8,128)(2,1)} %get-tuple-element.439), channel_id=1, source_target_pairs={{0,8},{4,12},{8,0},{12,4},{16,24},{20,28},{24,16},{28,20},{1,9},{5... | collective-permute-start | bytes 8650760 | tf_op jit(solution)/shard_map/ppermute | solution.py:68
  511.6 64.7 %collective-permute-start.51 = (bf16[512,2816]{1,0:T(8,128)(2,1)}, bf16[512,2816]{1,0:T(8,128)(2,1)}, u32[]{:S(2)}, u32[]{:S(2)}) collective-permute-start(bf16[512,2816]{1,0:T(8,128)(2,1)} %get-tuple-element.440), channel_id=1, source_target_pairs={{0,16},{4,20},{8,24},{12,28},{16,0},{20,4},{24,8},{28,12},{1,17},{... | collective-permute-start | bytes 8650760 | tf_op jit(solution)/shard_map/ppermute | solution.py:68
  576.3 65.7 %collective-permute-start.55 = (bf16[1024,2048]{1,0:T(8,128)(2,1)}, bf16[1024,2048]{1,0:T(8,128)(2,1)}, u32[]{:S(2)}, u32[]{:S(2)}) collective-permute-start(bf16[1024,2048]{1,0:T(8,128)(2,1)} %shard_map.379), channel_id=1, source_target_pairs={{0,4},{4,0},{8,12},{12,8},{16,20},{20,16},{24,28},{28,24},{1,5},{5... | collective-permute-start | bytes 12582920 | tf_op jit(solution)/shard_map/ppermute | solution.py:68
  576.3 65.1 %collective-permute-start.52 = (bf16[512,2816]{1,0:T(8,128)(2,1)}, bf16[512,2816]{1,0:T(8,128)(2,1)S(1)}, u32[]{:S(2)}, u32[]{:S(2)}) collective-permute-start(bf16[512,2816]{1,0:T(8,128)(2,1)} %get-tuple-element.449), channel_id=1, source_target_pairs={{0,8},{4,12},{8,0},{12,4},{16,24},{20,28},{24,16},{28,20},{1,9},{5... | collective-permute-start | bytes 8650760 | tf_op jit(solution)/shard_map/ppermute | solution.py:68
  577.1 64.9 %collective-permute-start.53 = (bf16[512,2816]{1,0:T(8,128)(2,1)}, bf16[512,2816]{1,0:T(8,128)(2,1)}, u32[]{:S(2)}, u32[]{:S(2)}) collective-permute-start(bf16[512,2816]{1,0:T(8,128)(2,1)} %get-tuple-element.450), channel_id=1, source_target_pairs={{0,16},{4,20},{8,24},{12,28},{16,0},{20,4},{24,8},{28,12},{1,17},{... | collective-permute-start | bytes 8650760 | tf_op jit(solution)/shard_map/ppermute | solution.py:68
  685.8 140.4 %reduce-scatter.14.cloned.1.call-start = ((), (), s32[]{:S(2)}) async-start(), calls=%async_computation.15 | async-start | bytes 3604480 | tf_op jit(solution)/shard_map/reduce_scatter | solution.py:796
  730.9 127.2 %reduce-scatter.10.cloned.1.call-start = ((), (), s32[]{:S(2)}) async-start(), calls=%async_computation.13 | async-start | bytes 1310720 | tf_op jit(solution)/shard_map/reduce_scatter | solution.py:796
  798.3 73.1 %reduce-scatter.8.cloned.1.call-start = ((), (), s32[]{:S(2)}) async-start(), calls=%async_computation.12 | async-start | bytes 1474560 | tf_op jit(solution)/shard_map/reduce_scatter | solution.py:796
  (144 other events, 3005.4 us)
Sparse Core Ops, SparseCore 0:
  11.7 34.2 all-gather.6
  48.2 26.9 all-gather.8
  77.4 58.6 all-gather.10
  138.5 60.4 all-gather.12
  215.5 34.5 all-gather.14
  284.3 105.8 all-gather.16
  498.0 193.8 reduce-scatter.5
  694.3 58.9 reduce-scatter.11
  755.5 56.0 reduce-scatter.13
  813.7 26.9 reduce-scatter.9
  843.2 28.1 reduce-scatter.7
